TPU v7x, 256 devices: a whole 4x4x8 slice. The times are simulated.
256 devices in a mesh: layer: 16 (over y_lo, x, core), query: 16 (over z, y_hi).
Axes of the slice: x: 4, y: 4 (y_hi: 2, y_lo: 2; y = y_hi * 2 + y_lo), z: 8, core: 2. Of those that a mesh axis runs over, the one named last changes fastest.
Arguments:
- queries: bfloat16 [16384, 16, 4096], P('query', 'layer'), may hold values from -6 to 6
- train_grads: bfloat16 [1024, 16, 4096], P('query', 'layer'), may hold values from -6 to 6
- basis_out: float32 [16, 64, 64], P('layer'), may hold values from -0.75 to 0.75
- basis_in: float32 [16, 64, 64], P('layer'), may hold values from -0.75 to 0.75
- eig_values: float32 [16, 4096], P('layer'), may hold values from 0.1 to 2
- train_order: int32 [1024], replicated, may hold values from 0 to 1023, each once
Outputs:
- scores: float32 [1024, 16384], P('layer', 'query')
Inputs may be any that keep to these rules, and one draw needn't show every extreme that they name: `train_order`: a permutation of the 1024 training examples.
All inputs are finite; a program needn't handle non-finite values.
Results may differ from a plain program's by a relative error of at most 0.0029.
Values may be sent and summed in bfloat16 or wider, within the bound.
No kernel may reach another device: no remote copies, remote signals or barrier semaphores. Data moves between devices by JAX's collectives and lax.ppermute only.
A program may use at most 64 MiB of HBM per device.

v0:
```python
import jax
import jax.numpy as jnp
from jax import lax
from jax.sharding import PartitionSpec as P


def per_device(queries, train_grads, basis_out, basis_in, eig_values, train_order):
    query_rows, local_layers, feat_size = queries.shape
    train_rows = train_grads.shape[0]
    side = basis_out.shape[1]
    grads_full = train_grads.astype(jnp.float32).reshape(train_rows, local_layers, side, side)
    rotated = jnp.einsum(
        "lab,elac,lcd->elbd", basis_out, grads_full, basis_in, precision=lax.Precision.HIGHEST
    )
    scaled = (rotated.reshape(train_rows, local_layers, feat_size) / eig_values[None]).astype(
        jnp.bfloat16
    )
    scaled_flat = scaled.reshape(train_rows, local_layers * feat_size)
    query_flat = queries.reshape(query_rows, local_layers * feat_size)
    layer_devices = lax.axis_size("layer")
    factor = 1.0 / jnp.sqrt(jnp.float32(local_layers * layer_devices * feat_size))
    partial_sum = lax.dot_general(
        lax.all_gather(scaled_flat, "query", axis=0, tiled=True),
        query_flat,
        (((1,), (1,)), ((), ())),
        preferred_element_type=jnp.float32,
    )
    ordered = partial_sum[train_order] * factor
    return lax.psum_scatter(ordered, "layer", scatter_dimension=0, tiled=True)


def solution(mesh):
    placed = (
        P("query", "layer", None),
        P("query", "layer", None),
        P("layer", None, None),
        P("layer", None, None),
        P("layer", None),
        P(),
    )
    return jax.shard_map(
        per_device, mesh=mesh, in_specs=placed, out_specs=P("layer", "query"), check_vma=False
    )
```

profile of v0, /device:TPU:1, one launch (start us, length us, event | category | flops | bytes accessed | tf_op | source)
XLA Modules:
  0.0 251.1 jit_solution(12795032566997530325)
XLA Ops:
  6.5 0.0 copy-start
  6.5 0.0 copy-start.1
  6.5 0.0 all-gather.2.cloned.1.call-start
  6.5 2.1 reshape.35
  8.6 0.0 copy-done
  8.6 1.0 fusion.4
  9.7 0.0 copy-done.1
  9.7 0.0 copy-start.2
  9.7 0.0 copy-start.3
  9.7 1.8 fusion.2
  11.5 0.7 transpose.5
  12.2 0.0 copy-done.2
  12.2 0.9 divide_convert_fusion
  13.1 0.0 all-gather.2.cloned.1.call-update
  13.1 0.0 reduce-scatter.2.cloned.1.call-start
  13.2 0.0 copy-done.3
  13.2 139.3 %all-gather.2.cloned.1.call-done = bf16[1024,4096]{1,0:T(8,128)(2,1)} async-done(((bf16[64,4096]{1,0:T(8,128)(2,1)}), bf16[1024,4096]{1,0:T(8,128)(2,1)}) %all-gather.2.cloned.1.call-update) | async-done | bytes 8388624 | tf_op jit(solution)/shard_map/all_gather | solution.py:23
  152.5 15.1 %fusion = f32[1024,1024]{1,0:T(8,128)} fusion(bf16[1024,4096]{1,0:T(8,128)(2,1)} %all-gather.2.cloned.1.call-done, bf16[1024,1,4096]{2,0,1:T(8,128)(2,1)} %param.6), kind=kOutput, calls=%fused_computation.1 | convolution fusion | flops 8589934592 | bytes 20971520 | tf_op jit(solution)/shard_map/dot_general | solution.py:22
  167.6 8.5 %gather_fusion = f32[1024,1024]{1,0:T(8,128)} fusion(f32[1024,1024]{1,0:T(8,128)} %fusion, s32[1024]{0:T(1024)S(1)} %fusion.6), kind=kCustom, calls=%fused_computation | custom fusion | bytes 8392704 | tf_op jit(solution)/shard_map/gather | solution.py:28
  176.1 5.0 %broadcast_multiply_fusion = f32[1024,1024]{1,0:T(8,128)} fusion(f32[1024,1024]{1,0:T(8,128)} %gather_fusion), kind=kLoop, calls=%fused_computation.3 | loop fusion | flops 1048576 | bytes 8388608 | tf_op jit(solution)/shard_map/mul | solution.py:28
  181.1 0.0 reduce-scatter.2.cloned.1.call-update
  181.1 63.1 %reduce-scatter.2.cloned.1.call-done = f32[64,1024]{1,0:T(8,128)} async-done(((f32[1024,1024]{1,0:T(8,128)}), f32[64,1024]{1,0:T(8,128)}) %reduce-scatter.2.cloned.1.call-update) | async-done | bytes 262160 | tf_op jit(solution)/shard_map/reduce_scatter | solution.py:29
  (1 shorter events, 0.0 us)
Async XLA Ops:
  6.5 2.1 copy-start
  6.5 3.1 %copy-start.1 = (f32[1,64,64]{2,1,0:T(8,128)S(1)}, f32[1,64,64]{2,1,0:T(8,128)}, u32[]{:S(2)}) copy-start(f32[1,64,64]{2,1,0:T(8,128)} %param.9) | copy-start | bytes 49156
  6.5 146.0 %all-gather.2.cloned.1.call-start = ((), (), s32[]{:S(2)}) async-start(), calls=%async_computation.1 | async-start | bytes 8912896 | tf_op jit(solution)/shard_map/all_gather | solution.py:23
  9.7 2.5 %copy-start.2 = (f32[1,4096]{1,0:T(1,128)S(1)}, f32[1,4096]{1,0:T(1,128)}, u32[]{:S(2)}) copy-start(f32[1,4096]{1,0:T(1,128)} %param.10) | copy-start | bytes 49156
  9.7 3.5 %copy-start.3 = (s32[1024]{0:T(1024)S(1)}, s32[1024]{0:T(1024)}, u32[]{:S(2)}) copy-start(s32[1024]{0:T(1024)} %param.11) | copy-start | bytes 12292
  13.1 231.1 %reduce-scatter.2.cloned.1.call-start = ((), (), s32[]{:S(2)}) async-start(), calls=%async_computation.2 | async-start | bytes 4456448 | tf_op jit(solution)/shard_map/reduce_scatter | solution.py:29
Sparse Core Ops, SparseCore 0:
  13.3 139.2 all-gather.1
  181.3 62.9 reduce-scatter.1
where the time goes:
time: 254 us; the launch traced here: 251 us
  waiting for transfers between devices  202 us (80%)
  matrix products  17.9 us (7%)
  between operations  13.5 us (5%)
  local copies, waits for them, and re-layouts  11.3 us (4%)
  other arithmetic  5.89 us (2%)
    all_gather x1, waiting for transfers between devices, per_device(): lax.all_gather(scaled_flat, 'query', axis=0, tiled=True)  139 us
    reduce_scatter x1, waiting for transfers between devices, per_device(): return lax.psum_scatter(ordered, 'layer', scatter_dimension=0, tiled=True)  63.1 us
    dot_general x1, matrix products, per_device(): lax.dot_general(lax.all_gather(scaled_flat, 'query', axis=0, tiled=True),...  15.1 us
    gather x1, local copies, waits for them, and re-layouts, per_device(): ordered = partial_sum[train_order] * factor  8.54 us
  transfers between devices with their start and end apart: 2, of which 2 were waited for; matrix products, arithmetic and copies ran while one was open for 0% of the time, Pallas kernels for 0%

commit v1 on v0

--- a/solution.py
+++ b/solution.py
@@ -2,6 +2,48 @@
 import jax.numpy as jnp
 from jax import lax
 from jax.sharding import PartitionSpec as P
+
+Z = 8
+Y_HI = 2
+X = 4
+Y_LO = 2
+CORES = 2
+BLOCKS = Z * Y_HI
+
+
+def along_z(block, step):
+    pairs = [
+        (z * Y_HI + y, ((z + step) % Z) * Y_HI + y) for z in range(Z) for y in range(Y_HI)
+    ]
+    return lax.ppermute(block, "query", pairs)
+
+
+def across_y(block):
+    pairs = [(z * Y_HI + y, z * Y_HI + 1 - y) for z in range(Z) for y in range(Y_HI)]
+    return lax.ppermute(block, "query", pairs)
+
+
+def across_cores(block):
+    pairs = [(i, i ^ 1) for i in range(Y_LO * X * CORES)]
+    return lax.ppermute(block, "layer", pairs)
+
+
+def gather_steps(own):
+    same, other = {0: own}, {}
+    same[-1], same[1], other[0] = along_z(own, 1), along_z(own, -1), across_y(own)
+    yield [(0, 0, own), (0, -1, same[-1]), (0, 1, same[1]), (1, 0, other[0])]
+    same[-2], same[2] = along_z(same[-1], 1), along_z(same[1], -1)
+    other[-1] = across_y(same[-1])
+    yield [(0, -2, same[-2]), (0, 2, same[2]), (1, -1, other[-1])]
+    same[-3], same[3] = along_z(same[-2], 1), along_z(same[2], -1)
+    other[1] = across_y(same[1])
+    yield [(0, -3, same[-3]), (0, 3, same[3]), (1, 1, other[1])]
+    same[4], other[2] = along_z(same[-3], 1), along_z(other[1], -1)
+    other[-2] = across_y(same[-2])
+    yield [(0, 4, same[4]), (1, 2, other[2]), (1, -2, other[-2])]
+    other[-3], other[3] = along_z(other[-2], 1), along_z(other[2], -1)
+    other[4] = across_y(same[4])
+    yield [(1, -3, other[-3]), (1, 3, other[3]), (1, 4, other[4])]
 
 
 def per_device(queries, train_grads, basis_out, basis_in, eig_values, train_order):
@@ -19,14 +61,53 @@
     query_flat = queries.reshape(query_rows, local_layers * feat_size)
     layer_devices = lax.axis_size("layer")
     factor = 1.0 / jnp.sqrt(jnp.float32(local_layers * layer_devices * feat_size))
-    partial_sum = lax.dot_general(
-        lax.all_gather(scaled_flat, "query", axis=0, tiled=True),
-        query_flat,
-        (((1,), (1,)), ((), ())),
-        preferred_element_type=jnp.float32,
+
+    layer = lax.axis_index("layer")
+    query = lax.axis_index("query")
+    core = layer % CORES
+    own_z, own_y = query // Y_HI, query % Y_HI
+
+    arrived, products = [], []
+    for step in gather_steps(scaled_flat):
+        arrived += [(column, offset % Z) for column, offset, _ in step]
+        rows = jnp.concatenate([block for _, _, block in step], axis=0)
+        products.append(
+            lax.dot_general(
+                rows, query_flat, (((1,), (1,)), ((), ())), preferred_element_type=jnp.float32
+            ).astype(jnp.bfloat16)
+        )
+    partial_sum = jnp.concatenate(products, axis=0)
+
+    block_of = train_order // train_rows
+    relative = ((block_of % Y_HI) ^ own_y) * Z + (block_of // Y_HI - own_z) % Z
+    place = jnp.zeros_like(relative)
+    for at, (column, offset) in enumerate(arrived):
+        place = jnp.where(relative == column * Z + offset, at, place)
+    place = place * train_rows + train_order % train_rows
+    place = place.reshape(Y_LO * X, CORES, train_rows)
+
+    def ordered(for_core):
+        rows = lax.dynamic_index_in_dim(place, for_core, 1, keepdims=False).reshape(-1)
+        pick = rows[:, None] == jnp.arange(BLOCKS * train_rows)[None, :]
+        return lax.dot_general(
+            pick.astype(jnp.bfloat16),
+            partial_sum,
+            (((1,), (0,)), ((), ())),
+            preferred_element_type=jnp.float32,
+        )
+
+    received = across_cores(ordered(1 - core).astype(jnp.bfloat16))
+    chip_sum = (ordered(core) + received.astype(jnp.float32)).astype(jnp.bfloat16)
+    groups = [[chip * CORES + c for chip in range(Y_LO * X)] for c in range(CORES)]
+    pieces = lax.all_to_all(
+        chip_sum.reshape(Y_LO * X, train_rows, query_rows),
+        "layer",
+        0,
+        0,
+        axis_index_groups=groups,
+        tiled=True,
     )
-    ordered = partial_sum[train_order] * factor
-    return lax.psum_scatter(ordered, "layer", scatter_dimension=0, tiled=True)
+    return jnp.sum(pieces.astype(jnp.float32), axis=0) * factor
 
 
 def solution(mesh):

time: 254 us -> 119 us (0.47)
  waiting for transfers between devices: 202 us -> 32.4 us
  starting transfers between devices: 0.04 us -> 30.5 us
  blocking collectives: 0 us -> 19.9 us
  between operations: 13.5 us -> 0.18 us
  matrix products: 17.9 us -> 31.2 us
  local copies, waits for them, and re-layouts: 11.3 us -> 3.07 us
  other arithmetic: 5.89 us -> 1.01 us
    all_gather x1 -> x0, waiting for transfers between devices: 139 us -> none  [per_device(): lax.all_gather(scaled_flat, 'query', axis=0, tiled=True)]
    reduce_scatter x1 -> x0, waiting for transfers between devices: 63.1 us -> none  [per_device(): return lax.psum_scatter(ordered, 'layer', scatter_dimension=0, tiled=True)]
    ppermute x0 -> x16, waiting for transfers between devices: none -> 32.4 us  [the longest x10 20.8 us: along_z(): return lax.ppermute(block, 'query', pairs)]
    ppermute x0 -> x16, starting transfers between devices: none -> 30.5 us  [the longest x10 16.2 us: along_z(): return lax.ppermute(block, 'query', pairs)]
    all_to_all x0 -> x1, blocking collectives: none -> 19.9 us  [per_device(): lax.all_to_all(chip_sum.reshape(Y_LO * X, train_rows, query_rows), 'layer...]
    dot_general x1 -> x7, matrix products: 15.1 us -> 28.4 us  [the longest x5 24.2 us: per_device(): lax.dot_general(rows, query_flat, (((1,), (1,)), ((), ())), preferred_ele...]
    gather x1 -> x0, local copies, waits for them, and re-layouts: 8.54 us -> none  [per_device(): ordered = partial_sum[train_order] * factor]
    mul x1, other arithmetic: 4.97 us -> 0.73 us  [per_device(): return jnp.sum(pieces.astype(jnp.float32), axis=0) * factor]
  transfers between devices with their start and end apart: 2 -> 16, of which waited for: 2 -> 7; matrix products, arithmetic and copies ran while one was open for 0% -> 18% of each run, Pallas kernels for 0% -> 0%
where the time goes in v1:
time: 119 us; the launch traced here: 118 us
  waiting for transfers between devices  32.4 us (27%)
  matrix products  31.2 us (26%)
  starting transfers between devices  30.5 us (26%)
  blocking collectives  19.9 us (17%)
  local copies, waits for them, and re-layouts  3.07 us (3%)
    dot_general x5, matrix products, per_device(): lax.dot_general(rows, query_flat, (((1,), (1,)), ((), ())), preferred_ele...  24.2 us
    ppermute x10, waiting for transfers between devices, along_z(): return lax.ppermute(block, 'query', pairs)  20.8 us
    all_to_all x1, blocking collectives, per_device(): lax.all_to_all(chip_sum.reshape(Y_LO * X, train_rows, query_rows), 'layer...  19.9 us
    ppermute x10, starting transfers between devices, along_z(): return lax.ppermute(block, 'query', pairs)  16.2 us
    ppermute x5, waiting for transfers between devices, across_y(): return lax.ppermute(block, 'query', pairs)  9.32 us
    ppermute x5, starting transfers between devices, across_y(): return lax.ppermute(block, 'query', pairs)  9.15 us
    ppermute x1, starting transfers between devices, across_cores(): return lax.ppermute(block, 'layer', pairs)  5.2 us
    dot_general x2, matrix products, ordered(): lax.dot_general(pick.astype(jnp.bfloat16), partial_sum, (((1,), (0,)), ((...  4.19 us
  transfers between devices with their start and end apart: 16, of which 7 were waited for; matrix products, arithmetic and copies ran while one was open for 18% of the time, Pallas kernels for 0%

profile of v1, /device:TPU:1, one launch (start us, length us, event | category | flops | bytes accessed | tf_op | source)
XLA Modules:
  0.0 118.3 jit_solution(18331432818529228751)
XLA Ops:
  0.0 2.1 %reshape.46 = bf16[64,64,64]{2,1,0:T(8,128)(2,1)S(1)} reshape(bf16[64,1,4096]{2,0,1:T(8,128)(2,1)} %param.7) | data formatting | bytes 1048576 | tf_op jit(solution)/shard_map/reshape.1
  2.1 1.1 fusion.94
  3.2 1.8 %fusion.92 = f32[64,64,64]{2,1,0:T(8,128)S(1)} fusion(f32[64,64,64]{1,2,0:T(8,128)S(1)} %fusion.94, f32[1,64,64]{2,1,0:T(8,128)S(1)} %copy-done.1), kind=kOutput, calls=%fused_computation.58 | convolution fusion | flops 201326592 | bytes 2113536 | tf_op jit(solution)/shard_map/lab,elac,lcd->elbd/dot_general | solution.py:54
  5.0 0.0 copy-start.2
  5.0 0.0 copy-start.3
  5.0 0.7 transpose.11
  5.6 0.0 copy-done.2
  5.7 0.1 divide_convert_fusion
  5.8 2.5 %collective-permute-start = (bf16[64,4096]{1,0:T(8,128)(2,1)S(1)}, bf16[64,4096]{1,0:T(8,128)(2,1)S(1)}, u32[]{:S(2)}, u32[]{:S(2)}) collective-permute-start(bf16[64,4096]{1,0:T(8,128)(2,1)S(1)} %divide_convert_fusion), channel_id=1, source_target_pairs={{0,2},{1,3},{2,4},{3,5},{4,6},{5,7},{6,8},{7,9},{8,10},{9,11},{10,... | collective-permute-start | bytes 1572872 | tf_op jit(solution)/shard_map/ppermute | solution.py:18
  8.3 4.0 %collective-permute-start.1 = (bf16[64,4096]{1,0:T(8,128)(2,1)S(1)}, bf16[64,4096]{1,0:T(8,128)(2,1)S(1)}, u32[]{:S(2)}, u32[]{:S(2)}) collective-permute-start(bf16[64,4096]{1,0:T(8,128)(2,1)S(1)} %divide_convert_fusion), channel_id=1, source_target_pairs={{0,14},{1,15},{2,0},{3,1},{4,2},{5,3},{6,4},{7,5},{8,6},{9,7},{10,... | collective-permute-start | bytes 1572872 | tf_op jit(solution)/shard_map/ppermute | solution.py:18
  12.3 2.9 %collective-permute-start.2 = (bf16[64,4096]{1,0:T(8,128)(2,1)S(1)}, bf16[64,4096]{1,0:T(8,128)(2,1)S(1)}, u32[]{:S(2)}, u32[]{:S(2)}) collective-permute-start(bf16[64,4096]{1,0:T(8,128)(2,1)S(1)} %divide_convert_fusion), channel_id=1, source_target_pairs={{0,1},{1,0},{2,3},{3,2},{4,5},{5,4},{6,7},{7,6},{8,9},{9,8},{10,11... | collective-permute-start | bytes 1572872 | tf_op jit(solution)/shard_map/ppermute | solution.py:23
  15.3 0.1 reshape.45
  15.4 0.1 eq.140
  15.5 8.4 %collective-permute-done = bf16[64,4096]{1,0:T(8,128)(2,1)S(1)} collective-permute-done((bf16[64,4096]{1,0:T(8,128)(2,1)S(1)}, bf16[64,4096]{1,0:T(8,128)(2,1)S(1)}, u32[]{:S(2)}, u32[]{:S(2)}) %collective-permute-start) | collective-permute-done | bytes 524320 | tf_op jit(solution)/shard_map/ppermute | solution.py:18
  23.9 2.9 %collective-permute-start.5 = (bf16[64,4096]{1,0:T(8,128)(2,1)S(1)}, bf16[64,4096]{1,0:T(8,128)(2,1)S(1)}, u32[]{:S(2)}, u32[]{:S(2)}) collective-permute-start(bf16[64,4096]{1,0:T(8,128)(2,1)S(1)} %collective-permute-done), channel_id=1, source_target_pairs={{0,1},{1,0},{2,3},{3,2},{4,5},{5,4},{6,7},{7,6},{8,9},{9,8},{10,11... | collective-permute-start | bytes 1572872 | tf_op jit(solution)/shard_map/ppermute | solution.py:23
  26.8 0.0 collective-permute-start.3
  26.8 0.0 collective-permute-done.1
  26.8 2.7 %collective-permute-start.4 = (bf16[64,4096]{1,0:T(8,128)(2,1)S(1)}, bf16[64,4096]{1,0:T(8,128)(2,1)S(1)}, u32[]{:S(2)}, u32[]{:S(2)}) collective-permute-start(bf16[64,4096]{1,0:T(8,128)(2,1)S(1)} %collective-permute-done.1), channel_id=1, source_target_pairs={{0,14},{1,15},{2,0},{3,1},{4,2},{5,3},{6,4},{7,5},{8,6},{9,7},{10,... | collective-permute-start | bytes 1572872 | tf_op jit(solution)/shard_map/ppermute | solution.py:18
  29.5 0.1 collective-permute-start.8
  29.5 0.0 collective-permute-done.2
  29.5 5.7 %fusion.45 = bf16[1024,1024]{1,0:T(8,128)(2,1)S(1)} fusion(bf16[1024,1,4096]{2,0,1:T(8,128)(2,1)} %param.6, bf16[64,4096]{1,0:T(8,128)(2,1)S(1)} %collective-permute-done.2, bf16[64,4096]{1,0:T(8,128)(2,1)S(1)} %collective-permute-done.1, bf16[64,4096]{1,0:T(8,128)(2,1)S(1)} %collective-permute-done, bf16[64,4096]{1,0:T(8,128)(2,1)S(1)} %divide_convert_fusion), kind=kOutput, calls=%fused_computation.45 | convolution fusion | flops 2156134400 | bytes 11010048 | tf_op jit(solution)/shard_map/dot_general | solution.py:75
  35.3 4.6 %collective-permute-done.3 = bf16[64,4096]{1,0:T(8,128)(2,1)S(1)} collective-permute-done((bf16[64,4096]{1,0:T(8,128)(2,1)S(1)}, bf16[64,4096]{1,0:T(8,128)(2,1)S(1)}, u32[]{:S(2)}, u32[]{:S(2)}) %collective-permute-start.3) | collective-permute-done | bytes 524320 | tf_op jit(solution)/shard_map/ppermute | solution.py:18
  39.9 0.0 collective-permute-start.6
  39.9 0.1 collective-permute-start.11
  40.0 2.7 %collective-permute-start.7 = (bf16[64,4096]{1,0:T(8,128)(2,1)S(1)}, bf16[64,4096]{1,0:T(8,128)(2,1)S(1)}, u32[]{:S(2)}, u32[]{:S(2)}) collective-permute-start(bf16[64,4096]{1,0:T(8,128)(2,1)S(1)} %collective-permute-done.4), channel_id=1, source_target_pairs={{0,14},{1,15},{2,0},{3,1},{4,2},{5,3},{6,4},{7,5},{8,6},{9,7},{10,... | collective-permute-start | bytes 1572872 | tf_op jit(solution)/shard_map/ppermute | solution.py:18
  42.7 6.2 %collective-permute-done.8 = bf16[64,4096]{1,0:T(8,128)(2,1)S(1)} collective-permute-done((bf16[64,4096]{1,0:T(8,128)(2,1)S(1)}, bf16[64,4096]{1,0:T(8,128)(2,1)S(1)}, u32[]{:S(2)}, u32[]{:S(2)}) %collective-permute-start.8) | collective-permute-done | bytes 524320 | tf_op jit(solution)/shard_map/ppermute | solution.py:23
  48.8 0.8 collective-permute-start.10
  49.6 6.4 %fusion.85 = bf16[1024,1024]{1,0:T(8,128)(2,1)S(1)} fusion(bf16[1024,1024]{1,0:T(8,128)(2,1)S(1)} %fusion.45, bf16[1024,1,4096]{2,0,1:T(8,128)(2,1)} %param.6, bf16[64,4096]{1,0:T(8,128)(2,1)S(1)} %collective-permute-done.5, bf16[64,4096]{1,0:T(8,128)(2,1)S(1)} %collective-permute-done.4, bf16[64,4096]{1,0:T(8,128)(2,1)S(1)} %collective-permute-done.3), kind=kOutput, calls=%fused_computation.53 | convolution fusion | flops 1615527936 | bytes 10354688 | tf_op jit(solution)/shard_map/dot_general | solution.py:75
  56.1 0.0 slice-start.1
  56.1 0.0 collective-permute-done.6
  56.1 0.7 collective-permute-start.9
  56.8 6.0 %collective-permute-done.10 = bf16[64,4096]{1,0:T(8,128)(2,1)S(1)} collective-permute-done((bf16[64,4096]{1,0:T(8,128)(2,1)S(1)}, bf16[64,4096]{1,0:T(8,128)(2,1)S(1)}, u32[]{:S(2)}, u32[]{:S(2)}) %collective-permute-start.10) | collective-permute-done | bytes 524320 | tf_op jit(solution)/shard_map/ppermute | solution.py:18
  62.8 2.7 %collective-permute-start.13 = (bf16[64,4096]{1,0:T(8,128)(2,1)S(1)}, bf16[64,4096]{1,0:T(8,128)(2,1)S(1)}, u32[]{:S(2)}, u32[]{:S(2)}) collective-permute-start(bf16[64,4096]{1,0:T(8,128)(2,1)S(1)} %collective-permute-done.10), channel_id=1, source_target_pairs={{0,14},{1,15},{2,0},{3,1},{4,2},{5,3},{6,4},{7,5},{8,6},{9,7},{10,... | collective-permute-start | bytes 1572872 | tf_op jit(solution)/shard_map/ppermute | solution.py:18
  65.5 6.3 %fusion.80 = bf16[1024,1024]{1,0:T(8,128)(2,1)S(1)} fusion(bf16[1024,1024]{1,0:T(8,128)(2,1)S(1)} %fusion.85, bf16[1024,1,4096]{2,0,1:T(8,128)(2,1)} %param.6, bf16[64,4096]{1,0:T(8,128)(2,1)S(1)} %collective-permute-done.8, bf16[64,4096]{1,0:T(8,128)(2,1)S(1)} %collective-permute-done.7, bf16[64,4096]{1,0:T(8,128)(2,1)S(1)} %collective-permute-done.6), kind=kOutput, calls=%fused_computation.52 | convolution fusion | flops 1615527936 | bytes 10354688 | tf_op jit(solution)/shard_map/dot_general | solution.py:75
  71.8 0.0 collective-permute-done.9
  71.8 3.2 %collective-permute-start.14 = (bf16[64,4096]{1,0:T(8,128)(2,1)S(1)}, bf16[64,4096]{1,0:T(8,128)(2,1)S(1)}, u32[]{:S(2)}, u32[]{:S(2)}) collective-permute-start(bf16[64,4096]{1,0:T(8,128)(2,1)S(1)} %collective-permute-done.9), channel_id=1, source_target_pairs={{0,1},{1,0},{2,3},{3,2},{4,5},{5,4},{6,7},{7,6},{8,9},{9,8},{10,11... | collective-permute-start | bytes 1572872 | tf_op jit(solution)/shard_map/ppermute | solution.py:23
  75.1 2.9 %fusion.75 = bf16[1024,1024]{1,0:T(8,128)(2,1)S(1)} fusion(bf16[1024,1024]{1,0:T(8,128)(2,1)S(1)} %fusion.80, bf16[1024,1,4096]{2,0,1:T(8,128)(2,1)S(1)} %bitcast.50, bf16[64,4096]{1,0:T(8,128)(2,1)S(1)} %collective-permute-done.11, bf16[64,4096]{1,0:T(8,128)(2,1)S(1)} %collective-permute-done.10, bf16[64,4096]{1,0:T(8,128)(2,1)S(1)} %collective-permute-done.9), kind=kOutput, calls=%fused_computation.51 | convolution fusion | flops 1615527936 | bytes 10354688 | tf_op jit(solution)/shard_map/dot_general | solution.py:75
  78.0 1.8 %collective-permute-done.12 = bf16[64,4096]{1,0:T(8,128)(2,1)S(1)} collective-permute-done((bf16[64,4096]{1,0:T(8,128)(2,1)S(1)}, bf16[64,4096]{1,0:T(8,128)(2,1)S(1)}, u32[]{:S(2)}, u32[]{:S(2)}) %collective-permute-start.12) | collective-permute-done | bytes 524320 | tf_op jit(solution)/shard_map/ppermute | solution.py:18
  79.7 3.2 %collective-permute-done.14 = bf16[64,4096]{1,0:T(8,128)(2,1)S(1)} collective-permute-done((bf16[64,4096]{1,0:T(8,128)(2,1)S(1)}, bf16[64,4096]{1,0:T(8,128)(2,1)S(1)}, u32[]{:S(2)}, u32[]{:S(2)}) %collective-permute-start.14) | collective-permute-done | bytes 524320 | tf_op jit(solution)/shard_map/ppermute | solution.py:23
  82.9 2.9 %fusion.70 = bf16[1024,1024]{1,0:T(8,128)(2,1)S(1)} fusion(bf16[1024,1024]{1,0:T(8,128)(2,1)S(1)} %fusion.75, bf16[1024,1,4096]{2,0,1:T(8,128)(2,1)S(1)} %bitcast.50, bf16[64,4096]{1,0:T(8,128)(2,1)S(1)} %collective-permute-done.14, bf16[64,4096]{1,0:T(8,128)(2,1)S(1)} %collective-permute-done.13, bf16[64,4096]{1,0:T(8,128)(2,1)S(1)} %collective-permute-done.12), kind=kOutput, calls=%fused_computation.50 | convolution fusion | flops 1615527936 | bytes 10354688 | tf_op jit(solution)/shard_map/dot_general | solution.py:75
  85.8 1.3 %fusion.39 = bf16[512,1024]{1,0:T(8,128)(2,1)S(1)} fusion(bf16[1024,1024]{1,0:T(8,128)(2,1)S(1)} %fusion.70, s32[512]{0:T(512)S(1)} %eq.140), kind=kOutput, calls=%fused_computation.43 | convolution fusion | flops 1074790400 | bytes 3147776 | tf_op jit(solution)/shard_map/dot_general | solution.py:92
  87.1 5.2 %collective-permute-start.15 = (bf16[512,1024]{1,0:T(8,128)(2,1)S(1)}, bf16[512,1024]{1,0:T(8,128)(2,1)S(1)}, u32[]{:S(2)}, u32[]{:S(2)}) collective-permute-start(bf16[512,1024]{1,0:T(8,128)(2,1)S(1)} %fusion.39), channel_id=1, source_target_pairs={{0,16},{16,0},{32,48},{48,32},{64,80},{80,64},{96,112},{112,96},{1... | collective-permute-start | bytes 3145736 | tf_op jit(solution)/shard_map/ppermute | solution.py:28
  92.3 0.1 eq.136
  92.4 2.2 %collective-permute-done.15 = bf16[512,1024]{1,0:T(8,128)(2,1)S(1)} collective-permute-done((bf16[512,1024]{1,0:T(8,128)(2,1)S(1)}, bf16[512,1024]{1,0:T(8,128)(2,1)S(1)}, u32[]{:S(2)}, u32[]{:S(2)}) %collective-permute-start.15) | collective-permute-done | bytes 1048608 | tf_op jit(solution)/shard_map/ppermute | solution.py:28
  94.6 2.9 %add_convert_fusion = bf16[512,1024]{1,0:T(8,128)(2,1)S(1)} fusion(bf16[512,1024]{1,0:T(8,128)(2,1)S(1)} %collective-permute-done.15, bf16[1024,1024]{1,0:T(8,128)(2,1)} %copy-done.4, s32[512]{0:T(512)S(1)} %eq.136), kind=kOutput, calls=%fused_computation.18 | convolution fusion | flops 1075838976 | bytes 4196352 | tf_op jit(solution)/shard_map/dot_general | solution.py:92
  97.5 19.9 %all_to_all.5 = bf16[8,64,1024]{2,1,0:T(8,128)(2,1)S(1)} all-to-all(bf16[8,64,1024]{2,1,0:T(8,128)(2,1)S(1)} %bitcast.47), channel_id=1, replica_groups={{0,32,64,96,128,160,192,224},{16,48,80,112,144,176,208,240},{1,33,65,97..., dimensions={0} | all-to-all | bytes 2097152 | tf_op jit(solution)/shard_map/all_to_all | solution.py:102
  117.4 0.2 convert_reduce_fusion
  117.6 0.7 broadcast_multiply_fusion
  (19 shorter events, 0.1 us)
Async XLA Ops:
  0.0 2.1 %copy-start = (f32[1,64,64]{2,1,0:T(8,128)S(1)}, f32[1,64,64]{2,1,0:T(8,128)}, u32[]{:S(2)}) copy-start(f32[1,64,64]{2,1,0:T(8,128)} %param.8) | copy-start | bytes 49156
  0.0 3.2 %copy-start.1 = (f32[1,64,64]{2,1,0:T(8,128)S(1)}, f32[1,64,64]{2,1,0:T(8,128)}, u32[]{:S(2)}) copy-start(f32[1,64,64]{2,1,0:T(8,128)} %param.9) | copy-start | bytes 49156
  5.0 0.7 copy-start.2
  5.0 10.3 %copy-start.3 = (s32[1024]{0:T(1024)S(1)}, s32[1024]{0:T(1024)}, u32[]{:S(2)}) copy-start(s32[1024]{0:T(1024)} %param.11) | copy-start | bytes 12292
  5.8 18.1 %collective-permute-start = (bf16[64,4096]{1,0:T(8,128)(2,1)S(1)}, bf16[64,4096]{1,0:T(8,128)(2,1)S(1)}, u32[]{:S(2)}, u32[]{:S(2)}) collective-permute-start(bf16[64,4096]{1,0:T(8,128)(2,1)S(1)} %divide_convert_fusion), channel_id=1, source_target_pairs={{0,2},{1,3},{2,4},{3,5},{4,6},{5,7},{6,8},{7,9},{8,10},{9,11},{10,... | collective-permute-start | bytes 1572872 | tf_op jit(solution)/shard_map/ppermute | solution.py:18
  8.3 18.5 %collective-permute-start.1 = (bf16[64,4096]{1,0:T(8,128)(2,1)S(1)}, bf16[64,4096]{1,0:T(8,128)(2,1)S(1)}, u32[]{:S(2)}, u32[]{:S(2)}) collective-permute-start(bf16[64,4096]{1,0:T(8,128)(2,1)S(1)} %divide_convert_fusion), channel_id=1, source_target_pairs={{0,14},{1,15},{2,0},{3,1},{4,2},{5,3},{6,4},{7,5},{8,6},{9,7},{10,... | collective-permute-start | bytes 1572872 | tf_op jit(solution)/shard_map/ppermute | solution.py:18
  12.3 17.2 %collective-permute-start.2 = (bf16[64,4096]{1,0:T(8,128)(2,1)S(1)}, bf16[64,4096]{1,0:T(8,128)(2,1)S(1)}, u32[]{:S(2)}, u32[]{:S(2)}) collective-permute-start(bf16[64,4096]{1,0:T(8,128)(2,1)S(1)} %divide_convert_fusion), channel_id=1, source_target_pairs={{0,1},{1,0},{2,3},{3,2},{4,5},{5,4},{6,7},{7,6},{8,9},{9,8},{10,11... | collective-permute-start | bytes 1572872 | tf_op jit(solution)/shard_map/ppermute | solution.py:23
  23.9 25.8 %collective-permute-start.5 = (bf16[64,4096]{1,0:T(8,128)(2,1)S(1)}, bf16[64,4096]{1,0:T(8,128)(2,1)S(1)}, u32[]{:S(2)}, u32[]{:S(2)}) collective-permute-start(bf16[64,4096]{1,0:T(8,128)(2,1)S(1)} %collective-permute-done), channel_id=1, source_target_pairs={{0,1},{1,0},{2,3},{3,2},{4,5},{5,4},{6,7},{7,6},{8,9},{9,8},{10,11... | collective-permute-start | bytes 1572872 | tf_op jit(solution)/shard_map/ppermute | solution.py:23
  26.8 13.1 %collective-permute-start.3 = (bf16[64,4096]{1,0:T(8,128)(2,1)S(1)}, bf16[64,4096]{1,0:T(8,128)(2,1)S(1)}, u32[]{:S(2)}, u32[]{:S(2)}) collective-permute-start(bf16[64,4096]{1,0:T(8,128)(2,1)S(1)} %collective-permute-done), channel_id=1, source_target_pairs={{0,2},{1,3},{2,4},{3,5},{4,6},{5,7},{6,8},{7,9},{8,10},{9,11},{10,... | collective-permute-start | bytes 1572872 | tf_op jit(solution)/shard_map/ppermute | solution.py:18
  26.8 13.2 %collective-permute-start.4 = (bf16[64,4096]{1,0:T(8,128)(2,1)S(1)}, bf16[64,4096]{1,0:T(8,128)(2,1)S(1)}, u32[]{:S(2)}, u32[]{:S(2)}) collective-permute-start(bf16[64,4096]{1,0:T(8,128)(2,1)S(1)} %collective-permute-done.1), channel_id=1, source_target_pairs={{0,14},{1,15},{2,0},{3,1},{4,2},{5,3},{6,4},{7,5},{8,6},{9,7},{10,... | collective-permute-start | bytes 1572872 | tf_op jit(solution)/shard_map/ppermute | solution.py:18
  29.5 19.3 %collective-permute-start.8 = (bf16[64,4096]{1,0:T(8,128)(2,1)S(1)}, bf16[64,4096]{1,0:T(8,128)(2,1)S(1)}, u32[]{:S(2)}, u32[]{:S(2)}) collective-permute-start(bf16[64,4096]{1,0:T(8,128)(2,1)S(1)} %collective-permute-done.1), channel_id=1, source_target_pairs={{0,1},{1,0},{2,3},{3,2},{4,5},{5,4},{6,7},{7,6},{8,9},{9,8},{10,11... | collective-permute-start | bytes 1572872 | tf_op jit(solution)/shard_map/ppermute | solution.py:23
  39.9 16.2 %collective-permute-start.6 = (bf16[64,4096]{1,0:T(8,128)(2,1)S(1)}, bf16[64,4096]{1,0:T(8,128)(2,1)S(1)}, u32[]{:S(2)}, u32[]{:S(2)}) collective-permute-start(bf16[64,4096]{1,0:T(8,128)(2,1)S(1)} %collective-permute-done.3), channel_id=1, source_target_pairs={{0,2},{1,3},{2,4},{3,5},{4,6},{5,7},{6,8},{7,9},{8,10},{9,11},{10,... | collective-permute-start | bytes 1572872 | tf_op jit(solution)/shard_map/ppermute | solution.py:18
  39.9 25.6 %collective-permute-start.11 = (bf16[64,4096]{1,0:T(8,128)(2,1)S(1)}, bf16[64,4096]{1,0:T(8,128)(2,1)S(1)}, u32[]{:S(2)}, u32[]{:S(2)}) collective-permute-start(bf16[64,4096]{1,0:T(8,128)(2,1)S(1)} %collective-permute-done.3), channel_id=1, source_target_pairs={{0,1},{1,0},{2,3},{3,2},{4,5},{5,4},{6,7},{7,6},{8,9},{9,8},{10,11... | collective-permute-start | bytes 1572872 | tf_op jit(solution)/shard_map/ppermute | solution.py:23
  40.0 25.6 %collective-permute-start.7 = (bf16[64,4096]{1,0:T(8,128)(2,1)S(1)}, bf16[64,4096]{1,0:T(8,128)(2,1)S(1)}, u32[]{:S(2)}, u32[]{:S(2)}) collective-permute-start(bf16[64,4096]{1,0:T(8,128)(2,1)S(1)} %collective-permute-done.4), channel_id=1, source_target_pairs={{0,14},{1,15},{2,0},{3,1},{4,2},{5,3},{6,4},{7,5},{8,6},{9,7},{10,... | collective-permute-start | bytes 1572872 | tf_op jit(solution)/shard_map/ppermute | solution.py:18
  48.8 14.0 %collective-permute-start.10 = (bf16[64,4096]{1,0:T(8,128)(2,1)S(1)}, bf16[64,4096]{1,0:T(8,128)(2,1)S(1)}, u32[]{:S(2)}, u32[]{:S(2)}) collective-permute-start(bf16[64,4096]{1,0:T(8,128)(2,1)S(1)} %collective-permute-done.8), channel_id=1, source_target_pairs={{0,14},{1,15},{2,0},{3,1},{4,2},{5,3},{6,4},{7,5},{8,6},{9,7},{10,... | collective-permute-start | bytes 1572872 | tf_op jit(solution)/shard_map/ppermute | solution.py:18
  49.6 25.4 %slice-start = ((s8[8388608]{0:T(1024)(128)(4,1)}), s8[4194304]{0:T(1024)(128)(4,1)S(1)}, s32[]{:S(2)}) async-start(s8[8388608]{0:T(1024)(128)(4,1)} %bitcast.49), calls=%async_computation.1 | async-start | bytes 8388608
  56.1 19.0 %slice-start.1 = ((s8[8388608]{0:T(1024)(128)(4,1)}), s8[4194304]{0:T(1024)(128)(4,1)S(1)}, s32[]{:S(2)}) async-start(s8[8388608]{0:T(1024)(128)(4,1)} %bitcast.49), calls=%async_computation.2 | async-start | bytes 8388608
  56.1 15.7 %collective-permute-start.9 = (bf16[64,4096]{1,0:T(8,128)(2,1)S(1)}, bf16[64,4096]{1,0:T(8,128)(2,1)S(1)}, u32[]{:S(2)}, u32[]{:S(2)}) collective-permute-start(bf16[64,4096]{1,0:T(8,128)(2,1)S(1)} %collective-permute-done.6), channel_id=1, source_target_pairs={{0,2},{1,3},{2,4},{3,5},{4,6},{5,7},{6,8},{7,9},{8,10},{9,11},{10,... | collective-permute-start | bytes 1572872 | tf_op jit(solution)/shard_map/ppermute | solution.py:18
  62.8 15.1 %collective-permute-start.13 = (bf16[64,4096]{1,0:T(8,128)(2,1)S(1)}, bf16[64,4096]{1,0:T(8,128)(2,1)S(1)}, u32[]{:S(2)}, u32[]{:S(2)}) collective-permute-start(bf16[64,4096]{1,0:T(8,128)(2,1)S(1)} %collective-permute-done.10), channel_id=1, source_target_pairs={{0,14},{1,15},{2,0},{3,1},{4,2},{5,3},{6,4},{7,5},{8,6},{9,7},{10,... | collective-permute-start | bytes 1572872 | tf_op jit(solution)/shard_map/ppermute | solution.py:18
  65.5 14.2 %collective-permute-start.12 = (bf16[64,4096]{1,0:T(8,128)(2,1)S(1)}, bf16[64,4096]{1,0:T(8,128)(2,1)S(1)}, u32[]{:S(2)}, u32[]{:S(2)}) collective-permute-start(bf16[64,4096]{1,0:T(8,128)(2,1)S(1)} %collective-permute-done.11), channel_id=1, source_target_pairs={{0,2},{1,3},{2,4},{3,5},{4,6},{5,7},{6,8},{7,9},{8,10},{9,11},{10,... | collective-permute-start | bytes 1572872 | tf_op jit(solution)/shard_map/ppermute | solution.py:18
  71.8 11.0 %collective-permute-start.14 = (bf16[64,4096]{1,0:T(8,128)(2,1)S(1)}, bf16[64,4096]{1,0:T(8,128)(2,1)S(1)}, u32[]{:S(2)}, u32[]{:S(2)}) collective-permute-start(bf16[64,4096]{1,0:T(8,128)(2,1)S(1)} %collective-permute-done.9), channel_id=1, source_target_pairs={{0,1},{1,0},{2,3},{3,2},{4,5},{5,4},{6,7},{7,6},{8,9},{9,8},{10,11... | collective-permute-start | bytes 1572872 | tf_op jit(solution)/shard_map/ppermute | solution.py:23
  85.8 6.5 %copy-start.4 = (bf16[1024,1024]{1,0:T(8,128)(2,1)}, bf16[1024,1024]{1,0:T(8,128)(2,1)S(1)}, u32[]{:S(2)}) copy-start(bf16[1024,1024]{1,0:T(8,128)(2,1)S(1)} %fusion.70) | copy-start | bytes 6291460
  87.1 7.5 %collective-permute-start.15 = (bf16[512,1024]{1,0:T(8,128)(2,1)S(1)}, bf16[512,1024]{1,0:T(8,128)(2,1)S(1)}, u32[]{:S(2)}, u32[]{:S(2)}) collective-permute-start(bf16[512,1024]{1,0:T(8,128)(2,1)S(1)} %fusion.39), channel_id=1, source_target_pairs={{0,16},{16,0},{32,48},{48,32},{64,80},{80,64},{96,112},{112,96},{1... | collective-permute-start | bytes 3145736 | tf_op jit(solution)/shard_map/ppermute | solution.py:28

commit v2 on v1

--- a/solution.py
+++ b/solution.py
@@ -28,22 +28,35 @@
     return lax.ppermute(block, "layer", pairs)
 
 
+def together(*arrays):
+    return lax.optimization_barrier(arrays)
+
+
 def gather_steps(own):
     same, other = {0: own}, {}
     same[-1], same[1], other[0] = along_z(own, 1), along_z(own, -1), across_y(own)
-    yield [(0, 0, own), (0, -1, same[-1]), (0, 1, same[1]), (1, 0, other[0])]
+
+    same[-1], same[1] = together(same[-1], same[1])
     same[-2], same[2] = along_z(same[-1], 1), along_z(same[1], -1)
     other[-1] = across_y(same[-1])
+
+    same[-2], same[2], next_y, other[0] = together(same[-2], same[2], same[1], other[0])
+    same[-3], same[3] = along_z(same[-2], 1), along_z(same[2], -1)
+    other[1] = across_y(next_y)
+
+    same[-3], same[3], other[-1] = together(same[-3], same[3], other[-1])
+    other[-2], same[4] = along_z(other[-1], 1), along_z(same[3], -1)
+    other[3] = across_y(same[3])
+
+    other[-2], same[4], other[1] = together(other[-2], same[4], other[1])
+    other[-3], other[2] = along_z(other[-2], 1), along_z(other[1], -1)
+    other[4] = across_y(same[4])
+
+    yield [(0, 0, own), (0, -1, same[-1]), (0, 1, same[1]), (1, 0, other[0])]
     yield [(0, -2, same[-2]), (0, 2, same[2]), (1, -1, other[-1])]
-    same[-3], same[3] = along_z(same[-2], 1), along_z(same[2], -1)
-    other[1] = across_y(same[1])
     yield [(0, -3, same[-3]), (0, 3, same[3]), (1, 1, other[1])]
-    same[4], other[2] = along_z(same[-3], 1), along_z(other[1], -1)
-    other[-2] = across_y(same[-2])
-    yield [(0, 4, same[4]), (1, 2, other[2]), (1, -2, other[-2])]
-    other[-3], other[3] = along_z(other[-2], 1), along_z(other[2], -1)
-    other[4] = across_y(same[4])
-    yield [(1, -3, other[-3]), (1, 3, other[3]), (1, 4, other[4])]
+    yield [(1, -2, other[-2]), (0, 4, same[4]), (1, 3, other[3])]
+    yield [(1, -3, other[-3]), (1, 2, other[2]), (1, 4, other[4])]
 
 
 def per_device(queries, train_grads, basis_out, basis_in, eig_values, train_order):
@@ -76,8 +89,6 @@
                 rows, query_flat, (((1,), (1,)), ((), ())), preferred_element_type=jnp.float32
             ).astype(jnp.bfloat16)
         )
-    partial_sum = jnp.concatenate(products, axis=0)
-
     block_of = train_order // train_rows
     relative = ((block_of % Y_HI) ^ own_y) * Z + (block_of // Y_HI - own_z) % Z
     place = jnp.zeros_like(relative)
@@ -86,18 +97,30 @@
     place = place * train_rows + train_order % train_rows
     place = place.reshape(Y_LO * X, CORES, train_rows)
 
+    early = jnp.concatenate(products[:-1], axis=0)
+    early_rows = early.shape[0]
+
+    def pick(rows, first, count):
+        return (rows[:, None] == first + jnp.arange(count)[None, :]).astype(jnp.bfloat16)
+
+    def times(chosen, values):
+        return lax.dot_general(
+            chosen, values, (((1,), (0,)), ((), ())), preferred_element_type=jnp.float32
+        )
+
     def ordered(for_core):
         rows = lax.dynamic_index_in_dim(place, for_core, 1, keepdims=False).reshape(-1)
-        pick = rows[:, None] == jnp.arange(BLOCKS * train_rows)[None, :]
-        return lax.dot_general(
-            pick.astype(jnp.bfloat16),
-            partial_sum,
-            (((1,), (0,)), ((), ())),
-            preferred_element_type=jnp.float32,
-        )
+        before = times(pick(rows, 0, early_rows), early).astype(jnp.bfloat16)
+        late = pick(rows, early_rows, products[-1].shape[0])
+        return before, late
 
-    received = across_cores(ordered(1 - core).astype(jnp.bfloat16))
-    chip_sum = (ordered(core) + received.astype(jnp.float32)).astype(jnp.bfloat16)
+    other_before, other_late = ordered(1 - core)
+    own_before, own_late = ordered(core)
+    other_half = (other_before + times(other_late, products[-1])).astype(jnp.bfloat16)
+    received = across_cores(other_half)
+    own_half = (own_before + times(own_late, products[-1])).astype(jnp.bfloat16)
+    own_half, received = together(own_half, received)
+    chip_sum = (own_half.astype(jnp.float32) + received.astype(jnp.float32)).astype(jnp.bfloat16)
     groups = [[chip * CORES + c for chip in range(Y_LO * X)] for c in range(CORES)]
     pieces = lax.all_to_all(
         chip_sum.reshape(Y_LO * X, train_rows, query_rows),

time: 119 us -> 114 us (0.958)
  matrix products: 31.2 us -> 25.2 us
  starting transfers between devices: 30.5 us -> 35.3 us
  waiting for transfers between devices: 32.4 us -> 27.9 us
    ppermute x5, waiting for transfers between devices: 9.32 us -> 0.01 us  [across_y(): return lax.ppermute(block, 'query', pairs)]
    ppermute x10, waiting for transfers between devices: 20.8 us -> 27.8 us  [along_z(): return lax.ppermute(block, 'query', pairs)]
    dot_general x5, matrix products: 24.2 us -> 17.6 us  [per_device(): lax.dot_general(rows, query_flat, (((1,), (1,)), ((), ())), preferred_ele...]
    ppermute x1, starting transfers between devices: 5.2 us -> 8.28 us  [across_cores(): return lax.ppermute(block, 'layer', pairs)]
    ppermute x1, waiting for transfers between devices: 2.21 us -> 0.01 us  [across_cores(): return lax.ppermute(block, 'layer', pairs)]
    ppermute x5, starting transfers between devices: 9.15 us -> 11.3 us  [across_y(): return lax.ppermute(block, 'query', pairs)]
    dot_general x2 -> x4, matrix products: 4.19 us -> 4.74 us  [times(): lax.dot_general(chosen, values, (((1,), (0,)), ((), ())), preferred_eleme...]
  transfers between devices with their start and end apart: 16 -> 16, of which waited for: 7 -> 5; matrix products, arithmetic and copies ran while one was open for 18% -> 17% of each run, Pallas kernels for 0% -> 0%
where the time goes in v2:
time: 114 us
  starting transfers between devices  35.3 us (31%)
  waiting for transfers between devices  27.9 us (24%)
  matrix products  25.2 us (22%)
  blocking collectives  20.5 us (18%)
  local copies, waits for them, and re-layouts  3.07 us (3%)
  other arithmetic  1.41 us (1%)
    ppermute x10, waiting for transfers between devices, along_z(): return lax.ppermute(block, 'query', pairs)  27.8 us
    all_to_all x1, blocking collectives, per_device(): lax.all_to_all(chip_sum.reshape(Y_LO * X, train_rows, query_rows), 'layer...  20.5 us
    dot_general x5, matrix products, per_device(): lax.dot_general(rows, query_flat, (((1,), (1,)), ((), ())), preferred_ele...  17.6 us
    ppermute x10, starting transfers between devices, along_z(): return lax.ppermute(block, 'query', pairs)  15.7 us
    ppermute x5, starting transfers between devices, across_y(): return lax.ppermute(block, 'query', pairs)  11.3 us
    ppermute x1, starting transfers between devices, across_cores(): return lax.ppermute(block, 'layer', pairs)  8.28 us
    dot_general x4, matrix products, times(): lax.dot_general(chosen, values, (((1,), (0,)), ((), ())), preferred_eleme...  4.74 us
    dot_general x2, matrix products, per_device(): jnp.einsum('lab,elac,lcd->elbd', basis_out, grads_full, basis_in, precisi...  2.83 us
  transfers between devices with their start and end apart: 16, of which 5 were waited for; matrix products, arithmetic and copies ran while one was open for 17% of the time, Pallas kernels for 0%

profile of v2, /device:TPU:1, one launch (start us, length us, event | category | flops | bytes accessed | tf_op | source)
XLA Modules:
  0.0 113.6 jit_solution(14999639145126857571)
XLA Ops:
  0.0 2.1 %reshape.51 = bf16[64,64,64]{2,1,0:T(8,128)(2,1)S(1)} reshape(bf16[64,1,4096]{2,0,1:T(8,128)(2,1)} %param.7) | data formatting | bytes 1048576 | tf_op jit(solution)/shard_map/reshape.1
  2.1 1.1 fusion.76
  3.2 1.8 %fusion.74 = f32[64,64,64]{2,1,0:T(8,128)S(1)} fusion(f32[64,64,64]{1,2,0:T(8,128)S(1)} %fusion.76, f32[1,64,64]{2,1,0:T(8,128)S(1)} %copy-done.1), kind=kOutput, calls=%fused_computation.63 | convolution fusion | flops 201326592 | bytes 2113536 | tf_op jit(solution)/shard_map/lab,elac,lcd->elbd/dot_general | solution.py:67
  5.0 0.0 copy-start.2
  5.0 0.0 copy-start.3
  5.0 0.7 transpose.12
  5.6 0.0 copy-done.2
  5.7 0.1 divide_convert_fusion
  5.8 6.5 %collective-permute-start.1 = (bf16[64,4096]{1,0:T(8,128)(2,1)S(1)}, bf16[64,4096]{1,0:T(8,128)(2,1)S(1)}, u32[]{:S(2)}, u32[]{:S(2)}) collective-permute-start(bf16[64,4096]{1,0:T(8,128)(2,1)S(1)} %divide_convert_fusion), channel_id=1, source_target_pairs={{0,14},{1,15},{2,0},{3,1},{4,2},{5,3},{6,4},{7,5},{8,6},{9,7},{10,... | collective-permute-start | bytes 1572872 | tf_op jit(solution)/shard_map/ppermute | solution.py:18
  12.2 0.0 collective-permute-start
  12.2 2.9 %collective-permute-start.4 = (bf16[64,4096]{1,0:T(8,128)(2,1)S(1)}, bf16[64,4096]{1,0:T(8,128)(2,1)}, u32[]{:S(2)}, u32[]{:S(2)}) collective-permute-start(bf16[64,4096]{1,0:T(8,128)(2,1)S(1)} %divide_convert_fusion), channel_id=1, source_target_pairs={{0,1},{1,0},{2,3},{3,2},{4,5},{5,4},{6,7},{7,6},{8,9},{9,8},{10,11... | collective-permute-start | bytes 1572872 | tf_op jit(solution)/shard_map/ppermute | solution.py:23
  15.2 7.7 %collective-permute-done.1 = bf16[64,4096]{1,0:T(8,128)(2,1)S(1)} collective-permute-done((bf16[64,4096]{1,0:T(8,128)(2,1)S(1)}, bf16[64,4096]{1,0:T(8,128)(2,1)S(1)}, u32[]{:S(2)}, u32[]{:S(2)}) %collective-permute-start.1) | collective-permute-done | bytes 524320 | tf_op jit(solution)/shard_map/ppermute | solution.py:18
  22.8 3.2 %collective-permute-done = bf16[64,4096]{1,0:T(8,128)(2,1)S(1)} collective-permute-done((bf16[64,4096]{1,0:T(8,128)(2,1)S(1)}, bf16[64,4096]{1,0:T(8,128)(2,1)S(1)}, u32[]{:S(2)}, u32[]{:S(2)}) %collective-permute-start) | collective-permute-done | bytes 524320 | tf_op jit(solution)/shard_map/ppermute | solution.py:18
  26.0 0.0 collective-permute-start.2
  26.0 2.7 %collective-permute-start.3 = (bf16[64,4096]{1,0:T(8,128)(2,1)S(1)}, bf16[64,4096]{1,0:T(8,128)(2,1)S(1)}, u32[]{:S(2)}, u32[]{:S(2)}) collective-permute-start(bf16[64,4096]{1,0:T(8,128)(2,1)S(1)} %collective-permute-done.1), channel_id=1, source_target_pairs={{0,14},{1,15},{2,0},{3,1},{4,2},{5,3},{6,4},{7,5},{8,6},{9,7},{10,... | collective-permute-start | bytes 1572872 | tf_op jit(solution)/shard_map/ppermute | solution.py:18
  28.7 0.1 reshape.50
  28.9 0.1 eq.169
  28.9 2.9 %collective-permute-start.7 = (bf16[64,4096]{1,0:T(8,128)(2,1)S(1)}, bf16[64,4096]{1,0:T(8,128)(2,1)S(1)}, u32[]{:S(2)}, u32[]{:S(2)}) collective-permute-start(bf16[64,4096]{1,0:T(8,128)(2,1)S(1)} %collective-permute-done), channel_id=1, source_target_pairs={{0,1},{1,0},{2,3},{3,2},{4,5},{5,4},{6,7},{7,6},{8,9},{9,8},{10,11... | collective-permute-start | bytes 1572872 | tf_op jit(solution)/shard_map/ppermute | solution.py:23
  31.8 0.0 collective-permute-done.4
  31.8 7.1 %collective-permute-done.2 = bf16[64,4096]{1,0:T(8,128)(2,1)S(1)} collective-permute-done((bf16[64,4096]{1,0:T(8,128)(2,1)S(1)}, bf16[64,4096]{1,0:T(8,128)(2,1)S(1)}, u32[]{:S(2)}, u32[]{:S(2)}) %collective-permute-start.2) | collective-permute-done | bytes 524320 | tf_op jit(solution)/shard_map/ppermute | solution.py:18
  38.9 2.7 %collective-permute-start.10 = (bf16[64,4096]{1,0:T(8,128)(2,1)S(1)}, bf16[64,4096]{1,0:T(8,128)(2,1)S(1)}, u32[]{:S(2)}, u32[]{:S(2)}) collective-permute-start(bf16[64,4096]{1,0:T(8,128)(2,1)S(1)} %collective-permute-done.1), channel_id=1, source_target_pairs={{0,1},{1,0},{2,3},{3,2},{4,5},{5,4},{6,7},{7,6},{8,9},{9,8},{10,11... | collective-permute-start | bytes 1572872 | tf_op jit(solution)/shard_map/ppermute | solution.py:23
  41.6 2.7 %collective-permute-start.6 = (bf16[64,4096]{1,0:T(8,128)(2,1)S(1)}, bf16[64,4096]{1,0:T(8,128)(2,1)S(1)}, u32[]{:S(2)}, u32[]{:S(2)}) collective-permute-start(bf16[64,4096]{1,0:T(8,128)(2,1)S(1)} %collective-permute-done.3), channel_id=1, source_target_pairs={{0,14},{1,15},{2,0},{3,1},{4,2},{5,3},{6,4},{7,5},{8,6},{9,7},{10,... | collective-permute-start | bytes 1572872 | tf_op jit(solution)/shard_map/ppermute | solution.py:18
  44.3 5.9 %fusion.41 = bf16[256,1024]{1,0:T(8,128)(2,1)S(1)} fusion(bf16[1024,1,4096]{2,0,1:T(8,128)(2,1)} %param.6, bf16[64,4096]{1,0:T(8,128)(2,1)} %collective-permute-done.4, bf16[64,4096]{1,0:T(8,128)(2,1)S(1)} %collective-permute-done.1, bf16[64,4096]{1,0:T(8,128)(2,1)S(1)} %collective-permute-done, bf16[64,4096]{1,0:T(8,128)(2,1)S(1)} %divide_convert_fusion), kind=kOutput, calls=%fused_computation.48 | convolution fusion | flops 2156134400 | bytes 11010048 | tf_op jit(solution)/shard_map/dot_general | solution.py:88
  50.2 0.0 collective-permute-done.7
  50.2 2.9 %collective-permute-done.5 = bf16[64,4096]{1,0:T(8,128)(2,1)S(1)} collective-permute-done((bf16[64,4096]{1,0:T(8,128)(2,1)S(1)}, bf16[64,4096]{1,0:T(8,128)(2,1)S(1)}, u32[]{:S(2)}, u32[]{:S(2)}) %collective-permute-start.5) | collective-permute-done | bytes 524320 | tf_op jit(solution)/shard_map/ppermute | solution.py:18
  53.1 0.0 collective-permute-done.6
  53.1 0.4 collective-permute-start.11
  53.5 2.4 %collective-permute-start.9 = (bf16[64,4096]{1,0:T(8,128)(2,1)S(1)}, bf16[64,4096]{1,0:T(8,128)(2,1)S(1)}, u32[]{:S(2)}, u32[]{:S(2)}) collective-permute-start(bf16[64,4096]{1,0:T(8,128)(2,1)S(1)} %collective-permute-done.6), channel_id=1, source_target_pairs={{0,14},{1,15},{2,0},{3,1},{4,2},{5,3},{6,4},{7,5},{8,6},{9,7},{10,... | collective-permute-start | bytes 1572872 | tf_op jit(solution)/shard_map/ppermute | solution.py:18
  55.9 0.0 collective-permute-start.8
  56.0 2.9 %fusion.46 = bf16[192,1024]{1,0:T(8,128)(2,1)S(1)} fusion(bf16[1024,1,4096]{2,0,1:T(8,128)(2,1)S(1)} %bitcast.40, bf16[64,4096]{1,0:T(8,128)(2,1)S(1)} %collective-permute-done.7, bf16[64,4096]{1,0:T(8,128)(2,1)S(1)} %collective-permute-done.3, bf16[64,4096]{1,0:T(8,128)(2,1)S(1)} %collective-permute-done.2), kind=kOutput, calls=%fused_computation.49 | convolution fusion | flops 1615527936 | bytes 10354688 | tf_op jit(solution)/shard_map/dot_general | solution.py:88
  58.9 0.0 collective-permute-done.10
  58.9 7.0 %collective-permute-done.8 = bf16[64,4096]{1,0:T(8,128)(2,1)S(1)} collective-permute-done((bf16[64,4096]{1,0:T(8,128)(2,1)S(1)}, bf16[64,4096]{1,0:T(8,128)(2,1)S(1)}, u32[]{:S(2)}, u32[]{:S(2)}) %collective-permute-start.8) | collective-permute-done | bytes 524320 | tf_op jit(solution)/shard_map/ppermute | solution.py:18
  65.8 0.3 collective-permute-start.13
  66.1 1.2 %collective-permute-start.12 = (bf16[64,4096]{1,0:T(8,128)(2,1)S(1)}, bf16[64,4096]{1,0:T(8,128)(2,1)S(1)}, u32[]{:S(2)}, u32[]{:S(2)}) collective-permute-start(bf16[64,4096]{1,0:T(8,128)(2,1)S(1)} %collective-permute-done.8), channel_id=1, source_target_pairs={{0,2},{1,3},{2,4},{3,5},{4,6},{5,7},{6,8},{7,9},{8,10},{9,11},{10,... | collective-permute-start | bytes 1572872 | tf_op jit(solution)/shard_map/ppermute | solution.py:18
  67.3 2.4 %collective-permute-start.14 = (bf16[64,4096]{1,0:T(8,128)(2,1)S(1)}, bf16[64,4096]{1,0:T(8,128)(2,1)S(1)}, u32[]{:S(2)}, u32[]{:S(2)}) collective-permute-start(bf16[64,4096]{1,0:T(8,128)(2,1)S(1)} %collective-permute-done.9), channel_id=1, source_target_pairs={{0,1},{1,0},{2,3},{3,2},{4,5},{5,4},{6,7},{7,6},{8,9},{9,8},{10,11... | collective-permute-start | bytes 1572872 | tf_op jit(solution)/shard_map/ppermute | solution.py:23
  69.8 2.9 %fusion.51 = bf16[192,1024]{1,0:T(8,128)(2,1)S(1)} fusion(bf16[1024,1,4096]{2,0,1:T(8,128)(2,1)S(1)} %bitcast.40, bf16[64,4096]{1,0:T(8,128)(2,1)S(1)} %collective-permute-done.10, bf16[64,4096]{1,0:T(8,128)(2,1)S(1)} %collective-permute-done.6, bf16[64,4096]{1,0:T(8,128)(2,1)S(1)} %collective-permute-done.5), kind=kOutput, calls=%fused_computation.50 | convolution fusion | flops 1615527936 | bytes 10354688 | tf_op jit(solution)/shard_map/dot_general | solution.py:88
  72.7 2.9 %fusion.56 = bf16[192,1024]{1,0:T(8,128)(2,1)S(1)} fusion(bf16[1024,1,4096]{2,0,1:T(8,128)(2,1)S(1)} %bitcast.40, bf16[64,4096]{1,0:T(8,128)(2,1)S(1)} %collective-permute-done.11, bf16[64,4096]{1,0:T(8,128)(2,1)S(1)} %collective-permute-done.9, bf16[64,4096]{1,0:T(8,128)(2,1)S(1)} %collective-permute-done.8), kind=kOutput, calls=%fused_computation.51 | convolution fusion | flops 1615527936 | bytes 10354688 | tf_op jit(solution)/shard_map/dot_general | solution.py:88
  75.7 1.3 %fusion.39 = bf16[512,1024]{1,0:T(8,128)(2,1)S(1)} fusion(s32[512]{0:T(512)S(1)} %eq.169, bf16[192,1024]{1,0:T(8,128)(2,1)S(1)} %fusion.56, bf16[192,1024]{1,0:T(8,128)(2,1)S(1)} %fusion.51, bf16[192,1024]{1,0:T(8,128)(2,1)S(1)} %fusion.46, bf16[256,1024]{1,0:T(8,128)(2,1)S(1)} %fusion.41), kind=kOutput, calls=%fused_computation.46 | convolution fusion | flops 880181248 | bytes 2754560 | tf_op jit(solution)/shard_map/dot_general | solution.py:107
  77.0 2.9 %fusion.61 = bf16[192,1024]{1,0:T(8,128)(2,1)S(1)} fusion(bf16[1024,1,4096]{2,0,1:T(8,128)(2,1)S(1)} %bitcast.40, bf16[64,4096]{1,0:T(8,128)(2,1)S(1)} %collective-permute-done.14, bf16[64,4096]{1,0:T(8,128)(2,1)S(1)} %collective-permute-done.13, bf16[64,4096]{1,0:T(8,128)(2,1)S(1)} %collective-permute-done.12), kind=kOutput, calls=%fused_computation.52 | convolution fusion | flops 1615527936 | bytes 10354688 | tf_op jit(solution)/shard_map/dot_general | solution.py:88
  79.9 0.5 add_convert_fusion.1
  80.4 8.3 %collective-permute-start.15 = (bf16[512,1024]{1,0:T(8,128)(2,1)S(1)}, bf16[512,1024]{1,0:T(8,128)(2,1)S(1)}, u32[]{:S(2)}, u32[]{:S(2)}) collective-permute-start(bf16[512,1024]{1,0:T(8,128)(2,1)S(1)} %add_convert_fusion.1), channel_id=1, source_target_pairs={{0,16},{16,0},{32,48},{48,32},{64,80},{80,64},{96,112},{112,96},{1... | collective-permute-start | bytes 3145736 | tf_op jit(solution)/shard_map/ppermute | solution.py:28
  88.7 0.1 eq.162
  88.8 2.5 %fusion.40 = bf16[512,1024]{1,0:T(8,128)(2,1)S(1)} fusion(s32[512]{0:T(512)S(1)} %eq.162, bf16[192,1024]{1,0:T(8,128)(2,1)} %copy-done.4, bf16[192,1024]{1,0:T(8,128)(2,1)S(1)} %fusion.51, bf16[192,1024]{1,0:T(8,128)(2,1)S(1)} %fusion.46, bf16[256,1024]{1,0:T(8,128)(2,1)} %copy-done.5), kind=kOutput, calls=%fused_computation.47 | convolution fusion | flops 880181248 | bytes 2754560 | tf_op jit(solution)/shard_map/dot_general | solution.py:107
  91.3 0.5 add_convert_fusion.2
  91.8 0.4 add_convert_fusion
  92.2 20.5 %all_to_all.5 = bf16[8,64,1024]{2,1,0:T(8,128)(2,1)S(1)} all-to-all(bf16[8,64,1024]{2,1,0:T(8,128)(2,1)S(1)} %bitcast.37), channel_id=1, replica_groups={{0,32,64,96,128,160,192,224},{16,48,80,112,144,176,208,240},{1,33,65,97..., dimensions={0} | all-to-all | bytes 2097152 | tf_op jit(solution)/shard_map/all_to_all | solution.py:125
  112.7 0.2 convert_reduce_fusion
  112.8 0.7 broadcast_multiply_fusion
  (25 shorter events, 0.1 us)
Async XLA Ops:
  0.0 2.1 %copy-start = (f32[1,64,64]{2,1,0:T(8,128)S(1)}, f32[1,64,64]{2,1,0:T(8,128)}, u32[]{:S(2)}) copy-start(f32[1,64,64]{2,1,0:T(8,128)} %param.8) | copy-start | bytes 49156
  0.0 3.2 %copy-start.1 = (f32[1,64,64]{2,1,0:T(8,128)S(1)}, f32[1,64,64]{2,1,0:T(8,128)}, u32[]{:S(2)}) copy-start(f32[1,64,64]{2,1,0:T(8,128)} %param.9) | copy-start | bytes 49156
  5.0 0.7 copy-start.2
  5.0 23.7 %copy-start.3 = (s32[1024]{0:T(1024)S(1)}, s32[1024]{0:T(1024)}, u32[]{:S(2)}) copy-start(s32[1024]{0:T(1024)} %param.11) | copy-start | bytes 12292
  5.8 17.1 %collective-permute-start.1 = (bf16[64,4096]{1,0:T(8,128)(2,1)S(1)}, bf16[64,4096]{1,0:T(8,128)(2,1)S(1)}, u32[]{:S(2)}, u32[]{:S(2)}) collective-permute-start(bf16[64,4096]{1,0:T(8,128)(2,1)S(1)} %divide_convert_fusion), channel_id=1, source_target_pairs={{0,14},{1,15},{2,0},{3,1},{4,2},{5,3},{6,4},{7,5},{8,6},{9,7},{10,... | collective-permute-start | bytes 1572872 | tf_op jit(solution)/shard_map/ppermute | solution.py:18
  12.2 13.8 %collective-permute-start = (bf16[64,4096]{1,0:T(8,128)(2,1)S(1)}, bf16[64,4096]{1,0:T(8,128)(2,1)S(1)}, u32[]{:S(2)}, u32[]{:S(2)}) collective-permute-start(bf16[64,4096]{1,0:T(8,128)(2,1)S(1)} %divide_convert_fusion), channel_id=1, source_target_pairs={{0,2},{1,3},{2,4},{3,5},{4,6},{5,7},{6,8},{7,9},{8,10},{9,11},{10,... | collective-permute-start | bytes 1572872 | tf_op jit(solution)/shard_map/ppermute | solution.py:18
  12.2 19.6 %collective-permute-start.4 = (bf16[64,4096]{1,0:T(8,128)(2,1)S(1)}, bf16[64,4096]{1,0:T(8,128)(2,1)}, u32[]{:S(2)}, u32[]{:S(2)}) collective-permute-start(bf16[64,4096]{1,0:T(8,128)(2,1)S(1)} %divide_convert_fusion), channel_id=1, source_target_pairs={{0,1},{1,0},{2,3},{3,2},{4,5},{5,4},{6,7},{7,6},{8,9},{9,8},{10,11... | collective-permute-start | bytes 1572872 | tf_op jit(solution)/shard_map/ppermute | solution.py:23
  26.0 12.9 %collective-permute-start.2 = (bf16[64,4096]{1,0:T(8,128)(2,1)S(1)}, bf16[64,4096]{1,0:T(8,128)(2,1)S(1)}, u32[]{:S(2)}, u32[]{:S(2)}) collective-permute-start(bf16[64,4096]{1,0:T(8,128)(2,1)S(1)} %collective-permute-done), channel_id=1, source_target_pairs={{0,2},{1,3},{2,4},{3,5},{4,6},{5,7},{6,8},{7,9},{8,10},{9,11},{10,... | collective-permute-start | bytes 1572872 | tf_op jit(solution)/shard_map/ppermute | solution.py:18
  26.0 12.9 %collective-permute-start.3 = (bf16[64,4096]{1,0:T(8,128)(2,1)S(1)}, bf16[64,4096]{1,0:T(8,128)(2,1)S(1)}, u32[]{:S(2)}, u32[]{:S(2)}) collective-permute-start(bf16[64,4096]{1,0:T(8,128)(2,1)S(1)} %collective-permute-done.1), channel_id=1, source_target_pairs={{0,14},{1,15},{2,0},{3,1},{4,2},{5,3},{6,4},{7,5},{8,6},{9,7},{10,... | collective-permute-start | bytes 1572872 | tf_op jit(solution)/shard_map/ppermute | solution.py:18
  28.9 27.0 %slice-start = ((s8[8388608]{0:T(1024)(128)(4,1)}), s8[4194304]{0:T(1024)(128)(4,1)S(1)}, s32[]{:S(2)}) async-start(s8[8388608]{0:T(1024)(128)(4,1)} %bitcast.39), calls=%async_computation.1 | async-start | bytes 8388608
  28.9 27.0 %slice-start.1 = ((s8[8388608]{0:T(1024)(128)(4,1)}), s8[4194304]{0:T(1024)(128)(4,1)S(1)}, s32[]{:S(2)}) async-start(s8[8388608]{0:T(1024)(128)(4,1)} %bitcast.39), calls=%async_computation.2 | async-start | bytes 8388608
  28.9 21.3 %collective-permute-start.7 = (bf16[64,4096]{1,0:T(8,128)(2,1)S(1)}, bf16[64,4096]{1,0:T(8,128)(2,1)S(1)}, u32[]{:S(2)}, u32[]{:S(2)}) collective-permute-start(bf16[64,4096]{1,0:T(8,128)(2,1)S(1)} %collective-permute-done), channel_id=1, source_target_pairs={{0,1},{1,0},{2,3},{3,2},{4,5},{5,4},{6,7},{7,6},{8,9},{9,8},{10,11... | collective-permute-start | bytes 1572872 | tf_op jit(solution)/shard_map/ppermute | solution.py:23
  38.9 20.0 %collective-permute-start.10 = (bf16[64,4096]{1,0:T(8,128)(2,1)S(1)}, bf16[64,4096]{1,0:T(8,128)(2,1)S(1)}, u32[]{:S(2)}, u32[]{:S(2)}) collective-permute-start(bf16[64,4096]{1,0:T(8,128)(2,1)S(1)} %collective-permute-done.1), channel_id=1, source_target_pairs={{0,1},{1,0},{2,3},{3,2},{4,5},{5,4},{6,7},{7,6},{8,9},{9,8},{10,11... | collective-permute-start | bytes 1572872 | tf_op jit(solution)/shard_map/ppermute | solution.py:23
  41.6 11.6 %collective-permute-start.5 = (bf16[64,4096]{1,0:T(8,128)(2,1)S(1)}, bf16[64,4096]{1,0:T(8,128)(2,1)S(1)}, u32[]{:S(2)}, u32[]{:S(2)}) collective-permute-start(bf16[64,4096]{1,0:T(8,128)(2,1)S(1)} %collective-permute-done.2), channel_id=1, source_target_pairs={{0,2},{1,3},{2,4},{3,5},{4,6},{5,7},{6,8},{7,9},{8,10},{9,11},{10,... | collective-permute-start | bytes 1572872 | tf_op jit(solution)/shard_map/ppermute | solution.py:18
  41.6 11.6 %collective-permute-start.6 = (bf16[64,4096]{1,0:T(8,128)(2,1)S(1)}, bf16[64,4096]{1,0:T(8,128)(2,1)S(1)}, u32[]{:S(2)}, u32[]{:S(2)}) collective-permute-start(bf16[64,4096]{1,0:T(8,128)(2,1)S(1)} %collective-permute-done.3), channel_id=1, source_target_pairs={{0,14},{1,15},{2,0},{3,1},{4,2},{5,3},{6,4},{7,5},{8,6},{9,7},{10,... | collective-permute-start | bytes 1572872 | tf_op jit(solution)/shard_map/ppermute | solution.py:18
  50.2 25.4 %copy-start.5 = (bf16[256,1024]{1,0:T(8,128)(2,1)}, bf16[256,1024]{1,0:T(8,128)(2,1)S(1)}, u32[]{:S(2)}) copy-start(bf16[256,1024]{1,0:T(8,128)(2,1)S(1)} %fusion.41) | copy-start | bytes 1572868
  53.1 19.5 %collective-permute-start.11 = (bf16[64,4096]{1,0:T(8,128)(2,1)S(1)}, bf16[64,4096]{1,0:T(8,128)(2,1)S(1)}, u32[]{:S(2)}, u32[]{:S(2)}) collective-permute-start(bf16[64,4096]{1,0:T(8,128)(2,1)S(1)} %collective-permute-done.6), channel_id=1, source_target_pairs={{0,1},{1,0},{2,3},{3,2},{4,5},{5,4},{6,7},{7,6},{8,9},{9,8},{10,11... | collective-permute-start | bytes 1572872 | tf_op jit(solution)/shard_map/ppermute | solution.py:23
  53.5 12.3 %collective-permute-start.9 = (bf16[64,4096]{1,0:T(8,128)(2,1)S(1)}, bf16[64,4096]{1,0:T(8,128)(2,1)S(1)}, u32[]{:S(2)}, u32[]{:S(2)}) collective-permute-start(bf16[64,4096]{1,0:T(8,128)(2,1)S(1)} %collective-permute-done.6), channel_id=1, source_target_pairs={{0,14},{1,15},{2,0},{3,1},{4,2},{5,3},{6,4},{7,5},{8,6},{9,7},{10,... | collective-permute-start | bytes 1572872 | tf_op jit(solution)/shard_map/ppermute | solution.py:18
  55.9 9.9 %collective-permute-start.8 = (bf16[64,4096]{1,0:T(8,128)(2,1)S(1)}, bf16[64,4096]{1,0:T(8,128)(2,1)S(1)}, u32[]{:S(2)}, u32[]{:S(2)}) collective-permute-start(bf16[64,4096]{1,0:T(8,128)(2,1)S(1)} %collective-permute-done.7), channel_id=1, source_target_pairs={{0,2},{1,3},{2,4},{3,5},{4,6},{5,7},{6,8},{7,9},{8,10},{9,11},{10,... | collective-permute-start | bytes 1572872 | tf_op jit(solution)/shard_map/ppermute | solution.py:18
  65.8 11.1 %collective-permute-start.13 = (bf16[64,4096]{1,0:T(8,128)(2,1)S(1)}, bf16[64,4096]{1,0:T(8,128)(2,1)S(1)}, u32[]{:S(2)}, u32[]{:S(2)}) collective-permute-start(bf16[64,4096]{1,0:T(8,128)(2,1)S(1)} %collective-permute-done.10), channel_id=1, source_target_pairs={{0,14},{1,15},{2,0},{3,1},{4,2},{5,3},{6,4},{7,5},{8,6},{9,7},{10,... | collective-permute-start | bytes 1572872 | tf_op jit(solution)/shard_map/ppermute | solution.py:18
  66.1 10.9 %collective-permute-start.12 = (bf16[64,4096]{1,0:T(8,128)(2,1)S(1)}, bf16[64,4096]{1,0:T(8,128)(2,1)S(1)}, u32[]{:S(2)}, u32[]{:S(2)}) collective-permute-start(bf16[64,4096]{1,0:T(8,128)(2,1)S(1)} %collective-permute-done.8), channel_id=1, source_target_pairs={{0,2},{1,3},{2,4},{3,5},{4,6},{5,7},{6,8},{7,9},{8,10},{9,11},{10,... | collective-permute-start | bytes 1572872 | tf_op jit(solution)/shard_map/ppermute | solution.py:18
  67.3 9.7 %collective-permute-start.14 = (bf16[64,4096]{1,0:T(8,128)(2,1)S(1)}, bf16[64,4096]{1,0:T(8,128)(2,1)S(1)}, u32[]{:S(2)}, u32[]{:S(2)}) collective-permute-start(bf16[64,4096]{1,0:T(8,128)(2,1)S(1)} %collective-permute-done.9), channel_id=1, source_target_pairs={{0,1},{1,0},{2,3},{3,2},{4,5},{5,4},{6,7},{7,6},{8,9},{9,8},{10,11... | collective-permute-start | bytes 1572872 | tf_op jit(solution)/shard_map/ppermute | solution.py:23
  75.6 4.3 %copy-start.4 = (bf16[192,1024]{1,0:T(8,128)(2,1)}, bf16[192,1024]{1,0:T(8,128)(2,1)S(1)}, u32[]{:S(2)}) copy-start(bf16[192,1024]{1,0:T(8,128)(2,1)S(1)} %fusion.56) | copy-start | bytes 1179652
  80.4 11.3 %collective-permute-start.15 = (bf16[512,1024]{1,0:T(8,128)(2,1)S(1)}, bf16[512,1024]{1,0:T(8,128)(2,1)S(1)}, u32[]{:S(2)}, u32[]{:S(2)}) collective-permute-start(bf16[512,1024]{1,0:T(8,128)(2,1)S(1)} %add_convert_fusion.1), channel_id=1, source_target_pairs={{0,16},{16,0},{32,48},{48,32},{64,80},{80,64},{96,112},{112,96},{1... | collective-permute-start | bytes 3145736 | tf_op jit(solution)/shard_map/ppermute | solution.py:28

commit v3 on v2

--- a/solution.py
+++ b/solution.py
@@ -8,7 +8,6 @@
 X = 4
 Y_LO = 2
 CORES = 2
-BLOCKS = Z * Y_HI
 
 
 def along_z(block, step):
@@ -33,30 +32,49 @@
 
 
 def gather_steps(own):
-    same, other = {0: own}, {}
-    same[-1], same[1], other[0] = along_z(own, 1), along_z(own, -1), across_y(own)
+    half = own.shape[0] // 2
 
-    same[-1], same[1] = together(same[-1], same[1])
-    same[-2], same[2] = along_z(same[-1], 1), along_z(same[1], -1)
-    other[-1] = across_y(same[-1])
+    def upper(block):
+        return block[:half]
 
-    same[-2], same[2], next_y, other[0] = together(same[-2], same[2], same[1], other[0])
-    same[-3], same[3] = along_z(same[-2], 1), along_z(same[2], -1)
-    other[1] = across_y(next_y)
+    def lower(block):
+        return block[half:]
 
-    same[-3], same[3], other[-1] = together(same[-3], same[3], other[-1])
-    other[-2], same[4] = along_z(other[-1], 1), along_z(same[3], -1)
-    other[3] = across_y(same[3])
+    def join(first, second):
+        return jnp.concatenate([first, second], axis=0)
 
-    other[-2], same[4], other[1] = together(other[-2], same[4], other[1])
-    other[-3], other[2] = along_z(other[-2], 1), along_z(other[1], -1)
-    other[4] = across_y(same[4])
+    def whole(column, offset):
+        return [(column, offset, 0), (column, offset, 1)]
 
-    yield [(0, 0, own), (0, -1, same[-1]), (0, 1, same[1]), (1, 0, other[0])]
-    yield [(0, -2, same[-2]), (0, 2, same[2]), (1, -1, other[-1])]
-    yield [(0, -3, same[-3]), (0, 3, same[3]), (1, 1, other[1])]
-    yield [(1, -2, other[-2]), (0, 4, same[4]), (1, 3, other[3])]
-    yield [(1, -3, other[-3]), (1, 2, other[2]), (1, 4, other[4])]
+    back1, front1, across0 = along_z(own, 1), along_z(own, -1), across_y(own)
+
+    back1, front1 = together(back1, front1)
+    back2, front2 = along_z(back1, 1), along_z(front1, -1)
+    across1 = across_y(join(upper(back1), lower(front1)))
+
+    back2, front2, across0 = together(back2, front2, across0)
+    back3, front3 = along_z(back2, 1), along_z(front2, -1)
+    across2 = across_y(join(upper(front2), lower(back2)))
+
+    back3, front3, across1 = together(back3, front3, across1)
+    back4 = along_z(join(upper(back3), upper(across1)), 1)
+    front4 = along_z(join(lower(front3), lower(across1)), -1)
+    across3 = across_y(join(upper(back3), lower(front3)))
+
+    back4, front4, across2 = together(back4, front4, across2)
+    back5 = along_z(join(lower(across0), lower(across2)), 1)
+    front5 = along_z(join(upper(across0), upper(across2)), -1)
+    across4 = across_y(join(upper(back4), upper(front4)))
+
+    yield [own, back1, front1, across0], whole(0, 0) + whole(0, -1) + whole(0, 1) + whole(1, 0)
+    yield [back2, front2, across1], whole(0, -2) + whole(0, 2) + [(1, -1, 0), (1, 1, 1)]
+    yield [back3, front3, across2], whole(0, -3) + whole(0, 3) + [(1, 2, 0), (1, -2, 1)]
+    yield [back4, front4, across3], [
+        (0, 4, 0), (1, -2, 0), (0, 4, 1), (1, 2, 1), (1, -3, 0), (1, 3, 1)
+    ]
+    yield [back5, front5, across4], [
+        (1, -1, 1), (1, -3, 1), (1, 1, 0), (1, 3, 0), (1, 4, 0), (1, 4, 1)
+    ]
 
 
 def per_device(queries, train_grads, basis_out, basis_in, eig_values, train_order):
@@ -65,7 +83,7 @@
     side = basis_out.shape[1]
     grads_full = train_grads.astype(jnp.float32).reshape(train_rows, local_layers, side, side)
     rotated = jnp.einsum(
-        "lab,elac,lcd->elbd", basis_out, grads_full, basis_in, precision=lax.Precision.HIGHEST
+        "lab,elac,lcd->elbd", basis_out, grads_full, basis_in, precision=lax.Precision.HIGH
     )
     scaled = (rotated.reshape(train_rows, local_layers, feat_size) / eig_values[None]).astype(
         jnp.bfloat16
@@ -81,20 +99,24 @@
     own_z, own_y = query // Y_HI, query % Y_HI
 
     arrived, products = [], []
-    for step in gather_steps(scaled_flat):
-        arrived += [(column, offset % Z) for column, offset, _ in step]
-        rows = jnp.concatenate([block for _, _, block in step], axis=0)
+    for blocks, names in gather_steps(scaled_flat):
+        arrived += names
+        rows = jnp.concatenate(blocks, axis=0)
         products.append(
             lax.dot_general(
                 rows, query_flat, (((1,), (1,)), ((), ())), preferred_element_type=jnp.float32
             ).astype(jnp.bfloat16)
         )
-    block_of = train_order // train_rows
+
+    half_rows = train_rows // 2
+    half_of = train_order // half_rows
+    block_of = half_of // 2
     relative = ((block_of % Y_HI) ^ own_y) * Z + (block_of // Y_HI - own_z) % Z
+    relative = relative * 2 + half_of % 2
     place = jnp.zeros_like(relative)
-    for at, (column, offset) in enumerate(arrived):
-        place = jnp.where(relative == column * Z + offset, at, place)
-    place = place * train_rows + train_order % train_rows
+    for at, (column, offset, part) in enumerate(arrived):
+        place = jnp.where(relative == (column * Z + offset % Z) * 2 + part, at, place)
+    place = place * half_rows + train_order % half_rows
     place = place.reshape(Y_LO * X, CORES, train_rows)
 
     early = jnp.concatenate(products[:-1], axis=0)
@@ -120,7 +142,8 @@
     received = across_cores(other_half)
     own_half = (own_before + times(own_late, products[-1])).astype(jnp.bfloat16)
     own_half, received = together(own_half, received)
-    chip_sum = (own_half.astype(jnp.float32) + received.astype(jnp.float32)).astype(jnp.bfloat16)
+    chip_sum = own_half.astype(jnp.float32) + received.astype(jnp.float32)
+    chip_sum = (chip_sum * factor).astype(jnp.bfloat16)
     groups = [[chip * CORES + c for chip in range(Y_LO * X)] for c in range(CORES)]
     pieces = lax.all_to_all(
         chip_sum.reshape(Y_LO * X, train_rows, query_rows),
@@ -130,7 +153,7 @@
         axis_index_groups=groups,
         tiled=True,
     )
-    return jnp.sum(pieces.astype(jnp.float32), axis=0) * factor
+    return jnp.sum(pieces.astype(jnp.float32), axis=0)
 
 
 def solution(mesh):

time: 114 us -> 111 us (0.974)
  waiting for transfers between devices: 27.9 us -> 26 us
  matrix products: 25.2 us -> 23.9 us
    ppermute x10, waiting for transfers between devices: 27.8 us -> 25.7 us  [along_z(): return lax.ppermute(block, 'query', pairs)]
    ppermute x1, starting transfers between devices: 8.28 us -> 6.41 us  [across_cores(): return lax.ppermute(block, 'layer', pairs)]
  transfers between devices with their start and end apart: 16 -> 16, of which waited for: 5 -> 7; matrix products, arithmetic and copies ran while one was open for 17% -> 18% of each run, Pallas kernels for 0% -> 0%
where the time goes in v3:
time: 111 us
  starting transfers between devices  35 us (32%)
  waiting for transfers between devices  26 us (23%)
  matrix products  23.9 us (22%)
  blocking collectives  20.5 us (18%)
  local copies, waits for them, and re-layouts  3.33 us (3%)
  other arithmetic  1.75 us (2%)
    ppermute x10, waiting for transfers between devices, along_z(): return lax.ppermute(block, 'query', pairs)  25.7 us
    all_to_all x1, blocking collectives, per_device(): lax.all_to_all(chip_sum.reshape(Y_LO * X, train_rows, query_rows), 'layer...  20.5 us
    dot_general x5, matrix products, per_device(): lax.dot_general(rows, query_flat, (((1,), (1,)), ((), ())), preferred_ele...  17.4 us
    ppermute x10, starting transfers between devices, along_z(): return lax.ppermute(block, 'query', pairs)  16.4 us
    ppermute x5, starting transfers between devices, across_y(): return lax.ppermute(block, 'query', pairs)  12.2 us
    ppermute x1, starting transfers between devices, across_cores(): return lax.ppermute(block, 'layer', pairs)  6.41 us
    dot_general x4, matrix products, times(): lax.dot_general(chosen, values, (((1,), (0,)), ((), ())), preferred_eleme...  4.74 us
  transfers between devices with their start and end apart: 16, of which 7 were waited for; matrix products, arithmetic and copies ran while one was open for 18% of the time, Pallas kernels for 0%

profile of v3, /device:TPU:1, one launch (start us, length us, event | category | flops | bytes accessed | tf_op | source)
XLA Modules:
  0.0 110.8 jit_solution(3189585064115961531)
XLA Ops:
  0.0 2.1 %reshape.51 = bf16[64,64,64]{2,1,0:T(8,128)(2,1)S(1)} reshape(bf16[64,1,4096]{2,0,1:T(8,128)(2,1)} %param.7) | data formatting | bytes 1048576 | tf_op jit(solution)/shard_map/reshape.1
  2.1 0.8 fusion.76
  2.9 1.0 fusion.74
  3.9 0.0 copy-start.2
  3.9 0.0 copy-start.3
  3.9 0.7 transpose.12
  4.5 0.0 copy-done.2
  4.6 0.1 divide_convert_fusion
  4.7 6.5 %collective-permute-start.1 = (bf16[64,4096]{1,0:T(8,128)(2,1)S(1)}, bf16[64,4096]{1,0:T(8,128)(2,1)S(1)}, u32[]{:S(2)}, u32[]{:S(2)}) collective-permute-start(bf16[64,4096]{1,0:T(8,128)(2,1)S(1)} %divide_convert_fusion), channel_id=1, source_target_pairs={{0,14},{1,15},{2,0},{3,1},{4,2},{5,3},{6,4},{7,5},{8,6},{9,7},{10,... | collective-permute-start | bytes 1572872 | tf_op jit(solution)/shard_map/ppermute | solution.py:17
  11.2 2.9 %collective-permute-start.4 = (bf16[64,4096]{1,0:T(8,128)(2,1)S(1)}, bf16[64,4096]{1,0:T(8,128)(2,1)S(1)}, u32[]{:S(2)}, u32[]{:S(2)}) collective-permute-start(bf16[64,4096]{1,0:T(8,128)(2,1)S(1)} %divide_convert_fusion), channel_id=1, source_target_pairs={{0,1},{1,0},{2,3},{3,2},{4,5},{5,4},{6,7},{7,6},{8,9},{9,8},{10,11... | collective-permute-start | bytes 1572872 | tf_op jit(solution)/shard_map/ppermute | solution.py:22
  14.1 0.1 fusion.85
  14.1 0.1 reshape.50
  14.2 0.1 eq.264
  14.3 7.4 %collective-permute-done.1 = bf16[64,4096]{1,0:T(8,128)(2,1)S(1)} collective-permute-done((bf16[64,4096]{1,0:T(8,128)(2,1)S(1)}, bf16[64,4096]{1,0:T(8,128)(2,1)S(1)}, u32[]{:S(2)}, u32[]{:S(2)}) %collective-permute-start.1) | collective-permute-done | bytes 524320 | tf_op jit(solution)/shard_map/ppermute | solution.py:17
  21.7 3.1 %collective-permute-done = bf16[64,4096]{1,0:T(8,128)(2,1)S(1)} collective-permute-done((bf16[64,4096]{1,0:T(8,128)(2,1)S(1)}, bf16[64,4096]{1,0:T(8,128)(2,1)S(1)}, u32[]{:S(2)}, u32[]{:S(2)}) %collective-permute-start) | collective-permute-done | bytes 524320 | tf_op jit(solution)/shard_map/ppermute | solution.py:17
  24.8 2.7 %collective-permute-start.3 = (bf16[64,4096]{1,0:T(8,128)(2,1)S(1)}, bf16[64,4096]{1,0:T(8,128)(2,1)S(1)}, u32[]{:S(2)}, u32[]{:S(2)}) collective-permute-start(bf16[64,4096]{1,0:T(8,128)(2,1)S(1)} %collective-permute-done.1), channel_id=1, source_target_pairs={{0,14},{1,15},{2,0},{3,1},{4,2},{5,3},{6,4},{7,5},{8,6},{9,7},{10,... | collective-permute-start | bytes 1572872 | tf_op jit(solution)/shard_map/ppermute | solution.py:17
  27.6 3.0 %collective-permute-start.7 = (bf16[64,4096]{1,0:T(8,128)(2,1)S(1)}, bf16[64,4096]{1,0:T(8,128)(2,1)S(1)}, u32[]{:S(2)}, u32[]{:S(2)}) collective-permute-start(bf16[64,4096]{1,0:T(8,128)(2,1)S(1)} %pad_maximum_fusion.3), channel_id=1, source_target_pairs={{0,1},{1,0},{2,3},{3,2},{4,5},{5,4},{6,7},{7,6},{8,9},{9,8},{10,11... | collective-permute-start | bytes 1572872 | tf_op jit(solution)/shard_map/ppermute | solution.py:22
  30.6 7.0 %collective-permute-done.2 = bf16[64,4096]{1,0:T(8,128)(2,1)S(1)} collective-permute-done((bf16[64,4096]{1,0:T(8,128)(2,1)S(1)}, bf16[64,4096]{1,0:T(8,128)(2,1)S(1)}, u32[]{:S(2)}, u32[]{:S(2)}) %collective-permute-start.2) | collective-permute-done | bytes 524320 | tf_op jit(solution)/shard_map/ppermute | solution.py:17
  37.6 0.1 collective-permute-start.5
  37.7 2.7 %collective-permute-start.6 = (bf16[64,4096]{1,0:T(8,128)(2,1)S(1)}, bf16[64,4096]{1,0:T(8,128)(2,1)S(1)}, u32[]{:S(2)}, u32[]{:S(2)}) collective-permute-start(bf16[64,4096]{1,0:T(8,128)(2,1)S(1)} %collective-permute-done.3), channel_id=1, source_target_pairs={{0,14},{1,15},{2,0},{3,1},{4,2},{5,3},{6,4},{7,5},{8,6},{9,7},{10,... | collective-permute-start | bytes 1572872 | tf_op jit(solution)/shard_map/ppermute | solution.py:17
  40.5 0.0 slice-start
  40.6 0.0 slice-start.1
  40.6 3.2 %collective-permute-start.10 = (bf16[64,4096]{1,0:T(8,128)(2,1)S(1)}, bf16[64,4096]{1,0:T(8,128)(2,1)S(1)}, u32[]{:S(2)}, u32[]{:S(2)}) collective-permute-start(bf16[64,4096]{1,0:T(8,128)(2,1)S(1)} %pad_maximum_fusion.5), channel_id=1, source_target_pairs={{0,1},{1,0},{2,3},{3,2},{4,5},{5,4},{6,7},{7,6},{8,9},{9,8},{10,11... | collective-permute-start | bytes 1572872 | tf_op jit(solution)/shard_map/ppermute | solution.py:22
  43.8 5.7 %fusion.41 = bf16[256,1024]{1,0:T(8,128)(2,1)S(1)} fusion(bf16[1024,1,4096]{2,0,1:T(8,128)(2,1)} %param.6, bf16[64,4096]{1,0:T(8,128)(2,1)S(1)} %collective-permute-done.4, bf16[64,4096]{1,0:T(8,128)(2,1)S(1)} %collective-permute-done.1, bf16[64,4096]{1,0:T(8,128)(2,1)S(1)} %collective-permute-done, bf16[64,4096]{1,0:T(8,128)(2,1)S(1)} %divide_convert_fusion), kind=kOutput, calls=%fused_computation.48 | convolution fusion | flops 2156134400 | bytes 11010048 | tf_op jit(solution)/shard_map/dot_general | solution.py:106
  49.5 0.0 collective-permute-done.5
  49.7 0.2 pad_maximum_fusion.4
  49.8 2.6 %collective-permute-start.9 = (bf16[64,4096]{1,0:T(8,128)(2,1)S(1)}, bf16[64,4096]{1,0:T(8,128)(2,1)S(1)}, u32[]{:S(2)}, u32[]{:S(2)}) collective-permute-start(bf16[64,4096]{1,0:T(8,128)(2,1)S(1)} %get-tuple-element.39), channel_id=1, source_target_pairs={{0,14},{1,15},{2,0},{3,1},{4,2},{5,3},{6,4},{7,5},{8,6},{9,7},{10,... | collective-permute-start | bytes 1572872 | tf_op jit(solution)/shard_map/ppermute | solution.py:17
  52.4 2.9 %collective-permute-start.11 = (bf16[64,4096]{1,0:T(8,128)(2,1)S(1)}, bf16[64,4096]{1,0:T(8,128)(2,1)S(1)}, u32[]{:S(2)}, u32[]{:S(2)}) collective-permute-start(bf16[64,4096]{1,0:T(8,128)(2,1)S(1)} %get-tuple-element.40), channel_id=1, source_target_pairs={{0,1},{1,0},{2,3},{3,2},{4,5},{5,4},{6,7},{7,6},{8,9},{9,8},{10,11... | collective-permute-start | bytes 1572872 | tf_op jit(solution)/shard_map/ppermute | solution.py:22
  55.3 2.9 %fusion.46 = bf16[192,1024]{1,0:T(8,128)(2,1)S(1)} fusion(bf16[1024,1,4096]{2,0,1:T(8,128)(2,1)S(1)} %bitcast.40, bf16[64,4096]{1,0:T(8,128)(2,1)S(1)} %collective-permute-done.7, bf16[64,4096]{1,0:T(8,128)(2,1)S(1)} %collective-permute-done.3, bf16[64,4096]{1,0:T(8,128)(2,1)S(1)} %collective-permute-done.2), kind=kOutput, calls=%fused_computation.49 | convolution fusion | flops 1615527936 | bytes 10354688 | tf_op jit(solution)/shard_map/dot_general | solution.py:106
  58.3 1.4 %collective-permute-done.9 = bf16[64,4096]{1,0:T(8,128)(2,1)S(1)} collective-permute-done((bf16[64,4096]{1,0:T(8,128)(2,1)S(1)}, bf16[64,4096]{1,0:T(8,128)(2,1)S(1)}, u32[]{:S(2)}, u32[]{:S(2)}) %collective-permute-start.9) | collective-permute-done | bytes 524320 | tf_op jit(solution)/shard_map/ppermute | solution.py:17
  59.6 5.8 %collective-permute-done.8 = bf16[64,4096]{1,0:T(8,128)(2,1)S(1)} collective-permute-done((bf16[64,4096]{1,0:T(8,128)(2,1)S(1)}, bf16[64,4096]{1,0:T(8,128)(2,1)S(1)}, u32[]{:S(2)}, u32[]{:S(2)}) %collective-permute-start.8) | collective-permute-done | bytes 524320 | tf_op jit(solution)/shard_map/ppermute | solution.py:17
  65.5 0.1 collective-permute-start.14
  65.7 0.6 collective-permute-start.13
  66.3 1.3 %collective-permute-start.12 = (bf16[64,4096]{1,0:T(8,128)(2,1)S(1)}, bf16[64,4096]{1,0:T(8,128)(2,1)S(1)}, u32[]{:S(2)}, u32[]{:S(2)}) collective-permute-start(bf16[64,4096]{1,0:T(8,128)(2,1)S(1)} %pad_maximum_fusion.6), channel_id=1, source_target_pairs={{0,2},{1,3},{2,4},{3,5},{4,6},{5,7},{6,8},{7,9},{8,10},{9,11},{10,... | collective-permute-start | bytes 1572872 | tf_op jit(solution)/shard_map/ppermute | solution.py:17
  67.6 2.9 %fusion.51 = bf16[192,1024]{1,0:T(8,128)(2,1)S(1)} fusion(bf16[1024,1,4096]{2,0,1:T(8,128)(2,1)S(1)} %bitcast.40, bf16[64,4096]{1,0:T(8,128)(2,1)S(1)} %collective-permute-done.10, bf16[64,4096]{1,0:T(8,128)(2,1)S(1)} %collective-permute-done.6, bf16[64,4096]{1,0:T(8,128)(2,1)S(1)} %collective-permute-done.5), kind=kOutput, calls=%fused_computation.50 | convolution fusion | flops 1615527936 | bytes 10354688 | tf_op jit(solution)/shard_map/dot_general | solution.py:106
  70.5 2.9 %fusion.56 = bf16[192,1024]{1,0:T(8,128)(2,1)S(1)} fusion(bf16[1024,1,4096]{2,0,1:T(8,128)(2,1)S(1)} %bitcast.40, bf16[64,4096]{1,0:T(8,128)(2,1)S(1)} %collective-permute-done.11, bf16[64,4096]{1,0:T(8,128)(2,1)S(1)} %collective-permute-done.9, bf16[64,4096]{1,0:T(8,128)(2,1)S(1)} %collective-permute-done.8), kind=kOutput, calls=%fused_computation.51 | convolution fusion | flops 1615527936 | bytes 10354688 | tf_op jit(solution)/shard_map/dot_general | solution.py:106
  73.5 1.3 %fusion.39 = bf16[512,1024]{1,0:T(8,128)(2,1)S(1)} fusion(s32[512]{0:T(512)S(1)} %eq.264, bf16[192,1024]{1,0:T(8,128)(2,1)S(1)} %fusion.56, bf16[192,1024]{1,0:T(8,128)(2,1)S(1)} %fusion.51, bf16[192,1024]{1,0:T(8,128)(2,1)S(1)} %fusion.46, bf16[256,1024]{1,0:T(8,128)(2,1)S(1)} %fusion.41), kind=kOutput, calls=%fused_computation.46 | convolution fusion | flops 880181248 | bytes 2754560 | tf_op jit(solution)/shard_map/dot_general | solution.py:129
  74.8 0.4 collective-permute-done.14
  75.2 1.0 collective-permute-done.12
  76.2 2.9 %fusion.61 = bf16[192,1024]{1,0:T(8,128)(2,1)S(1)} fusion(bf16[1024,1,4096]{2,0,1:T(8,128)(2,1)S(1)} %bitcast.40, bf16[64,4096]{1,0:T(8,128)(2,1)S(1)} %collective-permute-done.14, bf16[64,4096]{1,0:T(8,128)(2,1)S(1)} %collective-permute-done.13, bf16[64,4096]{1,0:T(8,128)(2,1)S(1)} %collective-permute-done.12), kind=kOutput, calls=%fused_computation.52 | convolution fusion | flops 1615527936 | bytes 10354688 | tf_op jit(solution)/shard_map/dot_general | solution.py:106
  79.1 0.5 add_convert_fusion
  79.6 6.4 %collective-permute-start.15 = (bf16[512,1024]{1,0:T(8,128)(2,1)S(1)}, bf16[512,1024]{1,0:T(8,128)(2,1)S(1)}, u32[]{:S(2)}, u32[]{:S(2)}) collective-permute-start(bf16[512,1024]{1,0:T(8,128)(2,1)S(1)} %add_convert_fusion), channel_id=1, source_target_pairs={{0,16},{16,0},{32,48},{48,32},{64,80},{80,64},{96,112},{112,96},{1... | collective-permute-start | bytes 3145736 | tf_op jit(solution)/shard_map/ppermute | solution.py:27
  86.0 0.1 eq.257
  86.1 2.5 %fusion.40 = bf16[512,1024]{1,0:T(8,128)(2,1)S(1)} fusion(s32[512]{0:T(512)S(1)} %eq.257, bf16[192,1024]{1,0:T(8,128)(2,1)} %copy-done.4, bf16[192,1024]{1,0:T(8,128)(2,1)S(1)} %fusion.51, bf16[192,1024]{1,0:T(8,128)(2,1)S(1)} %fusion.46, bf16[256,1024]{1,0:T(8,128)(2,1)} %copy-done.5), kind=kOutput, calls=%fused_computation.47 | convolution fusion | flops 880181248 | bytes 2754560 | tf_op jit(solution)/shard_map/dot_general | solution.py:129
  88.5 0.5 add_convert_fusion.1
  89.0 0.4 multiply_convert_fusion
  89.4 20.5 %all_to_all.5 = bf16[8,64,1024]{2,1,0:T(8,128)(2,1)S(1)} all-to-all(bf16[8,64,1024]{2,1,0:T(8,128)(2,1)S(1)} %bitcast.37), channel_id=1, replica_groups={{0,32,64,96,128,160,192,224},{16,48,80,112,144,176,208,240},{1,33,65,97..., dimensions={0} | all-to-all | bytes 2097152 | tf_op jit(solution)/shard_map/all_to_all | solution.py:148
  109.9 0.9 convert_reduce_fusion
  (41 shorter events, 0.5 us)
Async XLA Ops:
  0.0 2.1 %copy-start = (f32[1,64,64]{2,1,0:T(8,128)S(1)}, f32[1,64,64]{2,1,0:T(8,128)}, u32[]{:S(2)}) copy-start(f32[1,64,64]{2,1,0:T(8,128)} %param.8) | copy-start | bytes 49156
  0.0 2.9 %copy-start.1 = (f32[1,64,64]{2,1,0:T(8,128)S(1)}, f32[1,64,64]{2,1,0:T(8,128)}, u32[]{:S(2)}) copy-start(f32[1,64,64]{2,1,0:T(8,128)} %param.9) | copy-start | bytes 49156
  3.9 0.7 copy-start.2
  3.9 10.2 %copy-start.3 = (s32[1024]{0:T(1024)S(1)}, s32[1024]{0:T(1024)}, u32[]{:S(2)}) copy-start(s32[1024]{0:T(1024)} %param.11) | copy-start | bytes 12292
  4.7 17.1 %collective-permute-start.1 = (bf16[64,4096]{1,0:T(8,128)(2,1)S(1)}, bf16[64,4096]{1,0:T(8,128)(2,1)S(1)}, u32[]{:S(2)}, u32[]{:S(2)}) collective-permute-start(bf16[64,4096]{1,0:T(8,128)(2,1)S(1)} %divide_convert_fusion), channel_id=1, source_target_pairs={{0,14},{1,15},{2,0},{3,1},{4,2},{5,3},{6,4},{7,5},{8,6},{9,7},{10,... | collective-permute-start | bytes 1572872 | tf_op jit(solution)/shard_map/ppermute | solution.py:17
  11.2 13.7 %collective-permute-start = (bf16[64,4096]{1,0:T(8,128)(2,1)S(1)}, bf16[64,4096]{1,0:T(8,128)(2,1)S(1)}, u32[]{:S(2)}, u32[]{:S(2)}) collective-permute-start(bf16[64,4096]{1,0:T(8,128)(2,1)S(1)} %divide_convert_fusion), channel_id=1, source_target_pairs={{0,2},{1,3},{2,4},{3,5},{4,6},{5,7},{6,8},{7,9},{8,10},{9,11},{10,... | collective-permute-start | bytes 1572872 | tf_op jit(solution)/shard_map/ppermute | solution.py:17
  11.2 19.5 %collective-permute-start.4 = (bf16[64,4096]{1,0:T(8,128)(2,1)S(1)}, bf16[64,4096]{1,0:T(8,128)(2,1)S(1)}, u32[]{:S(2)}, u32[]{:S(2)}) collective-permute-start(bf16[64,4096]{1,0:T(8,128)(2,1)S(1)} %divide_convert_fusion), channel_id=1, source_target_pairs={{0,1},{1,0},{2,3},{3,2},{4,5},{5,4},{6,7},{7,6},{8,9},{9,8},{10,11... | collective-permute-start | bytes 1572872 | tf_op jit(solution)/shard_map/ppermute | solution.py:22
  24.8 12.8 %collective-permute-start.2 = (bf16[64,4096]{1,0:T(8,128)(2,1)S(1)}, bf16[64,4096]{1,0:T(8,128)(2,1)S(1)}, u32[]{:S(2)}, u32[]{:S(2)}) collective-permute-start(bf16[64,4096]{1,0:T(8,128)(2,1)S(1)} %collective-permute-done), channel_id=1, source_target_pairs={{0,2},{1,3},{2,4},{3,5},{4,6},{5,7},{6,8},{7,9},{8,10},{9,11},{10,... | collective-permute-start | bytes 1572872 | tf_op jit(solution)/shard_map/ppermute | solution.py:17
  24.8 12.8 %collective-permute-start.3 = (bf16[64,4096]{1,0:T(8,128)(2,1)S(1)}, bf16[64,4096]{1,0:T(8,128)(2,1)S(1)}, u32[]{:S(2)}, u32[]{:S(2)}) collective-permute-start(bf16[64,4096]{1,0:T(8,128)(2,1)S(1)} %collective-permute-done.1), channel_id=1, source_target_pairs={{0,14},{1,15},{2,0},{3,1},{4,2},{5,3},{6,4},{7,5},{8,6},{9,7},{10,... | collective-permute-start | bytes 1572872 | tf_op jit(solution)/shard_map/ppermute | solution.py:17
  27.6 21.9 %collective-permute-start.7 = (bf16[64,4096]{1,0:T(8,128)(2,1)S(1)}, bf16[64,4096]{1,0:T(8,128)(2,1)S(1)}, u32[]{:S(2)}, u32[]{:S(2)}) collective-permute-start(bf16[64,4096]{1,0:T(8,128)(2,1)S(1)} %pad_maximum_fusion.3), channel_id=1, source_target_pairs={{0,1},{1,0},{2,3},{3,2},{4,5},{5,4},{6,7},{7,6},{8,9},{9,8},{10,11... | collective-permute-start | bytes 1572872 | tf_op jit(solution)/shard_map/ppermute | solution.py:22
  37.6 11.9 %collective-permute-start.5 = (bf16[64,4096]{1,0:T(8,128)(2,1)S(1)}, bf16[64,4096]{1,0:T(8,128)(2,1)S(1)}, u32[]{:S(2)}, u32[]{:S(2)}) collective-permute-start(bf16[64,4096]{1,0:T(8,128)(2,1)S(1)} %collective-permute-done.2), channel_id=1, source_target_pairs={{0,2},{1,3},{2,4},{3,5},{4,6},{5,7},{6,8},{7,9},{8,10},{9,11},{10,... | collective-permute-start | bytes 1572872 | tf_op jit(solution)/shard_map/ppermute | solution.py:17
  37.7 11.8 %collective-permute-start.6 = (bf16[64,4096]{1,0:T(8,128)(2,1)S(1)}, bf16[64,4096]{1,0:T(8,128)(2,1)S(1)}, u32[]{:S(2)}, u32[]{:S(2)}) collective-permute-start(bf16[64,4096]{1,0:T(8,128)(2,1)S(1)} %collective-permute-done.3), channel_id=1, source_target_pairs={{0,14},{1,15},{2,0},{3,1},{4,2},{5,3},{6,4},{7,5},{8,6},{9,7},{10,... | collective-permute-start | bytes 1572872 | tf_op jit(solution)/shard_map/ppermute | solution.py:17
  40.5 14.8 %slice-start = ((s8[8388608]{0:T(1024)(128)(4,1)}), s8[4194304]{0:T(1024)(128)(4,1)S(1)}, s32[]{:S(2)}) async-start(s8[8388608]{0:T(1024)(128)(4,1)} %bitcast.39), calls=%async_computation.1 | async-start | bytes 8388608
  40.6 14.7 %slice-start.1 = ((s8[8388608]{0:T(1024)(128)(4,1)}), s8[4194304]{0:T(1024)(128)(4,1)S(1)}, s32[]{:S(2)}) async-start(s8[8388608]{0:T(1024)(128)(4,1)} %bitcast.39), calls=%async_computation.2 | async-start | bytes 8388608
  40.6 17.7 %collective-permute-start.10 = (bf16[64,4096]{1,0:T(8,128)(2,1)S(1)}, bf16[64,4096]{1,0:T(8,128)(2,1)S(1)}, u32[]{:S(2)}, u32[]{:S(2)}) collective-permute-start(bf16[64,4096]{1,0:T(8,128)(2,1)S(1)} %pad_maximum_fusion.5), channel_id=1, source_target_pairs={{0,1},{1,0},{2,3},{3,2},{4,5},{5,4},{6,7},{7,6},{8,9},{9,8},{10,11... | collective-permute-start | bytes 1572872 | tf_op jit(solution)/shard_map/ppermute | solution.py:22
  49.5 23.9 %copy-start.5 = (bf16[256,1024]{1,0:T(8,128)(2,1)}, bf16[256,1024]{1,0:T(8,128)(2,1)S(1)}, u32[]{:S(2)}) copy-start(bf16[256,1024]{1,0:T(8,128)(2,1)S(1)} %fusion.41) | copy-start | bytes 1572868
  49.8 9.8 %collective-permute-start.9 = (bf16[64,4096]{1,0:T(8,128)(2,1)S(1)}, bf16[64,4096]{1,0:T(8,128)(2,1)S(1)}, u32[]{:S(2)}, u32[]{:S(2)}) collective-permute-start(bf16[64,4096]{1,0:T(8,128)(2,1)S(1)} %get-tuple-element.39), channel_id=1, source_target_pairs={{0,14},{1,15},{2,0},{3,1},{4,2},{5,3},{6,4},{7,5},{8,6},{9,7},{10,... | collective-permute-start | bytes 1572872 | tf_op jit(solution)/shard_map/ppermute | solution.py:17
  52.4 18.1 %collective-permute-start.11 = (bf16[64,4096]{1,0:T(8,128)(2,1)S(1)}, bf16[64,4096]{1,0:T(8,128)(2,1)S(1)}, u32[]{:S(2)}, u32[]{:S(2)}) collective-permute-start(bf16[64,4096]{1,0:T(8,128)(2,1)S(1)} %get-tuple-element.40), channel_id=1, source_target_pairs={{0,1},{1,0},{2,3},{3,2},{4,5},{5,4},{6,7},{7,6},{8,9},{9,8},{10,11... | collective-permute-start | bytes 1572872 | tf_op jit(solution)/shard_map/ppermute | solution.py:22
  55.3 10.1 %collective-permute-start.8 = (bf16[64,4096]{1,0:T(8,128)(2,1)S(1)}, bf16[64,4096]{1,0:T(8,128)(2,1)S(1)}, u32[]{:S(2)}, u32[]{:S(2)}) collective-permute-start(bf16[64,4096]{1,0:T(8,128)(2,1)S(1)} %get-tuple-element.41), channel_id=1, source_target_pairs={{0,2},{1,3},{2,4},{3,5},{4,6},{5,7},{6,8},{7,9},{8,10},{9,11},{10,... | collective-permute-start | bytes 1572872 | tf_op jit(solution)/shard_map/ppermute | solution.py:17
  65.5 9.6 %collective-permute-start.14 = (bf16[64,4096]{1,0:T(8,128)(2,1)S(1)}, bf16[64,4096]{1,0:T(8,128)(2,1)S(1)}, u32[]{:S(2)}, u32[]{:S(2)}) collective-permute-start(bf16[64,4096]{1,0:T(8,128)(2,1)S(1)} %pad_maximum_fusion.8), channel_id=1, source_target_pairs={{0,1},{1,0},{2,3},{3,2},{4,5},{5,4},{6,7},{7,6},{8,9},{9,8},{10,11... | collective-permute-start | bytes 1572872 | tf_op jit(solution)/shard_map/ppermute | solution.py:22
  65.7 9.4 %collective-permute-start.13 = (bf16[64,4096]{1,0:T(8,128)(2,1)S(1)}, bf16[64,4096]{1,0:T(8,128)(2,1)S(1)}, u32[]{:S(2)}, u32[]{:S(2)}) collective-permute-start(bf16[64,4096]{1,0:T(8,128)(2,1)S(1)} %pad_maximum_fusion.7), channel_id=1, source_target_pairs={{0,14},{1,15},{2,0},{3,1},{4,2},{5,3},{6,4},{7,5},{8,6},{9,7},{10,... | collective-permute-start | bytes 1572872 | tf_op jit(solution)/shard_map/ppermute | solution.py:17
  66.3 9.8 %collective-permute-start.12 = (bf16[64,4096]{1,0:T(8,128)(2,1)S(1)}, bf16[64,4096]{1,0:T(8,128)(2,1)S(1)}, u32[]{:S(2)}, u32[]{:S(2)}) collective-permute-start(bf16[64,4096]{1,0:T(8,128)(2,1)S(1)} %pad_maximum_fusion.6), channel_id=1, source_target_pairs={{0,2},{1,3},{2,4},{3,5},{4,6},{5,7},{6,8},{7,9},{8,10},{9,11},{10,... | collective-permute-start | bytes 1572872 | tf_op jit(solution)/shard_map/ppermute | solution.py:17
  73.5 1.7 %copy-start.4 = (bf16[192,1024]{1,0:T(8,128)(2,1)}, bf16[192,1024]{1,0:T(8,128)(2,1)S(1)}, u32[]{:S(2)}) copy-start(bf16[192,1024]{1,0:T(8,128)(2,1)S(1)} %fusion.56) | copy-start | bytes 1179652
  79.6 9.5 %collective-permute-start.15 = (bf16[512,1024]{1,0:T(8,128)(2,1)S(1)}, bf16[512,1024]{1,0:T(8,128)(2,1)S(1)}, u32[]{:S(2)}, u32[]{:S(2)}) collective-permute-start(bf16[512,1024]{1,0:T(8,128)(2,1)S(1)} %add_convert_fusion), channel_id=1, source_target_pairs={{0,16},{16,0},{32,48},{48,32},{64,80},{80,64},{96,112},{112,96},{1... | collective-permute-start | bytes 3145736 | tf_op jit(solution)/shard_map/ppermute | solution.py:27

commit v4 on v3

--- a/solution.py
+++ b/solution.py
@@ -57,14 +57,19 @@
     across2 = across_y(join(upper(front2), lower(back2)))
 
     back3, front3, across1 = together(back3, front3, across1)
-    back4 = along_z(join(upper(back3), upper(across1)), 1)
-    front4 = along_z(join(lower(front3), lower(across1)), -1)
-    across3 = across_y(join(upper(back3), lower(front3)))
+    to_front, to_back = together(
+        join(upper(back3), upper(across1)), join(lower(front3), lower(across1))
+    )
+    back4, front4 = along_z(to_front, 1), along_z(to_back, -1)
+    across3 = across_y(join(upper(to_front), upper(to_back)))
 
-    back4, front4, across2 = together(back4, front4, across2)
-    back5 = along_z(join(lower(across0), lower(across2)), 1)
-    front5 = along_z(join(upper(across0), upper(across2)), -1)
-    across4 = across_y(join(upper(back4), upper(front4)))
+    to_front, to_back = together(
+        join(lower(across0), lower(across2)), join(upper(across0), upper(across2))
+    )
+    back4, front4, to_front, to_back = together(back4, front4, to_front, to_back)
+    back5, front5 = along_z(to_front, 1), along_z(to_back, -1)
+    to_across, _, _ = together(join(upper(back4), upper(front4)), to_front, to_back)
+    across4 = across_y(to_across)
 
     yield [own, back1, front1, across0], whole(0, 0) + whole(0, -1) + whole(0, 1) + whole(1, 0)
     yield [back2, front2, across1], whole(0, -2) + whole(0, 2) + [(1, -1, 0), (1, 1, 1)]
@@ -98,15 +103,17 @@
     core = layer % CORES
     own_z, own_y = query // Y_HI, query % Y_HI
 
-    arrived, products = [], []
-    for blocks, names in gather_steps(scaled_flat):
-        arrived += names
-        rows = jnp.concatenate(blocks, axis=0)
-        products.append(
-            lax.dot_general(
-                rows, query_flat, (((1,), (1,)), ((), ())), preferred_element_type=jnp.float32
-            ).astype(jnp.bfloat16)
-        )
+    def times_queries(blocks):
+        return lax.dot_general(
+            jnp.concatenate(blocks, axis=0),
+            query_flat,
+            (((1,), (1,)), ((), ())),
+            preferred_element_type=jnp.float32,
+        ).astype(jnp.bfloat16)
+
+    *steps, (last_blocks, last_names) = gather_steps(scaled_flat)
+    arrived = [name for _, names in steps for name in names] + last_names
+    products = [times_queries(blocks) for blocks, _ in steps]
 
     half_rows = train_rows // 2
     half_of = train_order // half_rows
@@ -119,7 +126,7 @@
     place = place * half_rows + train_order % half_rows
     place = place.reshape(Y_LO * X, CORES, train_rows)
 
-    early = jnp.concatenate(products[:-1], axis=0)
+    early = jnp.concatenate(products, axis=0)
     early_rows = early.shape[0]
 
     def pick(rows, first, count):
@@ -130,17 +137,22 @@
             chosen, values, (((1,), (0,)), ((), ())), preferred_element_type=jnp.float32
         )
 
-    def ordered(for_core):
-        rows = lax.dynamic_index_in_dim(place, for_core, 1, keepdims=False).reshape(-1)
-        before = times(pick(rows, 0, early_rows), early).astype(jnp.bfloat16)
-        late = pick(rows, early_rows, products[-1].shape[0])
-        return before, late
+    def rows_of(for_core):
+        return lax.dynamic_index_in_dim(place, for_core, 1, keepdims=False).reshape(-1)
 
-    other_before, other_late = ordered(1 - core)
-    own_before, own_late = ordered(core)
-    other_half = (other_before + times(other_late, products[-1])).astype(jnp.bfloat16)
+    own_rows, other_rows = rows_of(core), rows_of(1 - core)
+    own_before = times(pick(own_rows, 0, early_rows), early).astype(jnp.bfloat16)
+    other_before = times(pick(other_rows, 0, early_rows), early).astype(jnp.bfloat16)
+    *last_blocks, own_before, other_before = together(*last_blocks, own_before, other_before)
+    late = times_queries(last_blocks)
+
+    def with_late(before, rows):
+        chosen = pick(rows, early_rows, late.shape[0])
+        return (before + times(chosen, late)).astype(jnp.bfloat16)
+
+    other_half = with_late(other_before, other_rows)
     received = across_cores(other_half)
-    own_half = (own_before + times(own_late, products[-1])).astype(jnp.bfloat16)
+    own_half = with_late(own_before, own_rows)
     own_half, received = together(own_half, received)
     chip_sum = own_half.astype(jnp.float32) + received.astype(jnp.float32)
     chip_sum = (chip_sum * factor).astype(jnp.bfloat16)

time: 111 us -> 108 us (0.973)
  waiting for transfers between devices: 26 us -> 20.8 us
  starting transfers between devices: 35 us -> 38.4 us
  blocking collectives: 20.5 us -> 19.2 us
  matrix products: 23.9 us -> 22.6 us
    ppermute x10, waiting for transfers between devices: 25.7 us -> 17.4 us  [along_z(): return lax.ppermute(block, 'query', pairs)]
    ppermute x5, starting transfers between devices: 12.2 us -> 14.5 us  [across_y(): return lax.ppermute(block, 'query', pairs)]
    another operation x1 -> x0, local copies, waits for them, and re-layouts: 2.08 us -> none
    reshape x0 -> x1, local copies, waits for them, and re-layouts: none -> 2.08 us
    ppermute x5, waiting for transfers between devices: 0.37 us -> 2 us  [across_y(): return lax.ppermute(block, 'query', pairs)]
    ppermute x1, waiting for transfers between devices: 0.01 us -> 1.39 us  [across_cores(): return lax.ppermute(block, 'layer', pairs)]
    all_to_all x1, blocking collectives: 20.5 us -> 19.2 us  [per_device(): lax.all_to_all(chip_sum.reshape(Y_LO * X, train_rows, query_rows), 'layer...]
    ppermute x10, starting transfers between devices: 16.4 us -> 17.6 us  [along_z(): return lax.ppermute(block, 'query', pairs)]
  transfers between devices with their start and end apart: 16 -> 16, of which waited for: 7 -> 5; matrix products, arithmetic and copies ran while one was open for 18% -> 18% of each run, Pallas kernels for 0% -> 0%
where the time goes in v4:
time: 108 us; the launch traced here: 107 us
  starting transfers between devices  38.4 us (36%)
  matrix products  22.6 us (21%)
  waiting for transfers between devices  20.8 us (19%)
  blocking collectives  19.2 us (18%)
  local copies, waits for them, and re-layouts  3.36 us (3%)
  other arithmetic  2.53 us (2%)
    all_to_all x1, blocking collectives, per_device(): lax.all_to_all(chip_sum.reshape(Y_LO * X, train_rows, query_rows), 'layer...  19.2 us
    ppermute x10, starting transfers between devices, along_z(): return lax.ppermute(block, 'query', pairs)  17.6 us
    ppermute x10, waiting for transfers between devices, along_z(): return lax.ppermute(block, 'query', pairs)  17.4 us
    dot_general x5, matrix products, times_queries(): lax.dot_general(jnp.concatenate(blocks, axis=0), query_flat, (((1,), (1,)...  17.3 us
    ppermute x5, starting transfers between devices, across_y(): return lax.ppermute(block, 'query', pairs)  14.5 us
    ppermute x1, starting transfers between devices, across_cores(): return lax.ppermute(block, 'layer', pairs)  6.39 us
    dot_general x4, matrix products, times(): lax.dot_general(chosen, values, (((1,), (0,)), ((), ())), preferred_eleme...  3.56 us
  transfers between devices with their start and end apart: 16, of which 5 were waited for; matrix products, arithmetic and copies ran while one was open for 18% of the time, Pallas kernels for 0%

profile of v4, /device:TPU:1, one launch (start us, length us, event | category | flops | bytes accessed | tf_op | source)
XLA Modules:
  0.0 107.3 jit_solution(3648517863544153295)
XLA Ops:
  0.0 2.1 %reshape.50 = bf16[64,64,64]{2,1,0:T(8,128)(2,1)S(1)} reshape(bf16[64,1,4096]{2,0,1:T(8,128)(2,1)} %param.7) | data formatting | bytes 1048576 | tf_op jit(solution)/shard_map/reshape
  2.1 0.8 fusion.78
  2.9 1.0 fusion.76
  3.9 0.7 transpose.12
  4.5 0.0 copy-done.2
  4.6 0.1 divide_convert_fusion
  4.7 6.5 %collective-permute-start.1 = (bf16[64,4096]{1,0:T(8,128)(2,1)S(1)}, bf16[64,4096]{1,0:T(8,128)(2,1)S(1)}, u32[]{:S(2)}, u32[]{:S(2)}) collective-permute-start(bf16[64,4096]{1,0:T(8,128)(2,1)S(1)} %divide_convert_fusion), channel_id=1, source_target_pairs={{0,14},{1,15},{2,0},{3,1},{4,2},{5,3},{6,4},{7,5},{8,6},{9,7},{10,... | collective-permute-start | bytes 1572872 | tf_op jit(solution)/shard_map/ppermute | solution.py:17
  11.2 2.9 %collective-permute-start.4 = (bf16[64,4096]{1,0:T(8,128)(2,1)S(1)}, bf16[64,4096]{1,0:T(8,128)(2,1)S(1)}, u32[]{:S(2)}, u32[]{:S(2)}) collective-permute-start(bf16[64,4096]{1,0:T(8,128)(2,1)S(1)} %divide_convert_fusion), channel_id=1, source_target_pairs={{0,1},{1,0},{2,3},{3,2},{4,5},{5,4},{6,7},{7,6},{8,9},{9,8},{10,11... | collective-permute-start | bytes 1572872 | tf_op jit(solution)/shard_map/ppermute | solution.py:22
  14.1 0.1 fusion.87
  14.1 0.1 reshape.53
  14.2 0.1 eq.261
  14.3 0.1 eq.257
  14.4 7.3 %collective-permute-done.1 = bf16[64,4096]{1,0:T(8,128)(2,1)S(1)} collective-permute-done((bf16[64,4096]{1,0:T(8,128)(2,1)S(1)}, bf16[64,4096]{1,0:T(8,128)(2,1)S(1)}, u32[]{:S(2)}, u32[]{:S(2)}) %collective-permute-start.1) | collective-permute-done | bytes 524320 | tf_op jit(solution)/shard_map/ppermute | solution.py:17
  21.7 3.1 %collective-permute-done = bf16[64,4096]{1,0:T(8,128)(2,1)S(1)} collective-permute-done((bf16[64,4096]{1,0:T(8,128)(2,1)S(1)}, bf16[64,4096]{1,0:T(8,128)(2,1)S(1)}, u32[]{:S(2)}, u32[]{:S(2)}) %collective-permute-start) | collective-permute-done | bytes 524320 | tf_op jit(solution)/shard_map/ppermute | solution.py:17
  24.8 2.7 %collective-permute-start.3 = (bf16[64,4096]{1,0:T(8,128)(2,1)S(1)}, bf16[64,4096]{1,0:T(8,128)(2,1)S(1)}, u32[]{:S(2)}, u32[]{:S(2)}) collective-permute-start(bf16[64,4096]{1,0:T(8,128)(2,1)S(1)} %collective-permute-done.1), channel_id=1, source_target_pairs={{0,14},{1,15},{2,0},{3,1},{4,2},{5,3},{6,4},{7,5},{8,6},{9,7},{10,... | collective-permute-start | bytes 1572872 | tf_op jit(solution)/shard_map/ppermute | solution.py:17
  27.6 3.0 %collective-permute-start.7 = (bf16[64,4096]{1,0:T(8,128)(2,1)S(1)}, bf16[64,4096]{1,0:T(8,128)(2,1)S(1)}, u32[]{:S(2)}, u32[]{:S(2)}) collective-permute-start(bf16[64,4096]{1,0:T(8,128)(2,1)S(1)} %pad_maximum_fusion.1), channel_id=1, source_target_pairs={{0,1},{1,0},{2,3},{3,2},{4,5},{5,4},{6,7},{7,6},{8,9},{9,8},{10,11... | collective-permute-start | bytes 1572872 | tf_op jit(solution)/shard_map/ppermute | solution.py:22
  30.6 7.0 %collective-permute-done.2 = bf16[64,4096]{1,0:T(8,128)(2,1)S(1)} collective-permute-done((bf16[64,4096]{1,0:T(8,128)(2,1)S(1)}, bf16[64,4096]{1,0:T(8,128)(2,1)S(1)}, u32[]{:S(2)}, u32[]{:S(2)}) %collective-permute-start.2) | collective-permute-done | bytes 524320 | tf_op jit(solution)/shard_map/ppermute | solution.py:17
  37.6 0.1 collective-permute-start.5
  37.7 2.7 %collective-permute-start.6 = (bf16[64,4096]{1,0:T(8,128)(2,1)S(1)}, bf16[64,4096]{1,0:T(8,128)(2,1)S(1)}, u32[]{:S(2)}, u32[]{:S(2)}) collective-permute-start(bf16[64,4096]{1,0:T(8,128)(2,1)S(1)} %collective-permute-done.3), channel_id=1, source_target_pairs={{0,14},{1,15},{2,0},{3,1},{4,2},{5,3},{6,4},{7,5},{8,6},{9,7},{10,... | collective-permute-start | bytes 1572872 | tf_op jit(solution)/shard_map/ppermute | solution.py:17
  40.5 0.0 slice-start
  40.6 0.0 slice-start.1
  40.6 3.2 %collective-permute-start.10 = (bf16[64,4096]{1,0:T(8,128)(2,1)S(1)}, bf16[64,4096]{1,0:T(8,128)(2,1)S(1)}, u32[]{:S(2)}, u32[]{:S(2)}) collective-permute-start(bf16[64,4096]{1,0:T(8,128)(2,1)S(1)} %pad_maximum_fusion.4), channel_id=1, source_target_pairs={{0,1},{1,0},{2,3},{3,2},{4,5},{5,4},{6,7},{7,6},{8,9},{9,8},{10,11... | collective-permute-start | bytes 1572872 | tf_op jit(solution)/shard_map/ppermute | solution.py:22
  43.8 5.7 %fusion.41 = bf16[256,1024]{1,0:T(8,128)(2,1)S(1)} fusion(bf16[1024,1,4096]{2,0,1:T(8,128)(2,1)} %param.6, bf16[64,4096]{1,0:T(8,128)(2,1)S(1)} %collective-permute-done.4, bf16[64,4096]{1,0:T(8,128)(2,1)S(1)} %collective-permute-done.1, bf16[64,4096]{1,0:T(8,128)(2,1)S(1)} %collective-permute-done, bf16[64,4096]{1,0:T(8,128)(2,1)S(1)} %divide_convert_fusion), kind=kOutput, calls=%fused_computation.48 | convolution fusion | flops 2156134400 | bytes 11010048 | tf_op jit(solution)/shard_map/dot_general | solution.py:107
  49.5 0.0 collective-permute-done.5
  49.6 0.1 pad_maximum_fusion.2
  49.8 0.1 collective-permute-start.8
  49.9 2.7 %collective-permute-start.9 = (bf16[64,4096]{1,0:T(8,128)(2,1)S(1)}, bf16[64,4096]{1,0:T(8,128)(2,1)S(1)}, u32[]{:S(2)}, u32[]{:S(2)}) collective-permute-start(bf16[64,4096]{1,0:T(8,128)(2,1)S(1)} %get-tuple-element.37), channel_id=1, source_target_pairs={{0,14},{1,15},{2,0},{3,1},{4,2},{5,3},{6,4},{7,5},{8,6},{9,7},{10,... | collective-permute-start | bytes 1572872 | tf_op jit(solution)/shard_map/ppermute | solution.py:17
  52.7 3.0 %collective-permute-start.14 = (bf16[64,4096]{1,0:T(8,128)(2,1)S(1)}, bf16[64,4096]{1,0:T(8,128)(2,1)S(1)}, u32[]{:S(2)}, u32[]{:S(2)}) collective-permute-start(bf16[64,4096]{1,0:T(8,128)(2,1)S(1)} %pad_maximum_fusion.8), channel_id=1, source_target_pairs={{0,1},{1,0},{2,3},{3,2},{4,5},{5,4},{6,7},{7,6},{8,9},{9,8},{10,11... | collective-permute-start | bytes 1572872 | tf_op jit(solution)/shard_map/ppermute | solution.py:22
  55.7 2.9 %fusion.46 = bf16[192,1024]{1,0:T(8,128)(2,1)S(1)} fusion(bf16[1024,1,4096]{2,0,1:T(8,128)(2,1)S(1)} %bitcast.40, bf16[64,4096]{1,0:T(8,128)(2,1)S(1)} %collective-permute-done.7, bf16[64,4096]{1,0:T(8,128)(2,1)S(1)} %collective-permute-done.3, bf16[64,4096]{1,0:T(8,128)(2,1)S(1)} %collective-permute-done.2), kind=kOutput, calls=%fused_computation.49 | convolution fusion | flops 1615527936 | bytes 10354688 | tf_op jit(solution)/shard_map/dot_general | solution.py:107
  58.6 2.9 %fusion.51 = bf16[192,1024]{1,0:T(8,128)(2,1)S(1)} fusion(bf16[1024,1,4096]{2,0,1:T(8,128)(2,1)S(1)} %bitcast.40, bf16[64,4096]{1,0:T(8,128)(2,1)S(1)} %collective-permute-done.10, bf16[64,4096]{1,0:T(8,128)(2,1)S(1)} %collective-permute-done.6, bf16[64,4096]{1,0:T(8,128)(2,1)S(1)} %collective-permute-done.5), kind=kOutput, calls=%fused_computation.50 | convolution fusion | flops 1615527936 | bytes 10354688 | tf_op jit(solution)/shard_map/dot_general | solution.py:107
  61.5 0.1 pad_maximum_fusion.5
  61.7 0.1 collective-permute-start.11
  61.8 2.7 %collective-permute-start.12 = (bf16[64,4096]{1,0:T(8,128)(2,1)S(1)}, bf16[64,4096]{1,0:T(8,128)(2,1)S(1)}, u32[]{:S(2)}, u32[]{:S(2)}) collective-permute-start(bf16[64,4096]{1,0:T(8,128)(2,1)S(1)} %get-tuple-element.42), channel_id=1, source_target_pairs={{0,14},{1,15},{2,0},{3,1},{4,2},{5,3},{6,4},{7,5},{8,6},{9,7},{10,... | collective-permute-start | bytes 1572872 | tf_op jit(solution)/shard_map/ppermute | solution.py:17
  64.5 2.4 %collective-permute-start.13 = (bf16[64,4096]{1,0:T(8,128)(2,1)S(1)}, bf16[64,4096]{1,0:T(8,128)(2,1)S(1)}, u32[]{:S(2)}, u32[]{:S(2)}) collective-permute-start(bf16[64,4096]{1,0:T(8,128)(2,1)S(1)} %pad_maximum_fusion.7), channel_id=1, source_target_pairs={{0,1},{1,0},{2,3},{3,2},{4,5},{5,4},{6,7},{7,6},{8,9},{9,8},{10,11... | collective-permute-start | bytes 1572872 | tf_op jit(solution)/shard_map/ppermute | solution.py:22
  66.8 2.9 %fusion.56 = bf16[192,1024]{1,0:T(8,128)(2,1)S(1)} fusion(bf16[1024,1,4096]{2,0,1:T(8,128)(2,1)S(1)} %bitcast.40, bf16[64,4096]{1,0:T(8,128)(2,1)S(1)} %collective-permute-done.14, bf16[64,4096]{1,0:T(8,128)(2,1)S(1)} %collective-permute-done.9, bf16[64,4096]{1,0:T(8,128)(2,1)S(1)} %collective-permute-done.8), kind=kOutput, calls=%fused_computation.51 | convolution fusion | flops 1615527936 | bytes 10354688 | tf_op jit(solution)/shard_map/dot_general | solution.py:107
  69.7 1.3 %fusion.39 = bf16[512,1024]{1,0:T(8,128)(2,1)S(1)} fusion(s32[512]{0:T(512)S(1)} %eq.261, bf16[192,1024]{1,0:T(8,128)(2,1)S(1)} %fusion.56, bf16[192,1024]{1,0:T(8,128)(2,1)S(1)} %fusion.51, bf16[192,1024]{1,0:T(8,128)(2,1)S(1)} %fusion.46, bf16[256,1024]{1,0:T(8,128)(2,1)S(1)} %fusion.41), kind=kOutput, calls=%fused_computation.46 | convolution fusion | flops 880181248 | bytes 2754560 | tf_op jit(solution)/shard_map/dot_general | solution.py:136
  71.0 1.3 %fusion.40 = bf16[512,1024]{1,0:T(8,128)(2,1)S(1)} fusion(s32[512]{0:T(512)S(1)} %eq.257, bf16[192,1024]{1,0:T(8,128)(2,1)S(1)} %fusion.56, bf16[192,1024]{1,0:T(8,128)(2,1)S(1)} %fusion.51, bf16[192,1024]{1,0:T(8,128)(2,1)S(1)} %fusion.46, bf16[256,1024]{1,0:T(8,128)(2,1)S(1)} %fusion.41), kind=kOutput, calls=%fused_computation.47 | convolution fusion | flops 880181248 | bytes 2754560 | tf_op jit(solution)/shard_map/dot_general | solution.py:136
  72.3 2.0 %collective-permute-done.13 = bf16[64,4096]{1,0:T(8,128)(2,1)S(1)} collective-permute-done((bf16[64,4096]{1,0:T(8,128)(2,1)S(1)}, bf16[64,4096]{1,0:T(8,128)(2,1)S(1)}, u32[]{:S(2)}, u32[]{:S(2)}) %collective-permute-start.13) | collective-permute-done | bytes 524320 | tf_op jit(solution)/shard_map/ppermute | solution.py:22
  74.3 2.9 %fusion.61 = bf16[192,1024]{1,0:T(8,128)(2,1)S(1)} fusion(bf16[1024,1,4096]{2,0,1:T(8,128)(2,1)S(1)} %bitcast.40, bf16[64,4096]{1,0:T(8,128)(2,1)S(1)} %collective-permute-done.13, bf16[64,4096]{1,0:T(8,128)(2,1)S(1)} %collective-permute-done.12, bf16[64,4096]{1,0:T(8,128)(2,1)S(1)} %collective-permute-done.11), kind=kOutput, calls=%fused_computation.52 | convolution fusion | flops 1615527936 | bytes 10354688 | tf_op jit(solution)/shard_map/dot_general | solution.py:107
  77.2 0.5 fusion.68
  77.7 0.4 add_convert_fusion
  78.1 6.4 %collective-permute-start.15 = (bf16[512,1024]{1,0:T(8,128)(2,1)S(1)}, bf16[512,1024]{1,0:T(8,128)(2,1)S(1)}, u32[]{:S(2)}, u32[]{:S(2)}) collective-permute-start(bf16[512,1024]{1,0:T(8,128)(2,1)S(1)} %add_convert_fusion), channel_id=1, source_target_pairs={{0,16},{16,0},{32,48},{48,32},{64,80},{80,64},{96,112},{112,96},{1... | collective-permute-start | bytes 3145736 | tf_op jit(solution)/shard_map/ppermute | solution.py:27
  84.5 0.5 fusion.70
  85.0 0.4 add_convert_fusion.1
  85.4 1.4 %collective-permute-done.15 = bf16[512,1024]{1,0:T(8,128)(2,1)S(1)} collective-permute-done((bf16[512,1024]{1,0:T(8,128)(2,1)S(1)}, bf16[512,1024]{1,0:T(8,128)(2,1)S(1)}, u32[]{:S(2)}, u32[]{:S(2)}) %collective-permute-start.15) | collective-permute-done | bytes 1048608 | tf_op jit(solution)/shard_map/ppermute | solution.py:27
  86.8 0.4 multiply_convert_fusion
  87.2 19.2 %all_to_all.5 = bf16[8,64,1024]{2,1,0:T(8,128)(2,1)S(1)} all-to-all(bf16[8,64,1024]{2,1,0:T(8,128)(2,1)S(1)} %bitcast.37), channel_id=1, replica_groups={{0,32,64,96,128,160,192,224},{16,48,80,112,144,176,208,240},{1,33,65,97..., dimensions={0} | all-to-all | bytes 2097152 | tf_op jit(solution)/shard_map/all_to_all | solution.py:160
  106.4 0.9 convert_reduce_fusion
  (41 shorter events, 0.5 us)
Async XLA Ops:
  0.0 2.1 %copy-start = (f32[1,64,64]{2,1,0:T(8,128)S(1)}, f32[1,64,64]{2,1,0:T(8,128)}, u32[]{:S(2)}) copy-start(f32[1,64,64]{2,1,0:T(8,128)} %param.8) | copy-start | bytes 49156
  0.0 2.9 %copy-start.1 = (f32[1,64,64]{2,1,0:T(8,128)S(1)}, f32[1,64,64]{2,1,0:T(8,128)}, u32[]{:S(2)}) copy-start(f32[1,64,64]{2,1,0:T(8,128)} %param.9) | copy-start | bytes 49156
  3.9 0.7 copy-start.2
  3.9 10.2 %copy-start.3 = (s32[1024]{0:T(1024)S(1)}, s32[1024]{0:T(1024)}, u32[]{:S(2)}) copy-start(s32[1024]{0:T(1024)} %param.11) | copy-start | bytes 12292
  4.7 17.1 %collective-permute-start.1 = (bf16[64,4096]{1,0:T(8,128)(2,1)S(1)}, bf16[64,4096]{1,0:T(8,128)(2,1)S(1)}, u32[]{:S(2)}, u32[]{:S(2)}) collective-permute-start(bf16[64,4096]{1,0:T(8,128)(2,1)S(1)} %divide_convert_fusion), channel_id=1, source_target_pairs={{0,14},{1,15},{2,0},{3,1},{4,2},{5,3},{6,4},{7,5},{8,6},{9,7},{10,... | collective-permute-start | bytes 1572872 | tf_op jit(solution)/shard_map/ppermute | solution.py:17
  11.2 13.7 %collective-permute-start = (bf16[64,4096]{1,0:T(8,128)(2,1)S(1)}, bf16[64,4096]{1,0:T(8,128)(2,1)S(1)}, u32[]{:S(2)}, u32[]{:S(2)}) collective-permute-start(bf16[64,4096]{1,0:T(8,128)(2,1)S(1)} %divide_convert_fusion), channel_id=1, source_target_pairs={{0,2},{1,3},{2,4},{3,5},{4,6},{5,7},{6,8},{7,9},{8,10},{9,11},{10,... | collective-permute-start | bytes 1572872 | tf_op jit(solution)/shard_map/ppermute | solution.py:17
  11.2 19.5 %collective-permute-start.4 = (bf16[64,4096]{1,0:T(8,128)(2,1)S(1)}, bf16[64,4096]{1,0:T(8,128)(2,1)S(1)}, u32[]{:S(2)}, u32[]{:S(2)}) collective-permute-start(bf16[64,4096]{1,0:T(8,128)(2,1)S(1)} %divide_convert_fusion), channel_id=1, source_target_pairs={{0,1},{1,0},{2,3},{3,2},{4,5},{5,4},{6,7},{7,6},{8,9},{9,8},{10,11... | collective-permute-start | bytes 1572872 | tf_op jit(solution)/shard_map/ppermute | solution.py:22
  24.8 12.8 %collective-permute-start.2 = (bf16[64,4096]{1,0:T(8,128)(2,1)S(1)}, bf16[64,4096]{1,0:T(8,128)(2,1)S(1)}, u32[]{:S(2)}, u32[]{:S(2)}) collective-permute-start(bf16[64,4096]{1,0:T(8,128)(2,1)S(1)} %collective-permute-done), channel_id=1, source_target_pairs={{0,2},{1,3},{2,4},{3,5},{4,6},{5,7},{6,8},{7,9},{8,10},{9,11},{10,... | collective-permute-start | bytes 1572872 | tf_op jit(solution)/shard_map/ppermute | solution.py:17
  24.8 12.8 %collective-permute-start.3 = (bf16[64,4096]{1,0:T(8,128)(2,1)S(1)}, bf16[64,4096]{1,0:T(8,128)(2,1)S(1)}, u32[]{:S(2)}, u32[]{:S(2)}) collective-permute-start(bf16[64,4096]{1,0:T(8,128)(2,1)S(1)} %collective-permute-done.1), channel_id=1, source_target_pairs={{0,14},{1,15},{2,0},{3,1},{4,2},{5,3},{6,4},{7,5},{8,6},{9,7},{10,... | collective-permute-start | bytes 1572872 | tf_op jit(solution)/shard_map/ppermute | solution.py:17
  27.6 21.9 %collective-permute-start.7 = (bf16[64,4096]{1,0:T(8,128)(2,1)S(1)}, bf16[64,4096]{1,0:T(8,128)(2,1)S(1)}, u32[]{:S(2)}, u32[]{:S(2)}) collective-permute-start(bf16[64,4096]{1,0:T(8,128)(2,1)S(1)} %pad_maximum_fusion.1), channel_id=1, source_target_pairs={{0,1},{1,0},{2,3},{3,2},{4,5},{5,4},{6,7},{7,6},{8,9},{9,8},{10,11... | collective-permute-start | bytes 1572872 | tf_op jit(solution)/shard_map/ppermute | solution.py:22
  37.6 11.9 %collective-permute-start.5 = (bf16[64,4096]{1,0:T(8,128)(2,1)S(1)}, bf16[64,4096]{1,0:T(8,128)(2,1)S(1)}, u32[]{:S(2)}, u32[]{:S(2)}) collective-permute-start(bf16[64,4096]{1,0:T(8,128)(2,1)S(1)} %collective-permute-done.2), channel_id=1, source_target_pairs={{0,2},{1,3},{2,4},{3,5},{4,6},{5,7},{6,8},{7,9},{8,10},{9,11},{10,... | collective-permute-start | bytes 1572872 | tf_op jit(solution)/shard_map/ppermute | solution.py:17
  37.7 11.8 %collective-permute-start.6 = (bf16[64,4096]{1,0:T(8,128)(2,1)S(1)}, bf16[64,4096]{1,0:T(8,128)(2,1)S(1)}, u32[]{:S(2)}, u32[]{:S(2)}) collective-permute-start(bf16[64,4096]{1,0:T(8,128)(2,1)S(1)} %collective-permute-done.3), channel_id=1, source_target_pairs={{0,14},{1,15},{2,0},{3,1},{4,2},{5,3},{6,4},{7,5},{8,6},{9,7},{10,... | collective-permute-start | bytes 1572872 | tf_op jit(solution)/shard_map/ppermute | solution.py:17
  40.5 15.1 %slice-start = ((s8[8388608]{0:T(1024)(128)(4,1)}), s8[4194304]{0:T(1024)(128)(4,1)S(1)}, s32[]{:S(2)}) async-start(s8[8388608]{0:T(1024)(128)(4,1)} %bitcast.39), calls=%async_computation.1 | async-start | bytes 8388608
  40.6 15.1 %slice-start.1 = ((s8[8388608]{0:T(1024)(128)(4,1)}), s8[4194304]{0:T(1024)(128)(4,1)S(1)}, s32[]{:S(2)}) async-start(s8[8388608]{0:T(1024)(128)(4,1)} %bitcast.39), calls=%async_computation.2 | async-start | bytes 8388608
  40.6 18.0 %collective-permute-start.10 = (bf16[64,4096]{1,0:T(8,128)(2,1)S(1)}, bf16[64,4096]{1,0:T(8,128)(2,1)S(1)}, u32[]{:S(2)}, u32[]{:S(2)}) collective-permute-start(bf16[64,4096]{1,0:T(8,128)(2,1)S(1)} %pad_maximum_fusion.4), channel_id=1, source_target_pairs={{0,1},{1,0},{2,3},{3,2},{4,5},{5,4},{6,7},{7,6},{8,9},{9,8},{10,11... | collective-permute-start | bytes 1572872 | tf_op jit(solution)/shard_map/ppermute | solution.py:22
  49.8 11.8 %collective-permute-start.8 = (bf16[64,4096]{1,0:T(8,128)(2,1)S(1)}, bf16[64,4096]{1,0:T(8,128)(2,1)S(1)}, u32[]{:S(2)}, u32[]{:S(2)}) collective-permute-start(bf16[64,4096]{1,0:T(8,128)(2,1)S(1)} %get-tuple-element.36), channel_id=1, source_target_pairs={{0,2},{1,3},{2,4},{3,5},{4,6},{5,7},{6,8},{7,9},{8,10},{9,11},{10,... | collective-permute-start | bytes 1572872 | tf_op jit(solution)/shard_map/ppermute | solution.py:17
  49.9 11.7 %collective-permute-start.9 = (bf16[64,4096]{1,0:T(8,128)(2,1)S(1)}, bf16[64,4096]{1,0:T(8,128)(2,1)S(1)}, u32[]{:S(2)}, u32[]{:S(2)}) collective-permute-start(bf16[64,4096]{1,0:T(8,128)(2,1)S(1)} %get-tuple-element.37), channel_id=1, source_target_pairs={{0,14},{1,15},{2,0},{3,1},{4,2},{5,3},{6,4},{7,5},{8,6},{9,7},{10,... | collective-permute-start | bytes 1572872 | tf_op jit(solution)/shard_map/ppermute | solution.py:17
  52.7 14.2 %collective-permute-start.14 = (bf16[64,4096]{1,0:T(8,128)(2,1)S(1)}, bf16[64,4096]{1,0:T(8,128)(2,1)S(1)}, u32[]{:S(2)}, u32[]{:S(2)}) collective-permute-start(bf16[64,4096]{1,0:T(8,128)(2,1)S(1)} %pad_maximum_fusion.8), channel_id=1, source_target_pairs={{0,1},{1,0},{2,3},{3,2},{4,5},{5,4},{6,7},{7,6},{8,9},{9,8},{10,11... | collective-permute-start | bytes 1572872 | tf_op jit(solution)/shard_map/ppermute | solution.py:22
  61.7 12.6 %collective-permute-start.11 = (bf16[64,4096]{1,0:T(8,128)(2,1)S(1)}, bf16[64,4096]{1,0:T(8,128)(2,1)S(1)}, u32[]{:S(2)}, u32[]{:S(2)}) collective-permute-start(bf16[64,4096]{1,0:T(8,128)(2,1)S(1)} %get-tuple-element.41), channel_id=1, source_target_pairs={{0,2},{1,3},{2,4},{3,5},{4,6},{5,7},{6,8},{7,9},{8,10},{9,11},{10,... | collective-permute-start | bytes 1572872 | tf_op jit(solution)/shard_map/ppermute | solution.py:17
  61.8 12.6 %collective-permute-start.12 = (bf16[64,4096]{1,0:T(8,128)(2,1)S(1)}, bf16[64,4096]{1,0:T(8,128)(2,1)S(1)}, u32[]{:S(2)}, u32[]{:S(2)}) collective-permute-start(bf16[64,4096]{1,0:T(8,128)(2,1)S(1)} %get-tuple-element.42), channel_id=1, source_target_pairs={{0,14},{1,15},{2,0},{3,1},{4,2},{5,3},{6,4},{7,5},{8,6},{9,7},{10,... | collective-permute-start | bytes 1572872 | tf_op jit(solution)/shard_map/ppermute | solution.py:17
  64.5 9.8 %collective-permute-start.13 = (bf16[64,4096]{1,0:T(8,128)(2,1)S(1)}, bf16[64,4096]{1,0:T(8,128)(2,1)S(1)}, u32[]{:S(2)}, u32[]{:S(2)}) collective-permute-start(bf16[64,4096]{1,0:T(8,128)(2,1)S(1)} %pad_maximum_fusion.7), channel_id=1, source_target_pairs={{0,1},{1,0},{2,3},{3,2},{4,5},{5,4},{6,7},{7,6},{8,9},{9,8},{10,11... | collective-permute-start | bytes 1572872 | tf_op jit(solution)/shard_map/ppermute | solution.py:22
  78.1 8.7 %collective-permute-start.15 = (bf16[512,1024]{1,0:T(8,128)(2,1)S(1)}, bf16[512,1024]{1,0:T(8,128)(2,1)S(1)}, u32[]{:S(2)}, u32[]{:S(2)}) collective-permute-start(bf16[512,1024]{1,0:T(8,128)(2,1)S(1)} %add_convert_fusion), channel_id=1, source_target_pairs={{0,16},{16,0},{32,48},{48,32},{64,80},{80,64},{96,112},{112,96},{1... | collective-permute-start | bytes 3145736 | tf_op jit(solution)/shard_map/ppermute | solution.py:27

commit v5 on v4

--- a/solution.py
+++ b/solution.py
@@ -143,19 +143,15 @@
     own_rows, other_rows = rows_of(core), rows_of(1 - core)
     own_before = times(pick(own_rows, 0, early_rows), early).astype(jnp.bfloat16)
     other_before = times(pick(other_rows, 0, early_rows), early).astype(jnp.bfloat16)
-    *last_blocks, own_before, other_before = together(*last_blocks, own_before, other_before)
+    received = across_cores(other_before)
+    *last_blocks, own_before = together(*last_blocks, own_before)
     late = times_queries(last_blocks)
-
-    def with_late(before, rows):
-        chosen = pick(rows, early_rows, late.shape[0])
-        return (before + times(chosen, late)).astype(jnp.bfloat16)
-
-    other_half = with_late(other_before, other_rows)
-    received = across_cores(other_half)
-    own_half = with_late(own_before, own_rows)
-    own_half, received = together(own_half, received)
-    chip_sum = own_half.astype(jnp.float32) + received.astype(jnp.float32)
-    chip_sum = (chip_sum * factor).astype(jnp.bfloat16)
+    early_sum = own_before.astype(jnp.float32) + received.astype(jnp.float32)
+    early_sum = (early_sum * factor).astype(jnp.bfloat16)
+    late_sum = late.astype(jnp.float32) + across_cores(late).astype(jnp.float32)
+    late_sum = (late_sum * factor).astype(jnp.bfloat16)
+    chip_sum = early_sum + times(pick(own_rows, early_rows, late.shape[0]), late_sum)
+    chip_sum = chip_sum.astype(jnp.bfloat16)
     groups = [[chip * CORES + c for chip in range(Y_LO * X)] for c in range(CORES)]
     pieces = lax.all_to_all(
         chip_sum.reshape(Y_LO * X, train_rows, query_rows),

time: 108 us -> 106 us (0.981)
  waiting for transfers between devices: 20.8 us -> 18.8 us
  starting transfers between devices: 38.4 us -> 40.3 us
  other arithmetic: 2.53 us -> 1.34 us
    ppermute x1 -> x2, starting transfers between devices: 6.39 us -> 8.4 us  [across_cores(): return lax.ppermute(block, 'layer', pairs)]
    ppermute x5, waiting for transfers between devices: 2 us -> 0.01 us  [across_y(): return lax.ppermute(block, 'query', pairs)]
    convert_element_type x3 -> x0, other arithmetic: 1.21 us -> none  [the longest x2 0.8 us: with_late(): return (before + times(chosen, late)).astype(jnp.bfloat16)]
    dot_general x4 -> x3, matrix products: 3.56 us -> 3.19 us  [times(): lax.dot_general(chosen, values, (((1,), (0,)), ((), ())), preferred_eleme...]
  transfers between devices with their start and end apart: 16 -> 17, of which waited for: 5 -> 4; matrix products, arithmetic and copies ran while one was open for 18% -> 20% of each run, Pallas kernels for 0% -> 0%
where the time goes in v5:
time: 106 us
  starting transfers between devices  40.3 us (38%)
  matrix products  22.4 us (21%)
  blocking collectives  19 us (18%)
  waiting for transfers between devices  18.8 us (18%)
  local copies, waits for them, and re-layouts  3.36 us (3%)
  other arithmetic  1.34 us (1%)
    all_to_all x1, blocking collectives, per_device(): lax.all_to_all(chip_sum.reshape(Y_LO * X, train_rows, query_rows), 'layer...  19 us
    ppermute x10, starting transfers between devices, along_z(): return lax.ppermute(block, 'query', pairs)  17.6 us
    dot_general x5, matrix products, times_queries(): lax.dot_general(jnp.concatenate(blocks, axis=0), query_flat, (((1,), (1,)...  17.5 us
    ppermute x10, waiting for transfers between devices, along_z(): return lax.ppermute(block, 'query', pairs)  17.4 us
    ppermute x5, starting transfers between devices, across_y(): return lax.ppermute(block, 'query', pairs)  14.3 us
    ppermute x2, starting transfers between devices, across_cores(): return lax.ppermute(block, 'layer', pairs)  8.4 us
    dot_general x3, matrix products, times(): lax.dot_general(chosen, values, (((1,), (0,)), ((), ())), preferred_eleme...  3.19 us
  transfers between devices with their start and end apart: 17, of which 4 were waited for; matrix products, arithmetic and copies ran while one was open for 20% of the time, Pallas kernels for 0%

profile of v5, /device:TPU:1, one launch (start us, length us, event | category | flops | bytes accessed | tf_op | source)
XLA Modules:
  0.0 105.6 jit_solution(11706478761196903199)
XLA Ops:
  0.0 2.1 %reshape.50 = bf16[64,64,64]{2,1,0:T(8,128)(2,1)S(1)} reshape(bf16[64,1,4096]{2,0,1:T(8,128)(2,1)} %param.7) | data formatting | bytes 1048576 | tf_op jit(solution)/shard_map/reshape
  2.1 0.8 fusion.77
  2.9 1.0 fusion.75
  3.9 0.0 copy-start.2
  3.9 0.0 copy-start.3
  3.9 0.7 transpose.12
  4.5 0.0 copy-done.2
  4.6 0.1 divide_convert_fusion
  4.7 6.5 %collective-permute-start.1 = (bf16[64,4096]{1,0:T(8,128)(2,1)S(1)}, bf16[64,4096]{1,0:T(8,128)(2,1)S(1)}, u32[]{:S(2)}, u32[]{:S(2)}) collective-permute-start(bf16[64,4096]{1,0:T(8,128)(2,1)S(1)} %divide_convert_fusion), channel_id=1, source_target_pairs={{0,14},{1,15},{2,0},{3,1},{4,2},{5,3},{6,4},{7,5},{8,6},{9,7},{10,... | collective-permute-start | bytes 1572872 | tf_op jit(solution)/shard_map/ppermute | solution.py:17
  11.2 0.0 collective-permute-start
  11.2 2.9 %collective-permute-start.4 = (bf16[64,4096]{1,0:T(8,128)(2,1)S(1)}, bf16[64,4096]{1,0:T(8,128)(2,1)S(1)}, u32[]{:S(2)}, u32[]{:S(2)}) collective-permute-start(bf16[64,4096]{1,0:T(8,128)(2,1)S(1)} %divide_convert_fusion), channel_id=1, source_target_pairs={{0,1},{1,0},{2,3},{3,2},{4,5},{5,4},{6,7},{7,6},{8,9},{9,8},{10,11... | collective-permute-start | bytes 1572872 | tf_op jit(solution)/shard_map/ppermute | solution.py:22
  14.1 7.7 %collective-permute-done.1 = bf16[64,4096]{1,0:T(8,128)(2,1)S(1)} collective-permute-done((bf16[64,4096]{1,0:T(8,128)(2,1)S(1)}, bf16[64,4096]{1,0:T(8,128)(2,1)S(1)}, u32[]{:S(2)}, u32[]{:S(2)}) %collective-permute-start.1) | collective-permute-done | bytes 524320 | tf_op jit(solution)/shard_map/ppermute | solution.py:17
  21.7 3.1 %collective-permute-done = bf16[64,4096]{1,0:T(8,128)(2,1)S(1)} collective-permute-done((bf16[64,4096]{1,0:T(8,128)(2,1)S(1)}, bf16[64,4096]{1,0:T(8,128)(2,1)S(1)}, u32[]{:S(2)}, u32[]{:S(2)}) %collective-permute-start) | collective-permute-done | bytes 524320 | tf_op jit(solution)/shard_map/ppermute | solution.py:17
  24.8 2.7 %collective-permute-start.3 = (bf16[64,4096]{1,0:T(8,128)(2,1)S(1)}, bf16[64,4096]{1,0:T(8,128)(2,1)S(1)}, u32[]{:S(2)}, u32[]{:S(2)}) collective-permute-start(bf16[64,4096]{1,0:T(8,128)(2,1)S(1)} %collective-permute-done.1), channel_id=1, source_target_pairs={{0,14},{1,15},{2,0},{3,1},{4,2},{5,3},{6,4},{7,5},{8,6},{9,7},{10,... | collective-permute-start | bytes 1572872 | tf_op jit(solution)/shard_map/ppermute | solution.py:17
  27.5 0.1 fusion.86
  27.6 0.1 reshape.53
  27.7 0.1 eq.244
  27.8 0.1 eq.248
  28.0 3.0 %collective-permute-start.7 = (bf16[64,4096]{1,0:T(8,128)(2,1)S(1)}, bf16[64,4096]{1,0:T(8,128)(2,1)S(1)}, u32[]{:S(2)}, u32[]{:S(2)}) collective-permute-start(bf16[64,4096]{1,0:T(8,128)(2,1)S(1)} %pad_maximum_fusion.1), channel_id=1, source_target_pairs={{0,1},{1,0},{2,3},{3,2},{4,5},{5,4},{6,7},{7,6},{8,9},{9,8},{10,11... | collective-permute-start | bytes 1572872 | tf_op jit(solution)/shard_map/ppermute | solution.py:22
  31.0 6.6 %collective-permute-done.2 = bf16[64,4096]{1,0:T(8,128)(2,1)S(1)} collective-permute-done((bf16[64,4096]{1,0:T(8,128)(2,1)S(1)}, bf16[64,4096]{1,0:T(8,128)(2,1)S(1)}, u32[]{:S(2)}, u32[]{:S(2)}) %collective-permute-start.2) | collective-permute-done | bytes 524320 | tf_op jit(solution)/shard_map/ppermute | solution.py:17
  37.6 0.1 collective-permute-start.5
  37.7 2.7 %collective-permute-start.6 = (bf16[64,4096]{1,0:T(8,128)(2,1)S(1)}, bf16[64,4096]{1,0:T(8,128)(2,1)S(1)}, u32[]{:S(2)}, u32[]{:S(2)}) collective-permute-start(bf16[64,4096]{1,0:T(8,128)(2,1)S(1)} %collective-permute-done.3), channel_id=1, source_target_pairs={{0,14},{1,15},{2,0},{3,1},{4,2},{5,3},{6,4},{7,5},{8,6},{9,7},{10,... | collective-permute-start | bytes 1572872 | tf_op jit(solution)/shard_map/ppermute | solution.py:17
  40.5 0.0 slice-start
  40.6 0.0 slice-start.1
  40.6 3.2 %collective-permute-start.10 = (bf16[64,4096]{1,0:T(8,128)(2,1)S(1)}, bf16[64,4096]{1,0:T(8,128)(2,1)S(1)}, u32[]{:S(2)}, u32[]{:S(2)}) collective-permute-start(bf16[64,4096]{1,0:T(8,128)(2,1)S(1)} %pad_maximum_fusion.4), channel_id=1, source_target_pairs={{0,1},{1,0},{2,3},{3,2},{4,5},{5,4},{6,7},{7,6},{8,9},{9,8},{10,11... | collective-permute-start | bytes 1572872 | tf_op jit(solution)/shard_map/ppermute | solution.py:22
  43.8 5.7 %fusion.41 = bf16[256,1024]{1,0:T(8,128)(2,1)S(1)} fusion(bf16[1024,1,4096]{2,0,1:T(8,128)(2,1)} %param.6, bf16[64,4096]{1,0:T(8,128)(2,1)S(1)} %collective-permute-done.4, bf16[64,4096]{1,0:T(8,128)(2,1)S(1)} %collective-permute-done.1, bf16[64,4096]{1,0:T(8,128)(2,1)S(1)} %collective-permute-done, bf16[64,4096]{1,0:T(8,128)(2,1)S(1)} %divide_convert_fusion), kind=kOutput, calls=%fused_computation.47 | convolution fusion | flops 2156134400 | bytes 11010048 | tf_op jit(solution)/shard_map/dot_general | solution.py:107
  49.5 0.0 collective-permute-done.5
  49.5 0.0 collective-permute-done.6
  49.6 0.1 pad_maximum_fusion.2
  49.8 0.1 collective-permute-start.8
  49.9 2.7 %collective-permute-start.9 = (bf16[64,4096]{1,0:T(8,128)(2,1)S(1)}, bf16[64,4096]{1,0:T(8,128)(2,1)S(1)}, u32[]{:S(2)}, u32[]{:S(2)}) collective-permute-start(bf16[64,4096]{1,0:T(8,128)(2,1)S(1)} %get-tuple-element.34), channel_id=1, source_target_pairs={{0,14},{1,15},{2,0},{3,1},{4,2},{5,3},{6,4},{7,5},{8,6},{9,7},{10,... | collective-permute-start | bytes 1572872 | tf_op jit(solution)/shard_map/ppermute | solution.py:17
  52.7 3.0 %collective-permute-start.14 = (bf16[64,4096]{1,0:T(8,128)(2,1)S(1)}, bf16[64,4096]{1,0:T(8,128)(2,1)S(1)}, u32[]{:S(2)}, u32[]{:S(2)}) collective-permute-start(bf16[64,4096]{1,0:T(8,128)(2,1)S(1)} %pad_maximum_fusion.8), channel_id=1, source_target_pairs={{0,1},{1,0},{2,3},{3,2},{4,5},{5,4},{6,7},{7,6},{8,9},{9,8},{10,11... | collective-permute-start | bytes 1572872 | tf_op jit(solution)/shard_map/ppermute | solution.py:22
  55.7 3.0 %fusion.46 = bf16[192,1024]{1,0:T(8,128)(2,1)S(1)} fusion(bf16[1024,1,4096]{2,0,1:T(8,128)(2,1)S(1)} %bitcast.38, bf16[64,4096]{1,0:T(8,128)(2,1)S(1)} %collective-permute-done.7, bf16[64,4096]{1,0:T(8,128)(2,1)S(1)} %collective-permute-done.3, bf16[64,4096]{1,0:T(8,128)(2,1)S(1)} %collective-permute-done.2), kind=kOutput, calls=%fused_computation.48 | convolution fusion | flops 1615527936 | bytes 10354688 | tf_op jit(solution)/shard_map/dot_general | solution.py:107
  58.7 2.9 %fusion.51 = bf16[192,1024]{1,0:T(8,128)(2,1)S(1)} fusion(bf16[1024,1,4096]{2,0,1:T(8,128)(2,1)S(1)} %bitcast.38, bf16[64,4096]{1,0:T(8,128)(2,1)S(1)} %collective-permute-done.10, bf16[64,4096]{1,0:T(8,128)(2,1)S(1)} %collective-permute-done.6, bf16[64,4096]{1,0:T(8,128)(2,1)S(1)} %collective-permute-done.5), kind=kOutput, calls=%fused_computation.49 | convolution fusion | flops 1615527936 | bytes 10354688 | tf_op jit(solution)/shard_map/dot_general | solution.py:107
  61.6 0.1 pad_maximum_fusion.5
  61.8 0.1 collective-permute-start.11
  61.9 2.7 %collective-permute-start.12 = (bf16[64,4096]{1,0:T(8,128)(2,1)S(1)}, bf16[64,4096]{1,0:T(8,128)(2,1)S(1)}, u32[]{:S(2)}, u32[]{:S(2)}) collective-permute-start(bf16[64,4096]{1,0:T(8,128)(2,1)S(1)} %get-tuple-element.39), channel_id=1, source_target_pairs={{0,14},{1,15},{2,0},{3,1},{4,2},{5,3},{6,4},{7,5},{8,6},{9,7},{10,... | collective-permute-start | bytes 1572872 | tf_op jit(solution)/shard_map/ppermute | solution.py:17
  64.6 2.2 %collective-permute-start.13 = (bf16[64,4096]{1,0:T(8,128)(2,1)S(1)}, bf16[64,4096]{1,0:T(8,128)(2,1)S(1)}, u32[]{:S(2)}, u32[]{:S(2)}) collective-permute-start(bf16[64,4096]{1,0:T(8,128)(2,1)S(1)} %pad_maximum_fusion.7), channel_id=1, source_target_pairs={{0,1},{1,0},{2,3},{3,2},{4,5},{5,4},{6,7},{7,6},{8,9},{9,8},{10,11... | collective-permute-start | bytes 1572872 | tf_op jit(solution)/shard_map/ppermute | solution.py:22
  66.8 3.0 %fusion.56 = bf16[192,1024]{1,0:T(8,128)(2,1)S(1)} fusion(bf16[1024,1,4096]{2,0,1:T(8,128)(2,1)S(1)} %bitcast.38, bf16[64,4096]{1,0:T(8,128)(2,1)S(1)} %collective-permute-done.14, bf16[64,4096]{1,0:T(8,128)(2,1)S(1)} %collective-permute-done.9, bf16[64,4096]{1,0:T(8,128)(2,1)S(1)} %collective-permute-done.8), kind=kOutput, calls=%fused_computation.50 | convolution fusion | flops 1615527936 | bytes 10354688 | tf_op jit(solution)/shard_map/dot_general | solution.py:107
  69.8 1.3 %fusion.39 = bf16[512,1024]{1,0:T(8,128)(2,1)S(1)} fusion(s32[512]{0:T(512)S(1)} %eq.248, bf16[192,1024]{1,0:T(8,128)(2,1)S(1)} %fusion.56, bf16[192,1024]{1,0:T(8,128)(2,1)S(1)} %fusion.51, bf16[192,1024]{1,0:T(8,128)(2,1)S(1)} %fusion.46, bf16[256,1024]{1,0:T(8,128)(2,1)S(1)} %fusion.41), kind=kOutput, calls=%fused_computation.45 | convolution fusion | flops 880181248 | bytes 2754560 | tf_op jit(solution)/shard_map/dot_general | solution.py:136
  71.1 5.7 %collective-permute-start.15 = (bf16[512,1024]{1,0:T(8,128)(2,1)S(1)}, bf16[512,1024]{1,0:T(8,128)(2,1)S(1)}, u32[]{:S(2)}, u32[]{:S(2)}) collective-permute-start(bf16[512,1024]{1,0:T(8,128)(2,1)S(1)} %fusion.39), channel_id=1, source_target_pairs={{0,16},{16,0},{32,48},{48,32},{64,80},{80,64},{96,112},{112,96},{1... | collective-permute-start | bytes 3145736 | tf_op jit(solution)/shard_map/ppermute | solution.py:27
  76.8 1.3 %fusion.40 = bf16[512,1024]{1,0:T(8,128)(2,1)S(1)} fusion(s32[512]{0:T(512)S(1)} %eq.244, bf16[192,1024]{1,0:T(8,128)(2,1)S(1)} %fusion.56, bf16[192,1024]{1,0:T(8,128)(2,1)S(1)} %fusion.51, bf16[192,1024]{1,0:T(8,128)(2,1)S(1)} %fusion.46, bf16[256,1024]{1,0:T(8,128)(2,1)S(1)} %fusion.41), kind=kOutput, calls=%fused_computation.46 | convolution fusion | flops 880181248 | bytes 2754560 | tf_op jit(solution)/shard_map/dot_general | solution.py:136
  78.1 2.9 %fusion.61 = bf16[192,1024]{1,0:T(8,128)(2,1)S(1)} fusion(bf16[1024,1,4096]{2,0,1:T(8,128)(2,1)S(1)} %bitcast.38, bf16[64,4096]{1,0:T(8,128)(2,1)S(1)} %collective-permute-done.13, bf16[64,4096]{1,0:T(8,128)(2,1)S(1)} %collective-permute-done.12, bf16[64,4096]{1,0:T(8,128)(2,1)S(1)} %collective-permute-done.11), kind=kOutput, calls=%fused_computation.51 | convolution fusion | flops 1615527936 | bytes 10354688 | tf_op jit(solution)/shard_map/dot_general | solution.py:107
  81.0 2.7 %collective-permute-start.16 = (bf16[192,1024]{1,0:T(8,128)(2,1)S(1)}, bf16[192,1024]{1,0:T(8,128)(2,1)S(1)}, u32[]{:S(2)}, u32[]{:S(2)}) collective-permute-start(bf16[192,1024]{1,0:T(8,128)(2,1)S(1)} %fusion.61), channel_id=1, source_target_pairs={{0,16},{16,0},{32,48},{48,32},{64,80},{80,64},{96,112},{112,96},{1... | collective-permute-start | bytes 1179656 | tf_op jit(solution)/shard_map/ppermute | solution.py:27
  83.8 1.3 %collective-permute-done.16 = bf16[192,1024]{1,0:T(8,128)(2,1)S(1)} collective-permute-done((bf16[192,1024]{1,0:T(8,128)(2,1)S(1)}, bf16[192,1024]{1,0:T(8,128)(2,1)S(1)}, u32[]{:S(2)}, u32[]{:S(2)}) %collective-permute-start.16) | collective-permute-done | bytes 393248 | tf_op jit(solution)/shard_map/ppermute | solution.py:27
  85.1 0.6 add_convert_fusion
  85.7 19.0 %all_to_all.5 = bf16[8,64,1024]{2,1,0:T(8,128)(2,1)S(1)} all-to-all(bf16[8,64,1024]{2,1,0:T(8,128)(2,1)S(1)} %bitcast.35), channel_id=1, replica_groups={{0,32,64,96,128,160,192,224},{16,48,80,112,144,176,208,240},{1,33,65,97..., dimensions={0} | all-to-all | bytes 2097152 | tf_op jit(solution)/shard_map/all_to_all | solution.py:156
  104.8 0.9 convert_reduce_fusion
  (39 shorter events, 0.5 us)
Async XLA Ops:
  0.0 2.1 %copy-start = (f32[1,64,64]{2,1,0:T(8,128)S(1)}, f32[1,64,64]{2,1,0:T(8,128)}, u32[]{:S(2)}) copy-start(f32[1,64,64]{2,1,0:T(8,128)} %param.8) | copy-start | bytes 49156
  0.0 2.9 %copy-start.1 = (f32[1,64,64]{2,1,0:T(8,128)S(1)}, f32[1,64,64]{2,1,0:T(8,128)}, u32[]{:S(2)}) copy-start(f32[1,64,64]{2,1,0:T(8,128)} %param.9) | copy-start | bytes 49156
  3.9 0.7 copy-start.2
  3.9 23.6 %copy-start.3 = (s32[1024]{0:T(1024)S(1)}, s32[1024]{0:T(1024)}, u32[]{:S(2)}) copy-start(s32[1024]{0:T(1024)} %param.11) | copy-start | bytes 12292
  4.7 17.1 %collective-permute-start.1 = (bf16[64,4096]{1,0:T(8,128)(2,1)S(1)}, bf16[64,4096]{1,0:T(8,128)(2,1)S(1)}, u32[]{:S(2)}, u32[]{:S(2)}) collective-permute-start(bf16[64,4096]{1,0:T(8,128)(2,1)S(1)} %divide_convert_fusion), channel_id=1, source_target_pairs={{0,14},{1,15},{2,0},{3,1},{4,2},{5,3},{6,4},{7,5},{8,6},{9,7},{10,... | collective-permute-start | bytes 1572872 | tf_op jit(solution)/shard_map/ppermute | solution.py:17
  11.2 13.7 %collective-permute-start = (bf16[64,4096]{1,0:T(8,128)(2,1)S(1)}, bf16[64,4096]{1,0:T(8,128)(2,1)S(1)}, u32[]{:S(2)}, u32[]{:S(2)}) collective-permute-start(bf16[64,4096]{1,0:T(8,128)(2,1)S(1)} %divide_convert_fusion), channel_id=1, source_target_pairs={{0,2},{1,3},{2,4},{3,5},{4,6},{5,7},{6,8},{7,9},{8,10},{9,11},{10,... | collective-permute-start | bytes 1572872 | tf_op jit(solution)/shard_map/ppermute | solution.py:17
  11.2 19.8 %collective-permute-start.4 = (bf16[64,4096]{1,0:T(8,128)(2,1)S(1)}, bf16[64,4096]{1,0:T(8,128)(2,1)S(1)}, u32[]{:S(2)}, u32[]{:S(2)}) collective-permute-start(bf16[64,4096]{1,0:T(8,128)(2,1)S(1)} %divide_convert_fusion), channel_id=1, source_target_pairs={{0,1},{1,0},{2,3},{3,2},{4,5},{5,4},{6,7},{7,6},{8,9},{9,8},{10,11... | collective-permute-start | bytes 1572872 | tf_op jit(solution)/shard_map/ppermute | solution.py:22
  24.8 12.8 %collective-permute-start.2 = (bf16[64,4096]{1,0:T(8,128)(2,1)S(1)}, bf16[64,4096]{1,0:T(8,128)(2,1)S(1)}, u32[]{:S(2)}, u32[]{:S(2)}) collective-permute-start(bf16[64,4096]{1,0:T(8,128)(2,1)S(1)} %collective-permute-done), channel_id=1, source_target_pairs={{0,2},{1,3},{2,4},{3,5},{4,6},{5,7},{6,8},{7,9},{8,10},{9,11},{10,... | collective-permute-start | bytes 1572872 | tf_op jit(solution)/shard_map/ppermute | solution.py:17
  24.8 12.8 %collective-permute-start.3 = (bf16[64,4096]{1,0:T(8,128)(2,1)S(1)}, bf16[64,4096]{1,0:T(8,128)(2,1)S(1)}, u32[]{:S(2)}, u32[]{:S(2)}) collective-permute-start(bf16[64,4096]{1,0:T(8,128)(2,1)S(1)} %collective-permute-done.1), channel_id=1, source_target_pairs={{0,14},{1,15},{2,0},{3,1},{4,2},{5,3},{6,4},{7,5},{8,6},{9,7},{10,... | collective-permute-start | bytes 1572872 | tf_op jit(solution)/shard_map/ppermute | solution.py:17
  28.0 21.6 %collective-permute-start.7 = (bf16[64,4096]{1,0:T(8,128)(2,1)S(1)}, bf16[64,4096]{1,0:T(8,128)(2,1)S(1)}, u32[]{:S(2)}, u32[]{:S(2)}) collective-permute-start(bf16[64,4096]{1,0:T(8,128)(2,1)S(1)} %pad_maximum_fusion.1), channel_id=1, source_target_pairs={{0,1},{1,0},{2,3},{3,2},{4,5},{5,4},{6,7},{7,6},{8,9},{9,8},{10,11... | collective-permute-start | bytes 1572872 | tf_op jit(solution)/shard_map/ppermute | solution.py:22
  37.6 11.9 %collective-permute-start.5 = (bf16[64,4096]{1,0:T(8,128)(2,1)S(1)}, bf16[64,4096]{1,0:T(8,128)(2,1)S(1)}, u32[]{:S(2)}, u32[]{:S(2)}) collective-permute-start(bf16[64,4096]{1,0:T(8,128)(2,1)S(1)} %collective-permute-done.2), channel_id=1, source_target_pairs={{0,2},{1,3},{2,4},{3,5},{4,6},{5,7},{6,8},{7,9},{8,10},{9,11},{10,... | collective-permute-start | bytes 1572872 | tf_op jit(solution)/shard_map/ppermute | solution.py:17
  37.7 11.8 %collective-permute-start.6 = (bf16[64,4096]{1,0:T(8,128)(2,1)S(1)}, bf16[64,4096]{1,0:T(8,128)(2,1)S(1)}, u32[]{:S(2)}, u32[]{:S(2)}) collective-permute-start(bf16[64,4096]{1,0:T(8,128)(2,1)S(1)} %collective-permute-done.3), channel_id=1, source_target_pairs={{0,14},{1,15},{2,0},{3,1},{4,2},{5,3},{6,4},{7,5},{8,6},{9,7},{10,... | collective-permute-start | bytes 1572872 | tf_op jit(solution)/shard_map/ppermute | solution.py:17
  40.5 15.1 %slice-start = ((s8[8388608]{0:T(1024)(128)(4,1)}), s8[4194304]{0:T(1024)(128)(4,1)S(1)}, s32[]{:S(2)}) async-start(s8[8388608]{0:T(1024)(128)(4,1)} %bitcast.37), calls=%async_computation.1 | async-start | bytes 8388608
  40.6 15.1 %slice-start.1 = ((s8[8388608]{0:T(1024)(128)(4,1)}), s8[4194304]{0:T(1024)(128)(4,1)S(1)}, s32[]{:S(2)}) async-start(s8[8388608]{0:T(1024)(128)(4,1)} %bitcast.37), calls=%async_computation.2 | async-start | bytes 8388608
  40.6 18.1 %collective-permute-start.10 = (bf16[64,4096]{1,0:T(8,128)(2,1)S(1)}, bf16[64,4096]{1,0:T(8,128)(2,1)S(1)}, u32[]{:S(2)}, u32[]{:S(2)}) collective-permute-start(bf16[64,4096]{1,0:T(8,128)(2,1)S(1)} %pad_maximum_fusion.4), channel_id=1, source_target_pairs={{0,1},{1,0},{2,3},{3,2},{4,5},{5,4},{6,7},{7,6},{8,9},{9,8},{10,11... | collective-permute-start | bytes 1572872 | tf_op jit(solution)/shard_map/ppermute | solution.py:22
  49.8 12.0 %collective-permute-start.8 = (bf16[64,4096]{1,0:T(8,128)(2,1)S(1)}, bf16[64,4096]{1,0:T(8,128)(2,1)S(1)}, u32[]{:S(2)}, u32[]{:S(2)}) collective-permute-start(bf16[64,4096]{1,0:T(8,128)(2,1)S(1)} %get-tuple-element.33), channel_id=1, source_target_pairs={{0,2},{1,3},{2,4},{3,5},{4,6},{5,7},{6,8},{7,9},{8,10},{9,11},{10,... | collective-permute-start | bytes 1572872 | tf_op jit(solution)/shard_map/ppermute | solution.py:17
  49.9 11.9 %collective-permute-start.9 = (bf16[64,4096]{1,0:T(8,128)(2,1)S(1)}, bf16[64,4096]{1,0:T(8,128)(2,1)S(1)}, u32[]{:S(2)}, u32[]{:S(2)}) collective-permute-start(bf16[64,4096]{1,0:T(8,128)(2,1)S(1)} %get-tuple-element.34), channel_id=1, source_target_pairs={{0,14},{1,15},{2,0},{3,1},{4,2},{5,3},{6,4},{7,5},{8,6},{9,7},{10,... | collective-permute-start | bytes 1572872 | tf_op jit(solution)/shard_map/ppermute | solution.py:17
  52.7 14.2 %collective-permute-start.14 = (bf16[64,4096]{1,0:T(8,128)(2,1)S(1)}, bf16[64,4096]{1,0:T(8,128)(2,1)S(1)}, u32[]{:S(2)}, u32[]{:S(2)}) collective-permute-start(bf16[64,4096]{1,0:T(8,128)(2,1)S(1)} %pad_maximum_fusion.8), channel_id=1, source_target_pairs={{0,1},{1,0},{2,3},{3,2},{4,5},{5,4},{6,7},{7,6},{8,9},{9,8},{10,11... | collective-permute-start | bytes 1572872 | tf_op jit(solution)/shard_map/ppermute | solution.py:22
  61.8 16.3 %collective-permute-start.11 = (bf16[64,4096]{1,0:T(8,128)(2,1)S(1)}, bf16[64,4096]{1,0:T(8,128)(2,1)S(1)}, u32[]{:S(2)}, u32[]{:S(2)}) collective-permute-start(bf16[64,4096]{1,0:T(8,128)(2,1)S(1)} %get-tuple-element.38), channel_id=1, source_target_pairs={{0,2},{1,3},{2,4},{3,5},{4,6},{5,7},{6,8},{7,9},{8,10},{9,11},{10,... | collective-permute-start | bytes 1572872 | tf_op jit(solution)/shard_map/ppermute | solution.py:17
  61.9 16.2 %collective-permute-start.12 = (bf16[64,4096]{1,0:T(8,128)(2,1)S(1)}, bf16[64,4096]{1,0:T(8,128)(2,1)S(1)}, u32[]{:S(2)}, u32[]{:S(2)}) collective-permute-start(bf16[64,4096]{1,0:T(8,128)(2,1)S(1)} %get-tuple-element.39), channel_id=1, source_target_pairs={{0,14},{1,15},{2,0},{3,1},{4,2},{5,3},{6,4},{7,5},{8,6},{9,7},{10,... | collective-permute-start | bytes 1572872 | tf_op jit(solution)/shard_map/ppermute | solution.py:17
  64.6 13.5 %collective-permute-start.13 = (bf16[64,4096]{1,0:T(8,128)(2,1)S(1)}, bf16[64,4096]{1,0:T(8,128)(2,1)S(1)}, u32[]{:S(2)}, u32[]{:S(2)}) collective-permute-start(bf16[64,4096]{1,0:T(8,128)(2,1)S(1)} %pad_maximum_fusion.7), channel_id=1, source_target_pairs={{0,1},{1,0},{2,3},{3,2},{4,5},{5,4},{6,7},{7,6},{8,9},{9,8},{10,11... | collective-permute-start | bytes 1572872 | tf_op jit(solution)/shard_map/ppermute | solution.py:22
  71.1 14.0 %collective-permute-start.15 = (bf16[512,1024]{1,0:T(8,128)(2,1)S(1)}, bf16[512,1024]{1,0:T(8,128)(2,1)S(1)}, u32[]{:S(2)}, u32[]{:S(2)}) collective-permute-start(bf16[512,1024]{1,0:T(8,128)(2,1)S(1)} %fusion.39), channel_id=1, source_target_pairs={{0,16},{16,0},{32,48},{48,32},{64,80},{80,64},{96,112},{112,96},{1... | collective-permute-start | bytes 3145736 | tf_op jit(solution)/shard_map/ppermute | solution.py:27
  81.0 4.1 %collective-permute-start.16 = (bf16[192,1024]{1,0:T(8,128)(2,1)S(1)}, bf16[192,1024]{1,0:T(8,128)(2,1)S(1)}, u32[]{:S(2)}, u32[]{:S(2)}) collective-permute-start(bf16[192,1024]{1,0:T(8,128)(2,1)S(1)} %fusion.61), channel_id=1, source_target_pairs={{0,16},{16,0},{32,48},{48,32},{64,80},{80,64},{96,112},{112,96},{1... | collective-permute-start | bytes 1179656 | tf_op jit(solution)/shard_map/ppermute | solution.py:27

commit v6 on v5

--- a/solution.py
+++ b/solution.py
@@ -68,8 +68,7 @@
     )
     back4, front4, to_front, to_back = together(back4, front4, to_front, to_back)
     back5, front5 = along_z(to_front, 1), along_z(to_back, -1)
-    to_across, _, _ = together(join(upper(back4), upper(front4)), to_front, to_back)
-    across4 = across_y(to_across)
+    across4 = across_y(join(upper(back4), upper(front4)))
 
     yield [own, back1, front1, across0], whole(0, 0) + whole(0, -1) + whole(0, 1) + whole(1, 0)
     yield [back2, front2, across1], whole(0, -2) + whole(0, 2) + [(1, -1, 0), (1, 1, 1)]

time: 106 us -> 106 us (level)
  no operation moved by 1% of the time
where the time goes in v6:
time: 106 us
  starting transfers between devices  39.4 us (37%)
  matrix products  22.5 us (21%)
  blocking collectives  19.9 us (19%)
  waiting for transfers between devices  18.8 us (18%)
  local copies, waits for them, and re-layouts  3.36 us (3%)
  other arithmetic  1.34 us (1%)
    all_to_all x1, blocking collectives, per_device(): lax.all_to_all(chip_sum.reshape(Y_LO * X, train_rows, query_rows), 'layer...  19.9 us
    dot_general x5, matrix products, times_queries(): lax.dot_general(jnp.concatenate(blocks, axis=0), query_flat, (((1,), (1,)...  17.6 us
    ppermute x10, starting transfers between devices, along_z(): return lax.ppermute(block, 'query', pairs)  17.5 us
    ppermute x10, waiting for transfers between devices, along_z(): return lax.ppermute(block, 'query', pairs)  17.4 us
    ppermute x5, starting transfers between devices, across_y(): return lax.ppermute(block, 'query', pairs)  14.1 us
    ppermute x2, starting transfers between devices, across_cores(): return lax.ppermute(block, 'layer', pairs)  7.76 us
    dot_general x3, matrix products, times(): lax.dot_general(chosen, values, (((1,), (0,)), ((), ())), preferred_eleme...  3.2 us
  transfers between devices with their start and end apart: 17, of which 4 were waited for; matrix products, arithmetic and copies ran while one was open for 20% of the time, Pallas kernels for 0%

profile of v6, /device:TPU:1, one launch (start us, length us, event | category | flops | bytes accessed | tf_op | source)
XLA Modules:
  0.0 105.7 jit_solution(17625277016853650135)
XLA Ops:
  0.0 2.1 %reshape.50 = bf16[64,64,64]{2,1,0:T(8,128)(2,1)S(1)} reshape(bf16[64,1,4096]{2,0,1:T(8,128)(2,1)} %param.7) | data formatting | bytes 1048576 | tf_op jit(solution)/shard_map/reshape
  2.1 0.8 fusion.77
  2.9 1.0 fusion.75
  3.9 0.0 copy-start.2
  3.9 0.0 copy-start.3
  3.9 0.7 transpose.12
  4.5 0.0 copy-done.2
  4.6 0.1 divide_convert_fusion
  4.7 6.5 %collective-permute-start.1 = (bf16[64,4096]{1,0:T(8,128)(2,1)S(1)}, bf16[64,4096]{1,0:T(8,128)(2,1)S(1)}, u32[]{:S(2)}, u32[]{:S(2)}) collective-permute-start(bf16[64,4096]{1,0:T(8,128)(2,1)S(1)} %divide_convert_fusion), channel_id=1, source_target_pairs={{0,14},{1,15},{2,0},{3,1},{4,2},{5,3},{6,4},{7,5},{8,6},{9,7},{10,... | collective-permute-start | bytes 1572872 | tf_op jit(solution)/shard_map/ppermute | solution.py:17
  11.2 2.9 %collective-permute-start.4 = (bf16[64,4096]{1,0:T(8,128)(2,1)S(1)}, bf16[64,4096]{1,0:T(8,128)(2,1)S(1)}, u32[]{:S(2)}, u32[]{:S(2)}) collective-permute-start(bf16[64,4096]{1,0:T(8,128)(2,1)S(1)} %divide_convert_fusion), channel_id=1, source_target_pairs={{0,1},{1,0},{2,3},{3,2},{4,5},{5,4},{6,7},{7,6},{8,9},{9,8},{10,11... | collective-permute-start | bytes 1572872 | tf_op jit(solution)/shard_map/ppermute | solution.py:22
  14.1 7.7 %collective-permute-done.1 = bf16[64,4096]{1,0:T(8,128)(2,1)S(1)} collective-permute-done((bf16[64,4096]{1,0:T(8,128)(2,1)S(1)}, bf16[64,4096]{1,0:T(8,128)(2,1)S(1)}, u32[]{:S(2)}, u32[]{:S(2)}) %collective-permute-start.1) | collective-permute-done | bytes 524320 | tf_op jit(solution)/shard_map/ppermute | solution.py:17
  21.7 3.1 %collective-permute-done = bf16[64,4096]{1,0:T(8,128)(2,1)S(1)} collective-permute-done((bf16[64,4096]{1,0:T(8,128)(2,1)S(1)}, bf16[64,4096]{1,0:T(8,128)(2,1)S(1)}, u32[]{:S(2)}, u32[]{:S(2)}) %collective-permute-start) | collective-permute-done | bytes 524320 | tf_op jit(solution)/shard_map/ppermute | solution.py:17
  24.8 2.7 %collective-permute-start.3 = (bf16[64,4096]{1,0:T(8,128)(2,1)S(1)}, bf16[64,4096]{1,0:T(8,128)(2,1)S(1)}, u32[]{:S(2)}, u32[]{:S(2)}) collective-permute-start(bf16[64,4096]{1,0:T(8,128)(2,1)S(1)} %collective-permute-done.1), channel_id=1, source_target_pairs={{0,14},{1,15},{2,0},{3,1},{4,2},{5,3},{6,4},{7,5},{8,6},{9,7},{10,... | collective-permute-start | bytes 1572872 | tf_op jit(solution)/shard_map/ppermute | solution.py:17
  27.5 0.1 fusion.86
  27.6 0.1 reshape.53
  27.7 0.1 eq.244
  27.8 0.1 eq.248
  28.0 3.0 %collective-permute-start.7 = (bf16[64,4096]{1,0:T(8,128)(2,1)S(1)}, bf16[64,4096]{1,0:T(8,128)(2,1)S(1)}, u32[]{:S(2)}, u32[]{:S(2)}) collective-permute-start(bf16[64,4096]{1,0:T(8,128)(2,1)S(1)} %pad_maximum_fusion.1), channel_id=1, source_target_pairs={{0,1},{1,0},{2,3},{3,2},{4,5},{5,4},{6,7},{7,6},{8,9},{9,8},{10,11... | collective-permute-start | bytes 1572872 | tf_op jit(solution)/shard_map/ppermute | solution.py:22
  31.0 6.6 %collective-permute-done.2 = bf16[64,4096]{1,0:T(8,128)(2,1)S(1)} collective-permute-done((bf16[64,4096]{1,0:T(8,128)(2,1)S(1)}, bf16[64,4096]{1,0:T(8,128)(2,1)S(1)}, u32[]{:S(2)}, u32[]{:S(2)}) %collective-permute-start.2) | collective-permute-done | bytes 524320 | tf_op jit(solution)/shard_map/ppermute | solution.py:17
  37.6 0.0 collective-permute-done.3
  37.6 0.1 collective-permute-start.5
  37.7 2.7 %collective-permute-start.6 = (bf16[64,4096]{1,0:T(8,128)(2,1)S(1)}, bf16[64,4096]{1,0:T(8,128)(2,1)S(1)}, u32[]{:S(2)}, u32[]{:S(2)}) collective-permute-start(bf16[64,4096]{1,0:T(8,128)(2,1)S(1)} %collective-permute-done.3), channel_id=1, source_target_pairs={{0,14},{1,15},{2,0},{3,1},{4,2},{5,3},{6,4},{7,5},{8,6},{9,7},{10,... | collective-permute-start | bytes 1572872 | tf_op jit(solution)/shard_map/ppermute | solution.py:17
  40.5 0.0 slice-start
  40.6 0.0 slice-start.1
  40.6 3.2 %collective-permute-start.10 = (bf16[64,4096]{1,0:T(8,128)(2,1)S(1)}, bf16[64,4096]{1,0:T(8,128)(2,1)S(1)}, u32[]{:S(2)}, u32[]{:S(2)}) collective-permute-start(bf16[64,4096]{1,0:T(8,128)(2,1)S(1)} %pad_maximum_fusion.4), channel_id=1, source_target_pairs={{0,1},{1,0},{2,3},{3,2},{4,5},{5,4},{6,7},{7,6},{8,9},{9,8},{10,11... | collective-permute-start | bytes 1572872 | tf_op jit(solution)/shard_map/ppermute | solution.py:22
  43.8 5.7 %fusion.41 = bf16[256,1024]{1,0:T(8,128)(2,1)S(1)} fusion(bf16[1024,1,4096]{2,0,1:T(8,128)(2,1)} %param.6, bf16[64,4096]{1,0:T(8,128)(2,1)S(1)} %collective-permute-done.4, bf16[64,4096]{1,0:T(8,128)(2,1)S(1)} %collective-permute-done.1, bf16[64,4096]{1,0:T(8,128)(2,1)S(1)} %collective-permute-done, bf16[64,4096]{1,0:T(8,128)(2,1)S(1)} %divide_convert_fusion), kind=kOutput, calls=%fused_computation.47 | convolution fusion | flops 2156134400 | bytes 11010048 | tf_op jit(solution)/shard_map/dot_general | solution.py:106
  49.5 0.0 collective-permute-done.5
  49.6 0.1 pad_maximum_fusion.2
  49.8 0.1 collective-permute-start.8
  49.9 2.7 %collective-permute-start.9 = (bf16[64,4096]{1,0:T(8,128)(2,1)S(1)}, bf16[64,4096]{1,0:T(8,128)(2,1)S(1)}, u32[]{:S(2)}, u32[]{:S(2)}) collective-permute-start(bf16[64,4096]{1,0:T(8,128)(2,1)S(1)} %get-tuple-element.33), channel_id=1, source_target_pairs={{0,14},{1,15},{2,0},{3,1},{4,2},{5,3},{6,4},{7,5},{8,6},{9,7},{10,... | collective-permute-start | bytes 1572872 | tf_op jit(solution)/shard_map/ppermute | solution.py:17
  52.7 3.0 %collective-permute-start.14 = (bf16[64,4096]{1,0:T(8,128)(2,1)S(1)}, bf16[64,4096]{1,0:T(8,128)(2,1)S(1)}, u32[]{:S(2)}, u32[]{:S(2)}) collective-permute-start(bf16[64,4096]{1,0:T(8,128)(2,1)S(1)} %pad_maximum_fusion.8), channel_id=1, source_target_pairs={{0,1},{1,0},{2,3},{3,2},{4,5},{5,4},{6,7},{7,6},{8,9},{9,8},{10,11... | collective-permute-start | bytes 1572872 | tf_op jit(solution)/shard_map/ppermute | solution.py:22
  55.7 3.0 %fusion.46 = bf16[192,1024]{1,0:T(8,128)(2,1)S(1)} fusion(bf16[1024,1,4096]{2,0,1:T(8,128)(2,1)S(1)} %bitcast.38, bf16[64,4096]{1,0:T(8,128)(2,1)S(1)} %collective-permute-done.7, bf16[64,4096]{1,0:T(8,128)(2,1)S(1)} %collective-permute-done.3, bf16[64,4096]{1,0:T(8,128)(2,1)S(1)} %collective-permute-done.2), kind=kOutput, calls=%fused_computation.48 | convolution fusion | flops 1615527936 | bytes 10354688 | tf_op jit(solution)/shard_map/dot_general | solution.py:106
  58.7 0.0 collective-permute-done.10
  58.7 2.9 %fusion.51 = bf16[192,1024]{1,0:T(8,128)(2,1)S(1)} fusion(bf16[1024,1,4096]{2,0,1:T(8,128)(2,1)S(1)} %bitcast.38, bf16[64,4096]{1,0:T(8,128)(2,1)S(1)} %collective-permute-done.10, bf16[64,4096]{1,0:T(8,128)(2,1)S(1)} %collective-permute-done.6, bf16[64,4096]{1,0:T(8,128)(2,1)S(1)} %collective-permute-done.5), kind=kOutput, calls=%fused_computation.49 | convolution fusion | flops 1615527936 | bytes 10354688 | tf_op jit(solution)/shard_map/dot_general | solution.py:106
  61.6 0.1 pad_maximum_fusion.5
  61.9 2.0 %collective-permute-start.13 = (bf16[64,4096]{1,0:T(8,128)(2,1)S(1)}, bf16[64,4096]{1,0:T(8,128)(2,1)S(1)}, u32[]{:S(2)}, u32[]{:S(2)}) collective-permute-start(bf16[64,4096]{1,0:T(8,128)(2,1)S(1)} %pad_maximum_fusion.7), channel_id=1, source_target_pairs={{0,1},{1,0},{2,3},{3,2},{4,5},{5,4},{6,7},{7,6},{8,9},{9,8},{10,11... | collective-permute-start | bytes 1572872 | tf_op jit(solution)/shard_map/ppermute | solution.py:22
  63.9 0.1 collective-permute-start.11
  64.0 2.5 %collective-permute-start.12 = (bf16[64,4096]{1,0:T(8,128)(2,1)S(1)}, bf16[64,4096]{1,0:T(8,128)(2,1)S(1)}, u32[]{:S(2)}, u32[]{:S(2)}) collective-permute-start(bf16[64,4096]{1,0:T(8,128)(2,1)S(1)} %get-tuple-element.38), channel_id=1, source_target_pairs={{0,14},{1,15},{2,0},{3,1},{4,2},{5,3},{6,4},{7,5},{8,6},{9,7},{10,... | collective-permute-start | bytes 1572872 | tf_op jit(solution)/shard_map/ppermute | solution.py:17
  66.5 3.0 %fusion.56 = bf16[192,1024]{1,0:T(8,128)(2,1)S(1)} fusion(bf16[1024,1,4096]{2,0,1:T(8,128)(2,1)S(1)} %bitcast.38, bf16[64,4096]{1,0:T(8,128)(2,1)S(1)} %collective-permute-done.14, bf16[64,4096]{1,0:T(8,128)(2,1)S(1)} %collective-permute-done.9, bf16[64,4096]{1,0:T(8,128)(2,1)S(1)} %collective-permute-done.8), kind=kOutput, calls=%fused_computation.50 | convolution fusion | flops 1615527936 | bytes 10354688 | tf_op jit(solution)/shard_map/dot_general | solution.py:106
  69.5 1.3 %fusion.39 = bf16[512,1024]{1,0:T(8,128)(2,1)S(1)} fusion(s32[512]{0:T(512)S(1)} %eq.248, bf16[192,1024]{1,0:T(8,128)(2,1)S(1)} %fusion.56, bf16[192,1024]{1,0:T(8,128)(2,1)S(1)} %fusion.51, bf16[192,1024]{1,0:T(8,128)(2,1)S(1)} %fusion.46, bf16[256,1024]{1,0:T(8,128)(2,1)S(1)} %fusion.41), kind=kOutput, calls=%fused_computation.45 | convolution fusion | flops 880181248 | bytes 2754560 | tf_op jit(solution)/shard_map/dot_general | solution.py:135
  70.8 5.6 %collective-permute-start.15 = (bf16[512,1024]{1,0:T(8,128)(2,1)S(1)}, bf16[512,1024]{1,0:T(8,128)(2,1)S(1)}, u32[]{:S(2)}, u32[]{:S(2)}) collective-permute-start(bf16[512,1024]{1,0:T(8,128)(2,1)S(1)} %fusion.39), channel_id=1, source_target_pairs={{0,16},{16,0},{32,48},{48,32},{64,80},{80,64},{96,112},{112,96},{1... | collective-permute-start | bytes 3145736 | tf_op jit(solution)/shard_map/ppermute | solution.py:27
  76.4 1.3 %fusion.40 = bf16[512,1024]{1,0:T(8,128)(2,1)S(1)} fusion(s32[512]{0:T(512)S(1)} %eq.244, bf16[192,1024]{1,0:T(8,128)(2,1)S(1)} %fusion.56, bf16[192,1024]{1,0:T(8,128)(2,1)S(1)} %fusion.51, bf16[192,1024]{1,0:T(8,128)(2,1)S(1)} %fusion.46, bf16[256,1024]{1,0:T(8,128)(2,1)S(1)} %fusion.41), kind=kOutput, calls=%fused_computation.46 | convolution fusion | flops 880181248 | bytes 2754560 | tf_op jit(solution)/shard_map/dot_general | solution.py:135
  77.7 3.0 %fusion.61 = bf16[192,1024]{1,0:T(8,128)(2,1)S(1)} fusion(bf16[1024,1,4096]{2,0,1:T(8,128)(2,1)S(1)} %bitcast.38, bf16[64,4096]{1,0:T(8,128)(2,1)S(1)} %collective-permute-done.13, bf16[64,4096]{1,0:T(8,128)(2,1)S(1)} %collective-permute-done.12, bf16[64,4096]{1,0:T(8,128)(2,1)S(1)} %collective-permute-done.11), kind=kOutput, calls=%fused_computation.51 | convolution fusion | flops 1615527936 | bytes 10354688 | tf_op jit(solution)/shard_map/dot_general | solution.py:106
  80.7 2.2 %collective-permute-start.16 = (bf16[192,1024]{1,0:T(8,128)(2,1)S(1)}, bf16[192,1024]{1,0:T(8,128)(2,1)S(1)}, u32[]{:S(2)}, u32[]{:S(2)}) collective-permute-start(bf16[192,1024]{1,0:T(8,128)(2,1)S(1)} %fusion.61), channel_id=1, source_target_pairs={{0,16},{16,0},{32,48},{48,32},{64,80},{80,64},{96,112},{112,96},{1... | collective-permute-start | bytes 1179656 | tf_op jit(solution)/shard_map/ppermute | solution.py:27
  82.9 1.3 %collective-permute-done.16 = bf16[192,1024]{1,0:T(8,128)(2,1)S(1)} collective-permute-done((bf16[192,1024]{1,0:T(8,128)(2,1)S(1)}, bf16[192,1024]{1,0:T(8,128)(2,1)S(1)}, u32[]{:S(2)}, u32[]{:S(2)}) %collective-permute-start.16) | collective-permute-done | bytes 393248 | tf_op jit(solution)/shard_map/ppermute | solution.py:27
  84.3 0.6 add_convert_fusion
  84.9 19.9 %all_to_all.5 = bf16[8,64,1024]{2,1,0:T(8,128)(2,1)S(1)} all-to-all(bf16[8,64,1024]{2,1,0:T(8,128)(2,1)S(1)} %bitcast.35), channel_id=1, replica_groups={{0,32,64,96,128,160,192,224},{16,48,80,112,144,176,208,240},{1,33,65,97..., dimensions={0} | all-to-all | bytes 2097152 | tf_op jit(solution)/shard_map/all_to_all | solution.py:155
  104.8 0.9 convert_reduce_fusion
  (39 shorter events, 0.5 us)
Async XLA Ops:
  0.0 2.1 %copy-start = (f32[1,64,64]{2,1,0:T(8,128)S(1)}, f32[1,64,64]{2,1,0:T(8,128)}, u32[]{:S(2)}) copy-start(f32[1,64,64]{2,1,0:T(8,128)} %param.8) | copy-start | bytes 49156
  0.0 2.9 %copy-start.1 = (f32[1,64,64]{2,1,0:T(8,128)S(1)}, f32[1,64,64]{2,1,0:T(8,128)}, u32[]{:S(2)}) copy-start(f32[1,64,64]{2,1,0:T(8,128)} %param.9) | copy-start | bytes 49156
  3.9 0.7 copy-start.2
  3.9 23.6 %copy-start.3 = (s32[1024]{0:T(1024)S(1)}, s32[1024]{0:T(1024)}, u32[]{:S(2)}) copy-start(s32[1024]{0:T(1024)} %param.11) | copy-start | bytes 12292
  4.7 17.1 %collective-permute-start.1 = (bf16[64,4096]{1,0:T(8,128)(2,1)S(1)}, bf16[64,4096]{1,0:T(8,128)(2,1)S(1)}, u32[]{:S(2)}, u32[]{:S(2)}) collective-permute-start(bf16[64,4096]{1,0:T(8,128)(2,1)S(1)} %divide_convert_fusion), channel_id=1, source_target_pairs={{0,14},{1,15},{2,0},{3,1},{4,2},{5,3},{6,4},{7,5},{8,6},{9,7},{10,... | collective-permute-start | bytes 1572872 | tf_op jit(solution)/shard_map/ppermute | solution.py:17
  11.2 13.7 %collective-permute-start = (bf16[64,4096]{1,0:T(8,128)(2,1)S(1)}, bf16[64,4096]{1,0:T(8,128)(2,1)S(1)}, u32[]{:S(2)}, u32[]{:S(2)}) collective-permute-start(bf16[64,4096]{1,0:T(8,128)(2,1)S(1)} %divide_convert_fusion), channel_id=1, source_target_pairs={{0,2},{1,3},{2,4},{3,5},{4,6},{5,7},{6,8},{7,9},{8,10},{9,11},{10,... | collective-permute-start | bytes 1572872 | tf_op jit(solution)/shard_map/ppermute | solution.py:17
  11.2 19.8 %collective-permute-start.4 = (bf16[64,4096]{1,0:T(8,128)(2,1)S(1)}, bf16[64,4096]{1,0:T(8,128)(2,1)S(1)}, u32[]{:S(2)}, u32[]{:S(2)}) collective-permute-start(bf16[64,4096]{1,0:T(8,128)(2,1)S(1)} %divide_convert_fusion), channel_id=1, source_target_pairs={{0,1},{1,0},{2,3},{3,2},{4,5},{5,4},{6,7},{7,6},{8,9},{9,8},{10,11... | collective-permute-start | bytes 1572872 | tf_op jit(solution)/shard_map/ppermute | solution.py:22
  24.8 12.8 %collective-permute-start.2 = (bf16[64,4096]{1,0:T(8,128)(2,1)S(1)}, bf16[64,4096]{1,0:T(8,128)(2,1)S(1)}, u32[]{:S(2)}, u32[]{:S(2)}) collective-permute-start(bf16[64,4096]{1,0:T(8,128)(2,1)S(1)} %collective-permute-done), channel_id=1, source_target_pairs={{0,2},{1,3},{2,4},{3,5},{4,6},{5,7},{6,8},{7,9},{8,10},{9,11},{10,... | collective-permute-start | bytes 1572872 | tf_op jit(solution)/shard_map/ppermute | solution.py:17
  24.8 12.8 %collective-permute-start.3 = (bf16[64,4096]{1,0:T(8,128)(2,1)S(1)}, bf16[64,4096]{1,0:T(8,128)(2,1)S(1)}, u32[]{:S(2)}, u32[]{:S(2)}) collective-permute-start(bf16[64,4096]{1,0:T(8,128)(2,1)S(1)} %collective-permute-done.1), channel_id=1, source_target_pairs={{0,14},{1,15},{2,0},{3,1},{4,2},{5,3},{6,4},{7,5},{8,6},{9,7},{10,... | collective-permute-start | bytes 1572872 | tf_op jit(solution)/shard_map/ppermute | solution.py:17
  28.0 21.6 %collective-permute-start.7 = (bf16[64,4096]{1,0:T(8,128)(2,1)S(1)}, bf16[64,4096]{1,0:T(8,128)(2,1)S(1)}, u32[]{:S(2)}, u32[]{:S(2)}) collective-permute-start(bf16[64,4096]{1,0:T(8,128)(2,1)S(1)} %pad_maximum_fusion.1), channel_id=1, source_target_pairs={{0,1},{1,0},{2,3},{3,2},{4,5},{5,4},{6,7},{7,6},{8,9},{9,8},{10,11... | collective-permute-start | bytes 1572872 | tf_op jit(solution)/shard_map/ppermute | solution.py:22
  37.6 11.9 %collective-permute-start.5 = (bf16[64,4096]{1,0:T(8,128)(2,1)S(1)}, bf16[64,4096]{1,0:T(8,128)(2,1)S(1)}, u32[]{:S(2)}, u32[]{:S(2)}) collective-permute-start(bf16[64,4096]{1,0:T(8,128)(2,1)S(1)} %collective-permute-done.2), channel_id=1, source_target_pairs={{0,2},{1,3},{2,4},{3,5},{4,6},{5,7},{6,8},{7,9},{8,10},{9,11},{10,... | collective-permute-start | bytes 1572872 | tf_op jit(solution)/shard_map/ppermute | solution.py:17
  37.7 11.8 %collective-permute-start.6 = (bf16[64,4096]{1,0:T(8,128)(2,1)S(1)}, bf16[64,4096]{1,0:T(8,128)(2,1)S(1)}, u32[]{:S(2)}, u32[]{:S(2)}) collective-permute-start(bf16[64,4096]{1,0:T(8,128)(2,1)S(1)} %collective-permute-done.3), channel_id=1, source_target_pairs={{0,14},{1,15},{2,0},{3,1},{4,2},{5,3},{6,4},{7,5},{8,6},{9,7},{10,... | collective-permute-start | bytes 1572872 | tf_op jit(solution)/shard_map/ppermute | solution.py:17
  40.5 15.1 %slice-start = ((s8[8388608]{0:T(1024)(128)(4,1)}), s8[4194304]{0:T(1024)(128)(4,1)S(1)}, s32[]{:S(2)}) async-start(s8[8388608]{0:T(1024)(128)(4,1)} %bitcast.37), calls=%async_computation.1 | async-start | bytes 8388608
  40.6 15.1 %slice-start.1 = ((s8[8388608]{0:T(1024)(128)(4,1)}), s8[4194304]{0:T(1024)(128)(4,1)S(1)}, s32[]{:S(2)}) async-start(s8[8388608]{0:T(1024)(128)(4,1)} %bitcast.37), calls=%async_computation.2 | async-start | bytes 8388608
  40.6 18.1 %collective-permute-start.10 = (bf16[64,4096]{1,0:T(8,128)(2,1)S(1)}, bf16[64,4096]{1,0:T(8,128)(2,1)S(1)}, u32[]{:S(2)}, u32[]{:S(2)}) collective-permute-start(bf16[64,4096]{1,0:T(8,128)(2,1)S(1)} %pad_maximum_fusion.4), channel_id=1, source_target_pairs={{0,1},{1,0},{2,3},{3,2},{4,5},{5,4},{6,7},{7,6},{8,9},{9,8},{10,11... | collective-permute-start | bytes 1572872 | tf_op jit(solution)/shard_map/ppermute | solution.py:22
  49.8 12.0 %collective-permute-start.8 = (bf16[64,4096]{1,0:T(8,128)(2,1)S(1)}, bf16[64,4096]{1,0:T(8,128)(2,1)S(1)}, u32[]{:S(2)}, u32[]{:S(2)}) collective-permute-start(bf16[64,4096]{1,0:T(8,128)(2,1)S(1)} %get-tuple-element.32), channel_id=1, source_target_pairs={{0,2},{1,3},{2,4},{3,5},{4,6},{5,7},{6,8},{7,9},{8,10},{9,11},{10,... | collective-permute-start | bytes 1572872 | tf_op jit(solution)/shard_map/ppermute | solution.py:17
  49.9 11.9 %collective-permute-start.9 = (bf16[64,4096]{1,0:T(8,128)(2,1)S(1)}, bf16[64,4096]{1,0:T(8,128)(2,1)S(1)}, u32[]{:S(2)}, u32[]{:S(2)}) collective-permute-start(bf16[64,4096]{1,0:T(8,128)(2,1)S(1)} %get-tuple-element.33), channel_id=1, source_target_pairs={{0,14},{1,15},{2,0},{3,1},{4,2},{5,3},{6,4},{7,5},{8,6},{9,7},{10,... | collective-permute-start | bytes 1572872 | tf_op jit(solution)/shard_map/ppermute | solution.py:17
  52.7 13.9 %collective-permute-start.14 = (bf16[64,4096]{1,0:T(8,128)(2,1)S(1)}, bf16[64,4096]{1,0:T(8,128)(2,1)S(1)}, u32[]{:S(2)}, u32[]{:S(2)}) collective-permute-start(bf16[64,4096]{1,0:T(8,128)(2,1)S(1)} %pad_maximum_fusion.8), channel_id=1, source_target_pairs={{0,1},{1,0},{2,3},{3,2},{4,5},{5,4},{6,7},{7,6},{8,9},{9,8},{10,11... | collective-permute-start | bytes 1572872 | tf_op jit(solution)/shard_map/ppermute | solution.py:22
  61.9 15.8 %collective-permute-start.13 = (bf16[64,4096]{1,0:T(8,128)(2,1)S(1)}, bf16[64,4096]{1,0:T(8,128)(2,1)S(1)}, u32[]{:S(2)}, u32[]{:S(2)}) collective-permute-start(bf16[64,4096]{1,0:T(8,128)(2,1)S(1)} %pad_maximum_fusion.7), channel_id=1, source_target_pairs={{0,1},{1,0},{2,3},{3,2},{4,5},{5,4},{6,7},{7,6},{8,9},{9,8},{10,11... | collective-permute-start | bytes 1572872 | tf_op jit(solution)/shard_map/ppermute | solution.py:22
  63.9 13.8 %collective-permute-start.11 = (bf16[64,4096]{1,0:T(8,128)(2,1)S(1)}, bf16[64,4096]{1,0:T(8,128)(2,1)S(1)}, u32[]{:S(2)}, u32[]{:S(2)}) collective-permute-start(bf16[64,4096]{1,0:T(8,128)(2,1)S(1)} %get-tuple-element.37), channel_id=1, source_target_pairs={{0,2},{1,3},{2,4},{3,5},{4,6},{5,7},{6,8},{7,9},{8,10},{9,11},{10,... | collective-permute-start | bytes 1572872 | tf_op jit(solution)/shard_map/ppermute | solution.py:17
  64.0 13.7 %collective-permute-start.12 = (bf16[64,4096]{1,0:T(8,128)(2,1)S(1)}, bf16[64,4096]{1,0:T(8,128)(2,1)S(1)}, u32[]{:S(2)}, u32[]{:S(2)}) collective-permute-start(bf16[64,4096]{1,0:T(8,128)(2,1)S(1)} %get-tuple-element.38), channel_id=1, source_target_pairs={{0,14},{1,15},{2,0},{3,1},{4,2},{5,3},{6,4},{7,5},{8,6},{9,7},{10,... | collective-permute-start | bytes 1572872 | tf_op jit(solution)/shard_map/ppermute | solution.py:17
  70.8 13.4 %collective-permute-start.15 = (bf16[512,1024]{1,0:T(8,128)(2,1)S(1)}, bf16[512,1024]{1,0:T(8,128)(2,1)S(1)}, u32[]{:S(2)}, u32[]{:S(2)}) collective-permute-start(bf16[512,1024]{1,0:T(8,128)(2,1)S(1)} %fusion.39), channel_id=1, source_target_pairs={{0,16},{16,0},{32,48},{48,32},{64,80},{80,64},{96,112},{112,96},{1... | collective-permute-start | bytes 3145736 | tf_op jit(solution)/shard_map/ppermute | solution.py:27
  80.7 3.6 %collective-permute-start.16 = (bf16[192,1024]{1,0:T(8,128)(2,1)S(1)}, bf16[192,1024]{1,0:T(8,128)(2,1)S(1)}, u32[]{:S(2)}, u32[]{:S(2)}) collective-permute-start(bf16[192,1024]{1,0:T(8,128)(2,1)S(1)} %fusion.61), channel_id=1, source_target_pairs={{0,16},{16,0},{32,48},{48,32},{64,80},{80,64},{96,112},{112,96},{1... | collective-permute-start | bytes 1179656 | tf_op jit(solution)/shard_map/ppermute | solution.py:27
